TPU v7x, 32 devices: a whole 2x2x4 slice. The times are simulated.
32 devices in a mesh: section: 2 (over x), dp: 4 (over z), tensor: 4 (over y, core).
Axes of the slice: x: 2, y: 2, z: 4, core: 2. Of those that a mesh axis runs over, the one named last changes fastest.
Arguments:
- layer_input: bfloat16 [4, 3328, 768], P(None, ('dp', 'tensor')), may hold values from -6 to 6
- cotangent: bfloat16 [4, 3328, 768], P(None, ('dp', 'tensor')), may hold values from -6 to 6
- region_count: int32 [4, 16], P(None, 'dp'), may hold values from 10 to 80
- region_mask: int32 [4, 16, 80], P(None, 'dp'), may hold values 0 or 1
- attn_weight: bfloat16 [2, 768, 12, 192], P('section', None, 'tensor'), may hold values from -0.21875 to 0.21875
- attn_bias: float32 [2, 12, 128], P('section', 'tensor'), may hold values from -0.6 to 0.6
- proj_weight: bfloat16 [2, 12, 64, 768], P('section', 'tensor'), may hold values from -1.5 to 1.5
- proj_bias: float32 [2, 768], P('section'), may hold values from -1.8 to 1.8
- first_gain: float32 [2, 768], P('section'), may hold values from 0.5 to 1.5
- first_shift: float32 [2, 768], P('section'), may hold values from -1.8 to 1.8
- up_weight: bfloat16 [2, 768, 3072], P('section', None, 'tensor'), may hold values from -0.21875 to 0.21875
- up_bias: float32 [2, 3072], P('section', 'tensor'), may hold values from -1.8 to 1.8
- down_weight: bfloat16 [2, 3072, 768], P('section', 'tensor'), may hold values from -0.109375 to 0.109375
- down_bias: float32 [2, 768], P('section'), may hold values from -1.8 to 1.8
- second_gain: float32 [2, 768], P('section'), may hold values from 0.5 to 1.5
- second_shift: float32 [2, 768], P('section'), may hold values from -1.8 to 1.8
Outputs:
- layer_outputs: bfloat16 [2, 4, 3328, 768], P('section', None, ('dp', 'tensor'))
- input_grads: float32 [2, 4, 3328, 768], P('section', None, ('dp', 'tensor'))
- grad_attn_weight: float32 [2, 768, 12, 192], P('section', None, 'tensor')
- grad_attn_bias: float32 [2, 12, 128], P('section', 'tensor')
- grad_proj_weight: float32 [2, 12, 64, 768], P('section', 'tensor')
- grad_proj_bias: float32 [2, 768], P('section')
- grad_first_gain: float32 [2, 768], P('section')
- grad_first_shift: float32 [2, 768], P('section')
- grad_up_weight: float32 [2, 768, 3072], P('section', None, 'tensor')
- grad_up_bias: float32 [2, 3072], P('section', 'tensor')
- grad_down_weight: float32 [2, 3072, 768], P('section', 'tensor')
- grad_down_bias: float32 [2, 768], P('section')
- grad_second_gain: float32 [2, 768], P('section')
- grad_second_shift: float32 [2, 768], P('section')
Inputs may be any that keep to these rules, and one draw needn't show every extreme that they name: `region_mask`: 1 marks a usable region slot.
All inputs are finite; a program needn't handle non-finite values. No bound on the sum of `region_mask` on one device may be relied on, other than what follows from the above.
Results may differ from a plain program's by a relative error of at most 0.025.
Values may be sent and summed in bfloat16 or wider, within the bound.
No kernel may reach another device: no remote copies, remote signals or barrier semaphores. Data moves between devices by JAX's collectives and lax.ppermute only.
A program may use at most 192 MiB of HBM per device.

v0:
```python
import jax
import jax.numpy as jnp
from jax import lax
from jax.sharding import PartitionSpec as P

HD = 64
CAPTION = 128
SEQLEN = 208


norm_eps = 1e-06
masked_value = -1000000000.0


def passed_along(value, axis, steps):
    count = lax.axis_size(axis)
    first, last = (max(0, -steps), min(count, count - steps))
    return lax.ppermute(value, axis, [(source, source + steps) for source in range(first, last)])


def layer_norm(residual, gain_vec, shift_vec):
    center = residual - jnp.mean(residual, axis=-1, keepdims=True)
    spread = jnp.mean(center * center, axis=-1, keepdims=True)
    return center * lax.rsqrt(spread + norm_eps) * gain_vec + shift_vec


def exact_gelu(inputs):
    return jax.nn.gelu(inputs, approximate=False)


def key_allowed(region_count, region_mask):
    regions = region_mask.shape[-1]
    slot_index = jnp.arange(CAPTION + regions, dtype=jnp.int32) - CAPTION
    caption_ones = jnp.ones(region_mask.shape[:-1] + (CAPTION,), jnp.int32)
    present = jnp.concatenate([caption_ones, region_mask], axis=-1) > 0
    return present & (slot_index < region_count[..., None])


def rows_product(source, weight):
    return jnp.dot(source, weight, preferred_element_type=jnp.float32)


def rows_back(source, weight):
    return jnp.einsum("nf,df->nd", source, weight, preferred_element_type=jnp.float32)


def split_heads(projected, sequences):
    pieces = projected.reshape(sequences, SEQLEN, -1, 3, HD)
    return (pieces[:, :, :, 0], pieces[:, :, :, 1], pieces[:, :, :, 2])


def masked_scores(queries, key_rows, allowed):
    scores = (
        jnp.einsum("sqhd,skhd->shqk", queries, key_rows, preferred_element_type=jnp.float32) * 0.125
    )
    return jnp.where(allowed[:, None, None, :], scores, masked_value)


def forward_layer(rows_in, allowed, params):
    (
        attn_w,
        full_bias,
        proj_w,
        proj_b,
        gain_one,
        shift_one,
        up_w,
        up_b,
        down_w,
        down_b,
        gain_two,
        shift_two,
    ) = params
    sequences = allowed.shape[0]
    gathered = lax.all_gather(rows_in, "tensor", axis=0, tiled=True)
    projected = (jnp.dot(gathered, attn_w, preferred_element_type=jnp.float32) + full_bias).astype(
        jnp.bfloat16
    )
    queries, key_rows, value_rows = split_heads(projected, sequences)
    scores = masked_scores(queries, key_rows, allowed)
    row_max = jnp.max(scores, axis=-1, keepdims=True)
    exp_scores = jnp.exp(scores - row_max)
    row_sum = jnp.sum(exp_scores, axis=-1, keepdims=True)
    weights_bf = (exp_scores / row_sum).astype(jnp.bfloat16)
    log_total = row_max + jnp.log(row_sum)
    context = jnp.einsum(
        "shqk,skhd->sqhd", weights_bf, value_rows, preferred_element_type=jnp.float32
    )
    context = context.astype(jnp.bfloat16).reshape(gathered.shape[0], -1)
    attended = lax.psum_scatter(
        rows_product(context, proj_w).astype(jnp.bfloat16),
        "tensor",
        scatter_dimension=0,
        tiled=True,
    ).astype(jnp.float32)
    resid_one = rows_in.astype(jnp.float32) + attended + proj_b
    hidden = layer_norm(resid_one, gain_one, shift_one)
    middle = lax.all_gather(hidden.astype(jnp.bfloat16), "tensor", axis=0, tiled=True)
    upward = jnp.dot(middle, up_w, preferred_element_type=jnp.float32) + up_b
    activated = exact_gelu(upward).astype(jnp.bfloat16)
    feed = lax.psum_scatter(
        rows_product(activated, down_w).astype(jnp.bfloat16),
        "tensor",
        scatter_dimension=0,
        tiled=True,
    ).astype(jnp.float32)
    resid_two = hidden + feed + down_b
    output = layer_norm(resid_two, gain_two, shift_two).astype(jnp.bfloat16)
    saved = (gathered, projected, log_total, context, resid_one, middle, upward, resid_two, allowed)
    return (output, saved)


def backward_layer(grad_out, saved, params):
    (
        attn_w,
        full_bias,
        proj_w,
        proj_b,
        gain_one,
        shift_one,
        up_w,
        up_b,
        down_w,
        down_b,
        gain_two,
        shift_two,
    ) = params
    gathered, projected, log_total, context, resid_one, middle, upward, resid_two, allowed = saved
    sequences = allowed.shape[0]
    _, norm_two_back = jax.vjp(layer_norm, resid_two, gain_two, shift_two)
    d_resid_two, g_gain_two, g_shift_two = norm_two_back(grad_out)
    g_down_bias = jnp.sum(d_resid_two, axis=0)
    feed_rows = lax.all_gather(d_resid_two.astype(jnp.bfloat16), "tensor", axis=0, tiled=True)
    activated = exact_gelu(upward).astype(jnp.bfloat16)
    g_down = jnp.einsum("nf,nd->fd", activated, feed_rows, preferred_element_type=jnp.float32)
    d_activated = jnp.einsum("nd,fd->nf", feed_rows, down_w, preferred_element_type=jnp.float32)
    _, gelu_back = jax.vjp(exact_gelu, upward)
    d_upward = gelu_back(d_activated)[0].astype(jnp.bfloat16)
    g_up = jnp.einsum("nd,nf->df", middle, d_upward, preferred_element_type=jnp.float32)
    g_up_bias = jnp.sum(d_upward.astype(jnp.float32), axis=0)
    d_hidden = lax.psum_scatter(
        rows_back(d_upward, up_w).astype(jnp.bfloat16), "tensor", scatter_dimension=0, tiled=True
    ).astype(jnp.float32)
    d_hidden = d_hidden + d_resid_two
    _, norm_one_back = jax.vjp(layer_norm, resid_one, gain_one, shift_one)
    d_resid_one, g_gain_one, g_shift_one = norm_one_back(d_hidden)
    g_proj_bias = jnp.sum(d_resid_one, axis=0)
    attn_rows = lax.all_gather(d_resid_one.astype(jnp.bfloat16), "tensor", axis=0, tiled=True)
    g_proj = jnp.einsum("nc,nd->cd", context, attn_rows, preferred_element_type=jnp.float32)
    d_context = jnp.einsum(
        "nd,cd->nc", attn_rows, proj_w, preferred_element_type=jnp.float32
    ).astype(jnp.bfloat16)
    queries, key_rows, value_rows = split_heads(projected, sequences)
    d_context = d_context.reshape(queries.shape)
    scores = masked_scores(queries, key_rows, allowed)
    probs_full = jnp.exp(scores - log_total)
    weights_bf = probs_full.astype(jnp.bfloat16)
    d_values = jnp.einsum(
        "shqk,sqhd->skhd", weights_bf, d_context, preferred_element_type=jnp.float32
    )
    d_weights = jnp.einsum(
        "sqhd,skhd->shqk", d_context, value_rows, preferred_element_type=jnp.float32
    )
    d_scores = probs_full * (d_weights - jnp.sum(d_weights * probs_full, axis=-1, keepdims=True))
    d_scores = d_scores.astype(jnp.bfloat16)
    d_queries = (
        jnp.einsum("shqk,skhd->sqhd", d_scores, key_rows, preferred_element_type=jnp.float32)
        * 0.125
    )
    d_keys = (
        jnp.einsum("shqk,sqhd->skhd", d_scores, queries, preferred_element_type=jnp.float32) * 0.125
    )
    d_projected = (
        jnp.stack([d_queries, d_keys, d_values], axis=3)
        .reshape(projected.shape)
        .astype(jnp.bfloat16)
    )
    g_attn = jnp.einsum("nd,ne->de", gathered, d_projected, preferred_element_type=jnp.float32)
    g_bias_all = jnp.sum(d_projected.astype(jnp.float32), axis=0)
    d_rows = lax.psum_scatter(
        rows_back(d_projected, attn_w).astype(jnp.bfloat16),
        "tensor",
        scatter_dimension=0,
        tiled=True,
    ).astype(jnp.float32)
    d_rows = d_rows + d_resid_one
    grads = (
        g_attn,
        g_bias_all,
        g_proj,
        g_proj_bias,
        g_gain_one,
        g_shift_one,
        g_up,
        g_up_bias,
        g_down,
        g_down_bias,
        g_gain_two,
        g_shift_two,
    )
    return (d_rows, grads)


def body(
    layer_input,
    cotangent,
    region_count,
    region_mask,
    attn_weight,
    attn_bias,
    proj_weight,
    proj_bias,
    first_gain,
    first_shift,
    up_weight,
    up_bias,
    down_weight,
    down_bias,
    second_gain,
    second_shift,
):
    section_id = lax.axis_index("section")
    micro_count = layer_input.shape[0]
    local_heads = attn_weight.shape[2]
    width = attn_weight.shape[1]
    bias_pieces = attn_bias[0].reshape(local_heads, 2, -1)
    full_bias = jnp.stack(
        [bias_pieces[:, 0], jnp.zeros_like(bias_pieces[:, 0]), bias_pieces[:, 1]], axis=1
    ).reshape(-1)
    attn_local = attn_weight[0].reshape(width, -1)
    proj_local = proj_weight[0].reshape(-1, width)
    up_local = up_weight[0]
    down_local = down_weight[0]
    unit_bias = up_bias[0]
    allowed = key_allowed(region_count, region_mask)
    params = (
        attn_local,
        full_bias,
        proj_local,
        proj_bias[0],
        first_gain[0],
        first_shift[0],
        up_local,
        unit_bias,
        down_local,
        down_bias[0],
        second_gain[0],
        second_shift[0],
    )
    received = jnp.zeros_like(layer_input[0])
    outputs_list = []
    inputs_list = []
    allowed_list = []
    for moment in range(micro_count + 1):
        own_rows = layer_input[min(moment, micro_count - 1)]
        section_rows = jnp.where(section_id == 0, own_rows, received)
        allowed_now = jnp.where(
            section_id == 0, allowed[min(moment, micro_count - 1)], allowed[max(moment - 1, 0)]
        )
        result, saved = forward_layer(section_rows, allowed_now, params)
        outputs_list.append(result)
        inputs_list.append(section_rows)
        allowed_list.append(allowed_now)
        if moment < micro_count:
            received = passed_along(result, "section", 1)
    layer_outputs = jnp.where(
        section_id == 0, jnp.stack(outputs_list[:micro_count]), jnp.stack(outputs_list[1:])
    )
    sent_back = jnp.zeros_like(layer_input[0])
    grad_list = []
    totals = None
    for moment in range(micro_count + 1):
        later = min(moment + 1, micro_count)
        earlier = max(moment - 1, 0)
        grad_in = jnp.where(
            section_id == 1, cotangent[min(moment, micro_count - 1)], sent_back
        ).astype(jnp.float32)
        again_rows = jnp.where(section_id == 1, inputs_list[later], inputs_list[earlier])
        again_allowed = jnp.where(section_id == 1, allowed_list[later], allowed_list[earlier])
        _, saved = forward_layer(again_rows, again_allowed, params)
        d_rows, grads = backward_layer(grad_in, saved, params)
        useful = jnp.where(section_id == 1, moment < micro_count, moment >= 1)
        masked_grads = jax.tree.map(lambda member: jnp.where(useful, member, 0.0), grads)
        if totals is None:
            totals = masked_grads
        else:
            totals = jax.tree.map(lambda running, member: running + member, totals, masked_grads)
        grad_list.append(d_rows)
        if moment < micro_count:
            sent_back = passed_along(d_rows.astype(jnp.bfloat16), "section", -1)
    input_grads = jnp.where(
        section_id == 1, jnp.stack(grad_list[:micro_count]), jnp.stack(grad_list[1:])
    )
    shares = (totals[0], totals[1], totals[2], totals[6], totals[7], totals[8])
    big_sums = (
        lax.psum(shares[0].astype(jnp.bfloat16), "dp").astype(jnp.float32),
        lax.psum(shares[1].astype(jnp.bfloat16), "dp").astype(jnp.float32),
        lax.psum(shares[2].astype(jnp.bfloat16), "dp").astype(jnp.float32),
        lax.psum(shares[3].astype(jnp.bfloat16), "dp").astype(jnp.float32),
        lax.psum(shares[4].astype(jnp.bfloat16), "dp").astype(jnp.float32),
        lax.psum(shares[5].astype(jnp.bfloat16), "dp").astype(jnp.float32),
    )
    row_totals = lax.psum(
        (totals[3], totals[4], totals[5], totals[9], totals[10], totals[11]), ("dp", "tensor")
    )
    bias_sum = big_sums[1].reshape(local_heads, 3, -1)
    grad_attn_bias = jnp.concatenate([bias_sum[:, 0], bias_sum[:, 2]], axis=1)
    return (
        layer_outputs[None],
        input_grads[None],
        big_sums[0].reshape(attn_weight.shape),
        grad_attn_bias[None],
        big_sums[2].reshape(proj_weight.shape),
        row_totals[0][None],
        row_totals[1][None],
        row_totals[2][None],
        big_sums[3][None],
        big_sums[4][None],
        big_sums[5][None],
        row_totals[3][None],
        row_totals[4][None],
        row_totals[5][None],
    )


def solution(mesh):
    placed = (
        P(None, ("dp", "tensor"), None),
        P(None, ("dp", "tensor"), None),
        P(None, "dp"),
        P(None, "dp", None),
        P("section", None, "tensor", None),
        P("section", "tensor", None),
        P("section", "tensor", None, None),
        P("section", None),
        P("section", None),
        P("section", None),
        P("section", None, "tensor"),
        P("section", "tensor"),
        P("section", "tensor", None),
        P("section", None),
        P("section", None),
        P("section", None),
    )
    return jax.shard_map(
        body,
        mesh=mesh,
        in_specs=placed,
        out_specs=(
            P("section", None, ("dp", "tensor"), None),
            P("section", None, ("dp", "tensor"), None),
            P("section", None, "tensor", None),
            P("section", "tensor", None),
            P("section", "tensor", None, None),
            P("section", None),
            P("section", None),
            P("section", None),
            P("section", None, "tensor"),
            P("section", "tensor"),
            P("section", "tensor", None),
            P("section", None),
            P("section", None),
            P("section", None),
        ),
        check_vma=False,
    )
```

profile of v0, /device:TPU:0, one launch (start us, length us, event | category | flops | bytes accessed | tf_op | source)
XLA Modules:
  0.0 1860.6 jit_solution(16804892463501792652)
XLA Ops:
  42.2 26.3 %reduce-scatter.31.cloned.1.call-done = bf16[208,768]{1,0:T(8,128)(2,1)} async-done(((bf16[832,768]{1,0:T(8,128)(2,1)}), bf16[208,768]{1,0:T(8,128)(2,1)}) %reduce-scatter.31.cloned.1.call-update) | async-done | bytes 319504 | tf_op jit(solution)/shard_map/reduce_scatter | solution.py:90
  101.4 26.3 %reduce-scatter.33.cloned.1.call-done = bf16[208,768]{1,0:T(8,128)(2,1)} async-done(((bf16[832,768]{1,0:T(8,128)(2,1)}), bf16[208,768]{1,0:T(8,128)(2,1)}) %reduce-scatter.33.cloned.1.call-update) | async-done | bytes 319504 | tf_op jit(solution)/shard_map/reduce_scatter | solution.py:101
  173.2 26.4 %reduce-scatter.51.cloned.1.call-done = bf16[208,768]{1,0:T(8,128)(2,1)} async-done(((bf16[832,768]{1,0:T(8,128)(2,1)}), bf16[208,768]{1,0:T(8,128)(2,1)}) %reduce-scatter.51.cloned.1.call-update) | async-done | bytes 319504 | tf_op jit(solution)/shard_map/reduce_scatter | solution.py:90
  236.4 25.7 %reduce-scatter.53.cloned.1.call-done = bf16[208,768]{1,0:T(8,128)(2,1)} async-done(((bf16[832,768]{1,0:T(8,128)(2,1)}), bf16[208,768]{1,0:T(8,128)(2,1)}) %reduce-scatter.53.cloned.1.call-update) | async-done | bytes 319504 | tf_op jit(solution)/shard_map/reduce_scatter | solution.py:101
  310.8 20.5 %reduce-scatter.35.cloned.1.call-done = bf16[208,768]{1,0:T(8,128)(2,1)} async-done(((bf16[832,768]{1,0:T(8,128)(2,1)}), bf16[208,768]{1,0:T(8,128)(2,1)}) %reduce-scatter.35.cloned.1.call-update) | async-done | bytes 319504 | tf_op jit(solution)/shard_map/reduce_scatter | solution.py:90
  331.3 29.6 %reduce-scatter.55.cloned.1.call-done = bf16[208,768]{1,0:T(8,128)(2,1)} async-done(((bf16[832,768]{1,0:T(8,128)(2,1)}), bf16[208,768]{1,0:T(8,128)(2,1)}) %reduce-scatter.55.cloned.1.call-update) | async-done | bytes 319504 | tf_op jit(solution)/shard_map/reduce_scatter | solution.py:141
  393.7 26.4 %reduce-scatter.37.cloned.1.call-done = bf16[208,768]{1,0:T(8,128)(2,1)} async-done(((bf16[832,768]{1,0:T(8,128)(2,1)}), bf16[208,768]{1,0:T(8,128)(2,1)}) %reduce-scatter.37.cloned.1.call-update) | async-done | bytes 319504 | tf_op jit(solution)/shard_map/reduce_scatter | solution.py:101
  469.4 26.4 %reduce-scatter.59.cloned.1.call-done = bf16[208,768]{1,0:T(8,128)(2,1)} async-done(((bf16[832,768]{1,0:T(8,128)(2,1)}), bf16[208,768]{1,0:T(8,128)(2,1)}) %reduce-scatter.59.cloned.1.call-update) | async-done | bytes 319504 | tf_op jit(solution)/shard_map/reduce_scatter | solution.py:90
  530.7 26.4 %reduce-scatter.61.cloned.1.call-done = bf16[208,768]{1,0:T(8,128)(2,1)} async-done(((bf16[832,768]{1,0:T(8,128)(2,1)}), bf16[208,768]{1,0:T(8,128)(2,1)}) %reduce-scatter.61.cloned.1.call-update) | async-done | bytes 319504 | tf_op jit(solution)/shard_map/reduce_scatter | solution.py:101
  601.3 25.7 %reduce-scatter.57.cloned.1.call-done = bf16[208,768]{1,0:T(8,128)(2,1)} async-done(((bf16[832,768]{1,0:T(8,128)(2,1)}), bf16[208,768]{1,0:T(8,128)(2,1)}) %reduce-scatter.57.cloned.1.call-update) | async-done | bytes 319504 | tf_op jit(solution)/shard_map/reduce_scatter | solution.py:180
  695.8 29.6 %reduce-scatter.63.cloned.1.call-done = bf16[208,768]{1,0:T(8,128)(2,1)} async-done(((bf16[832,768]{1,0:T(8,128)(2,1)}), bf16[208,768]{1,0:T(8,128)(2,1)}) %reduce-scatter.63.cloned.1.call-update) | async-done | bytes 319504 | tf_op jit(solution)/shard_map/reduce_scatter | solution.py:141
  758.4 26.4 %reduce-scatter.41.cloned.1.call-done = bf16[208,768]{1,0:T(8,128)(2,1)} async-done(((bf16[832,768]{1,0:T(8,128)(2,1)}), bf16[208,768]{1,0:T(8,128)(2,1)}) %reduce-scatter.41.cloned.1.call-update) | async-done | bytes 319504 | tf_op jit(solution)/shard_map/reduce_scatter | solution.py:101
  836.1 26.4 %reduce-scatter.67.cloned.1.call-done = bf16[208,768]{1,0:T(8,128)(2,1)} async-done(((bf16[832,768]{1,0:T(8,128)(2,1)}), bf16[208,768]{1,0:T(8,128)(2,1)}) %reduce-scatter.67.cloned.1.call-update) | async-done | bytes 319504 | tf_op jit(solution)/shard_map/reduce_scatter | solution.py:90
  940.1 25.8 %reduce-scatter.69.cloned.1.call-done = bf16[208,768]{1,0:T(8,128)(2,1)} async-done(((bf16[832,768]{1,0:T(8,128)(2,1)}), bf16[208,768]{1,0:T(8,128)(2,1)}) %reduce-scatter.69.cloned.1.call-update) | async-done | bytes 319504 | tf_op jit(solution)/shard_map/reduce_scatter | solution.py:101
  1034.5 29.6 %reduce-scatter.71.cloned.1.call-done = bf16[208,768]{1,0:T(8,128)(2,1)} async-done(((bf16[832,768]{1,0:T(8,128)(2,1)}), bf16[208,768]{1,0:T(8,128)(2,1)}) %reduce-scatter.71.cloned.1.call-update) | async-done | bytes 319504 | tf_op jit(solution)/shard_map/reduce_scatter | solution.py:141
  1097.1 26.4 %reduce-scatter.45.cloned.1.call-done = bf16[208,768]{1,0:T(8,128)(2,1)} async-done(((bf16[832,768]{1,0:T(8,128)(2,1)}), bf16[208,768]{1,0:T(8,128)(2,1)}) %reduce-scatter.45.cloned.1.call-update) | async-done | bytes 319504 | tf_op jit(solution)/shard_map/reduce_scatter | solution.py:101
  1175.7 26.4 %reduce-scatter.75.cloned.1.call-done = bf16[208,768]{1,0:T(8,128)(2,1)} async-done(((bf16[832,768]{1,0:T(8,128)(2,1)}), bf16[208,768]{1,0:T(8,128)(2,1)}) %reduce-scatter.75.cloned.1.call-update) | async-done | bytes 319504 | tf_op jit(solution)/shard_map/reduce_scatter | solution.py:90
  1280.1 25.8 %reduce-scatter.77.cloned.1.call-done = bf16[208,768]{1,0:T(8,128)(2,1)} async-done(((bf16[832,768]{1,0:T(8,128)(2,1)}), bf16[208,768]{1,0:T(8,128)(2,1)}) %reduce-scatter.77.cloned.1.call-update) | async-done | bytes 319504 | tf_op jit(solution)/shard_map/reduce_scatter | solution.py:101
  1353.3 21.0 %reduce-scatter.83.cloned.1.call-done = bf16[208,768]{1,0:T(8,128)(2,1)} async-done(((bf16[832,768]{1,0:T(8,128)(2,1)}), bf16[208,768]{1,0:T(8,128)(2,1)}) %reduce-scatter.83.cloned.1.call-update) | async-done | bytes 319504 | tf_op jit(solution)/shard_map/reduce_scatter | solution.py:90
  1374.2 29.6 %reduce-scatter.79.cloned.1.call-done = bf16[208,768]{1,0:T(8,128)(2,1)} async-done(((bf16[832,768]{1,0:T(8,128)(2,1)}), bf16[208,768]{1,0:T(8,128)(2,1)}) %reduce-scatter.79.cloned.1.call-update) | async-done | bytes 319504 | tf_op jit(solution)/shard_map/reduce_scatter | solution.py:141
  1480.8 26.4 %reduce-scatter.85.cloned.1.call-done = bf16[208,768]{1,0:T(8,128)(2,1)} async-done(((bf16[832,768]{1,0:T(8,128)(2,1)}), bf16[208,768]{1,0:T(8,128)(2,1)}) %reduce-scatter.85.cloned.1.call-update) | async-done | bytes 319504 | tf_op jit(solution)/shard_map/reduce_scatter | solution.py:101
  1585.2 20.3 %reduce-scatter.87.cloned.1.call-done = bf16[208,768]{1,0:T(8,128)(2,1)} async-done(((bf16[832,768]{1,0:T(8,128)(2,1)}), bf16[208,768]{1,0:T(8,128)(2,1)}) %reduce-scatter.87.cloned.1.call-update) | async-done | bytes 319504 | tf_op jit(solution)/shard_map/reduce_scatter | solution.py:141
  1683.9 62.6 %all-reduce.1 = (f32[1,768]{1,0:T(1,128)}, f32[1,768]{1,0:T(1,128)}, f32[1,768]{1,0:T(1,128)}, f32[1,768]{1,0:T(1,128)}, f32[1,768]{1,0:T(1,128)}, /*index=5*/f32[1,768]{1,0:T(1,128)}) all-reduce(f32[1,768]{1,0:T(1,128)S(1)} %broadcast_in_dim.394, ...), channel_id=1, replica_groups=mesh['section'=2,'dp'=4,'tensor'=4] {'dp','tensor'}, use_global_device_ids=true, to_apply=%region_128.129 | all-reduce | flops 4608 | bytes 36864 | tf_op jit(solution)/shard_map/psum | solution.py:303
  1765.6 80.0 %all-reduce.6.cloned.1.call-done = (bf16[1,768,3,192]{1,3,2,0:T(8,128)(2,1)}, bf16[1,3,64,768]{3,2,1,0:T(8,128)(2,1)}, bf16[1,768,768]{2,1,0:T(8,128)(2,1)}, bf16[1,768,768]{2,1,0:T(8,128)(2,1)}) async-done(((bf16[1,768,3,192]{1,3,2,0:T(8,128)(2,1)}, bf16[1,3,64,768]{3,2,1,0:T(8,128)(2,1)}, bf16[1,768,768]{2,1,0:T(8,128)(2,1)}, bf16[1,768,768]{2,1,0:T(8,128)(2,1)}), (bf16[1,768,3,192]{1,3,2,0:T(8,128)(2,1)}, ...) | async-done | bytes 3538960 | tf_op jit(solution)/shard_map/psum | solution.py:296
  (964 shorter events, 1126.2 us)
Async XLA Ops:
  236.4 65.4 %all-gather.54.cloned.1.call-start = ((), (), s32[]{:S(2)}) async-start(), calls=%async_computation.53 | async-start | bytes 1597440 | tf_op jit(solution)/shard_map/all_gather | solution.py:133
  310.7 72.7 %all-gather.36.cloned.1.call-start = ((), (), s32[]{:S(2)}) async-start(), calls=%async_computation.35 | async-start | bytes 1597440 | tf_op jit(solution)/shard_map/all_gather | solution.py:98
  561.4 65.6 %reduce-scatter.57.cloned.1.call-start = ((), (), s32[]{:S(2)}) async-start(), calls=%async_computation.56 | async-start | bytes 1597440 | tf_op jit(solution)/shard_map/reduce_scatter | solution.py:180
  601.3 67.3 %all-gather.62.cloned.1.call-start = ((), (), s32[]{:S(2)}) async-start(), calls=%async_computation.61 | async-start | bytes 1597440 | tf_op jit(solution)/shard_map/all_gather | solution.py:133
  677.5 70.6 %all-gather.40.cloned.1.call-start = ((), (), s32[]{:S(2)}) async-start(), calls=%async_computation.39 | async-start | bytes 1597440 | tf_op jit(solution)/shard_map/all_gather | solution.py:98
  798.6 63.9 %reduce-scatter.67.cloned.1.call-start = ((), (), s32[]{:S(2)}) async-start(), calls=%async_computation.66 | async-start | bytes 1597440 | tf_op jit(solution)/shard_map/reduce_scatter | solution.py:90
  869.7 66.6 %reduce-scatter.65.cloned.1.call-start = ((), (), s32[]{:S(2)}) async-start(), calls=%async_computation.64 | async-start | bytes 1597440 | tf_op jit(solution)/shard_map/reduce_scatter | solution.py:180
  920.4 65.0 %all-gather.42.cloned.1.call-start = ((), (), s32[]{:S(2)}) async-start(), calls=%async_computation.41 | async-start | bytes 1597440 | tf_op jit(solution)/shard_map/all_gather | solution.py:75
  921.0 84.4 %all-gather.70.cloned.1.call-start = ((), (), s32[]{:S(2)}) async-start(), calls=%async_computation.69 | async-start | bytes 1597440 | tf_op jit(solution)/shard_map/all_gather | solution.py:133
  970.8 63.8 %reduce-scatter.43.cloned.1.call-start = ((), (), s32[]{:S(2)}) async-start(), calls=%async_computation.42 | async-start | bytes 1597440 | tf_op jit(solution)/shard_map/reduce_scatter | solution.py:90
  1014.4 72.5 %all-gather.44.cloned.1.call-start = ((), (), s32[]{:S(2)}) async-start(), calls=%async_computation.43 | async-start | bytes 1597440 | tf_op jit(solution)/shard_map/all_gather | solution.py:98
  1138.1 64.0 %reduce-scatter.75.cloned.1.call-start = ((), (), s32[]{:S(2)}) async-start(), calls=%async_computation.74 | async-start | bytes 1597440 | tf_op jit(solution)/shard_map/reduce_scatter | solution.py:90
  1209.2 67.0 %reduce-scatter.73.cloned.1.call-start = ((), (), s32[]{:S(2)}) async-start(), calls=%async_computation.72 | async-start | bytes 1597440 | tf_op jit(solution)/shard_map/reduce_scatter | solution.py:180
  1241.3 64.7 %reduce-scatter.77.cloned.1.call-start = ((), (), s32[]{:S(2)}) async-start(), calls=%async_computation.76 | async-start | bytes 1597440 | tf_op jit(solution)/shard_map/reduce_scatter | solution.py:101
  1260.5 64.9 %all-gather.82.cloned.1.call-start = ((), (), s32[]{:S(2)}) async-start(), calls=%async_computation.81 | async-start | bytes 1597440 | tf_op jit(solution)/shard_map/all_gather | solution.py:75
  1261.1 83.7 %all-gather.78.cloned.1.call-start = ((), (), s32[]{:S(2)}) async-start(), calls=%async_computation.77 | async-start | bytes 1597440 | tf_op jit(solution)/shard_map/all_gather | solution.py:133
  1353.2 74.7 %all-gather.80.cloned.1.call-start = ((), (), s32[]{:S(2)}) async-start(), calls=%async_computation.79 | async-start | bytes 1597440 | tf_op jit(solution)/shard_map/all_gather | solution.py:148
  1410.5 67.0 %reduce-scatter.81.cloned.1.call-start = ((), (), s32[]{:S(2)}) async-start(), calls=%async_computation.80 | async-start | bytes 1597440 | tf_op jit(solution)/shard_map/reduce_scatter | solution.py:180
  1461.8 64.9 %all-gather.46.cloned.1.call-start = ((), (), s32[]{:S(2)}) async-start(), calls=%async_computation.45 | async-start | bytes 1597440 | tf_op jit(solution)/shard_map/all_gather | solution.py:75
  1462.3 95.7 %all-gather.86.cloned.1.call-start = ((), (), s32[]{:S(2)}) async-start(), calls=%async_computation.85 | async-start | bytes 1597440 | tf_op jit(solution)/shard_map/all_gather | solution.py:133
  1511.3 73.9 %reduce-scatter.47.cloned.1.call-start = ((), (), s32[]{:S(2)}) async-start(), calls=%async_computation.46 | async-start | bytes 1597440 | tf_op jit(solution)/shard_map/reduce_scatter | solution.py:90
  1620.2 137.0 %reduce-scatter.49.cloned.1.call-start = ((), (), s32[]{:S(2)}) async-start(), calls=%async_computation.48 | async-start | bytes 1597440 | tf_op jit(solution)/shard_map/reduce_scatter | solution.py:101
  1638.3 120.5 %reduce-scatter.89.cloned.1.call-start = ((), (), s32[]{:S(2)}) async-start(), calls=%async_computation.88 | async-start | bytes 1597440 | tf_op jit(solution)/shard_map/reduce_scatter | solution.py:180
  1666.1 179.6 %all-reduce.6.cloned.1.call-start = ((), (), s32[]{:S(2)}) async-start(), calls=%async_computation.90 | async-start | bytes 7077888 | tf_op jit(solution)/shard_map/psum | solution.py:296
  (247 other events, 4502.2 us)
Sparse Core Ops, SparseCore 0:
  101.3 26.3 reduce-scatter.32
  173.2 26.3 reduce-scatter.50
  235.7 26.3 reduce-scatter.52
  334.5 26.3 reduce-scatter.54
  393.8 26.3 reduce-scatter.36
  469.4 26.3 reduce-scatter.58
  530.8 26.3 reduce-scatter.60
  669.4 26.3 reduce-scatter.38
  699.0 26.3 reduce-scatter.62
  909.9 26.3 reduce-scatter.64
  939.6 26.3 reduce-scatter.68
  1008.2 26.3 reduce-scatter.42
  1037.7 26.3 reduce-scatter.70
  1097.2 26.3 reduce-scatter.44
  1175.7 26.3 reduce-scatter.74
  1249.9 26.3 reduce-scatter.72
  1279.6 26.3 reduce-scatter.76
  1347.9 26.3 reduce-scatter.82
  1377.4 26.3 reduce-scatter.78
  1451.1 26.3 reduce-scatter.80
  1549.4 26.3 reduce-scatter.46
  1650.6 26.3 reduce-scatter.48
  1679.7 26.4 reduce-scatter.88
  1710.0 135.5 all-reduce.5
  (37 shorter events, 729.1 us)
where the time goes:
time: 1870 us; the launch traced here: 1860 us
  waiting for transfers between devices  1120 us (60%)
  matrix products  353 us (19%)
  local copies, waits for them, and re-layouts  135 us (7%)
  other arithmetic  134 us (7%)
  blocking collectives  72 us (4%)
  starting transfers between devices  25.5 us (1%)
    reduce_scatter x10, waiting for transfers between devices, forward_layer(): lax.psum_scatter(rows_product(activated, down_w).astype(jnp.bfloat16), 't...  236 us
    reduce_scatter x10, waiting for transfers between devices, forward_layer(): lax.psum_scatter(rows_product(context, proj_w).astype(jnp.bfloat16), 'ten...  212 us
    all_gather x10, waiting for transfers between devices, forward_layer(): gathered = lax.all_gather(rows_in, 'tensor', axis=0, tiled=True)  152 us
    reduce_scatter x5, waiting for transfers between devices, backward_layer(): lax.psum_scatter(rows_back(d_upward, up_w).astype(jnp.bfloat16), 'tensor'...  139 us
    all_gather x10, waiting for transfers between devices, forward_layer(): lax.all_gather(hidden.astype(jnp.bfloat16), 'tensor', axis=0, tiled=True)  119 us
    dot_general x20, matrix products, rows_product(): return jnp.dot(source, weight, preferred_element_type=jnp.float32)  90.2 us
    psum x1, waiting for transfers between devices, body(): lax.psum(shares[0].astype(jnp.bfloat16), 'dp').astype(jnp.float32)  80 us
    all_gather x5, waiting for transfers between devices, backward_layer(): lax.all_gather(d_resid_one.astype(jnp.bfloat16), 'tensor', axis=0, tiled=...  72.8 us
  transfers between devices with their start and end apart: 69, of which 59 were waited for; matrix products, arithmetic and copies ran while one was open for 20% of the time, Pallas kernels for 0%

commit v1 on v0

v1 whole, which is shorter than its diff:
```python
import jax
import jax.numpy as jnp
from jax import lax
from jax.sharding import PartitionSpec as P

HD = 64
CAPTION = 128
SEQLEN = 208

norm_eps = 1e-06
masked_value = -1000000000.0
BF = jnp.bfloat16
F32 = jnp.float32


def layer_norm(residual, gain_vec, shift_vec):
    center = residual - jnp.mean(residual, axis=-1, keepdims=True)
    spread = jnp.mean(center * center, axis=-1, keepdims=True)
    return center * lax.rsqrt(spread + norm_eps) * gain_vec + shift_vec


def norm_parts(residual):
    center = residual - jnp.mean(residual, axis=-1, keepdims=True)
    rstd = lax.rsqrt(jnp.mean(center * center, axis=-1, keepdims=True) + norm_eps)
    return center * rstd, rstd


def norm_back(grad, normed, rstd, gain):
    g = grad * gain
    return rstd * (
        g
        - jnp.mean(g, axis=-1, keepdims=True)
        - normed * jnp.mean(g * normed, axis=-1, keepdims=True)
    )


def exact_gelu(inputs):
    return jax.nn.gelu(inputs, approximate=False)


def key_allowed(region_count, region_mask):
    regions = region_mask.shape[-1]
    slot_index = jnp.arange(CAPTION + regions, dtype=jnp.int32) - CAPTION
    caption_ones = jnp.ones(region_mask.shape[:-1] + (CAPTION,), jnp.int32)
    present = jnp.concatenate([caption_ones, region_mask], axis=-1) > 0
    return present & (slot_index < region_count[..., None])


def mm(a, b):
    return jnp.dot(a, b, preferred_element_type=F32)


def mm_t(a, b):
    return jnp.einsum("nf,df->nd", a, b, preferred_element_type=F32)


def mm_rows(a, b):
    return jnp.einsum("nf,nd->fd", a, b, preferred_element_type=F32)


def split_heads(projected, sequences):
    pieces = projected.reshape(sequences, SEQLEN, -1, 3, HD)
    return (pieces[:, :, :, 0], pieces[:, :, :, 1], pieces[:, :, :, 2])


def masked_scores(queries, key_rows, allowed):
    scores = jnp.einsum("sqhd,skhd->shqk", queries, key_rows, preferred_element_type=F32) * 0.125
    return jnp.where(allowed[:, None, None, :], scores, masked_value)


def forward_layer(rows_in, allowed, params):
    attn_w, full_bias, proj_w, proj_b, gain_one, shift_one, up_w, up_b, down_w, down_b, gain_two, shift_two = params
    sequences = allowed.shape[0]
    projected = (mm(rows_in, attn_w) + full_bias).astype(BF)
    queries, key_rows, value_rows = split_heads(projected, sequences)
    scores = masked_scores(queries, key_rows, allowed)
    row_max = jnp.max(scores, axis=-1, keepdims=True)
    exp_scores = jnp.exp(scores - row_max)
    row_sum = jnp.sum(exp_scores, axis=-1, keepdims=True)
    weights_bf = (exp_scores / row_sum).astype(BF)
    log_total = row_max + jnp.log(row_sum)
    context = jnp.einsum("shqk,skhd->sqhd", weights_bf, value_rows, preferred_element_type=F32)
    context = context.astype(BF).reshape(rows_in.shape[0], -1)
    resid_one = rows_in.astype(F32) + mm(context, proj_w) + proj_b
    hidden = layer_norm(resid_one, gain_one, shift_one)
    middle = hidden.astype(BF)
    upward = mm(middle, up_w) + up_b
    activated = exact_gelu(upward).astype(BF)
    resid_two = hidden + mm(activated, down_w) + down_b
    output = layer_norm(resid_two, gain_two, shift_two).astype(BF)
    saved = (rows_in, projected, log_total, context, resid_one, middle, upward, activated, resid_two, allowed)
    return output, saved


def backward_layer(grad_out, saved, params, full):
    attn_w, full_bias, proj_w, proj_b, gain_one, shift_one, up_w, up_b, down_w, down_b, gain_two, shift_two = params
    rows_in, projected, log_total, context, resid_one, middle, upward, activated, resid_two, allowed = saved
    sequences = allowed.shape[0]
    n_two, r_two = norm_parts(resid_two)
    d_resid_two = norm_back(grad_out, n_two, r_two, gain_two)
    feed_rows = d_resid_two.astype(BF)
    d_activated = mm_t(feed_rows, down_w)
    _, gelu_back = jax.vjp(exact_gelu, upward)
    d_upward = gelu_back(d_activated)[0].astype(BF)
    d_hidden = d_resid_two + mm_t(d_upward, up_w)
    n_one, r_one = norm_parts(resid_one)
    d_resid_one = norm_back(d_hidden, n_one, r_one, gain_one)
    attn_rows = d_resid_one.astype(BF)
    d_context = mm_t(attn_rows, proj_w).astype(BF)
    queries, key_rows, value_rows = split_heads(projected, sequences)
    d_context = d_context.reshape(queries.shape)
    scores = masked_scores(queries, key_rows, allowed)
    probs_full = jnp.exp(scores - log_total)
    weights_bf = probs_full.astype(BF)
    d_values = jnp.einsum("shqk,sqhd->skhd", weights_bf, d_context, preferred_element_type=F32)
    d_weights = jnp.einsum("sqhd,skhd->shqk", d_context, value_rows, preferred_element_type=F32)
    d_scores = probs_full * (d_weights - jnp.sum(d_weights * probs_full, axis=-1, keepdims=True))
    d_scores = d_scores.astype(BF)
    d_queries = jnp.einsum("shqk,skhd->sqhd", d_scores, key_rows, preferred_element_type=F32) * 0.125
    d_keys = jnp.einsum("shqk,sqhd->skhd", d_scores, queries, preferred_element_type=F32) * 0.125
    d_projected = jnp.stack([d_queries, d_keys, d_values], axis=3).reshape(projected.shape).astype(BF)
    d_rows = d_resid_one + mm_t(d_projected, attn_w)
    if not full:
        return d_rows, None
    grads = dict(
        down=mm_rows(activated, feed_rows).astype(BF),
        up=mm_rows(middle, d_upward).astype(BF),
        proj=mm_rows(context, attn_rows).astype(BF),
        attn=mm_rows(rows_in, d_projected).astype(BF),
        attn_bias=jnp.sum(d_projected.astype(F32), axis=0),
        up_bias=jnp.sum(d_upward.astype(F32), axis=0),
        gain_two=jnp.sum(grad_out * n_two, axis=0),
        shift_two=jnp.sum(grad_out, axis=0),
        down_bias=jnp.sum(d_resid_two, axis=0),
        gain_one=jnp.sum(d_hidden * n_one, axis=0),
        shift_one=jnp.sum(d_hidden, axis=0),
        proj_bias=jnp.sum(d_resid_one, axis=0),
    )
    return d_rows, grads


def swapped(value, axis, bit):
    count = lax.axis_size(axis)
    return lax.ppermute(value, axis, [(i, i ^ bit) for i in range(count)])


def chain_sum(value, axis):
    count = lax.axis_size(axis)
    if count == 1:
        return value
    if count % 2:
        return lax.psum(value, axis)
    here = lax.axis_index(axis)
    half = count // 2
    for step in range(half - 1):
        got = lax.ppermute(value, axis, [(step, step + 1), (count - 1 - step, count - 2 - step)])
        takes = (here == step + 1) | (here == count - 2 - step)
        value = jnp.where(takes, value + got, value)
    got = lax.ppermute(value, axis, [(half - 1, half), (half, half - 1)])
    value = value + got
    for step in range(half - 1, 0, -1):
        got = lax.ppermute(value, axis, [(step, step - 1), (count - 1 - step, count - step)])
        takes = (here == step - 1) | (here == count - step)
        value = jnp.where(takes, got, value)
    return value


def gathered(value):
    far = swapped(value, "tensor", 2)
    return [value, swapped(value, "tensor", 1), far, swapped(far, "tensor", 1)]


def scattered(parts):
    own, near, far, both = parts
    keep = own + swapped(near, "tensor", 1)
    send = far + swapped(both, "tensor", 1)
    return keep + swapped(send, "tensor", 2)


def body(
    layer_input, cotangent, region_count, region_mask, attn_weight, attn_bias, proj_weight, proj_bias,
    first_gain, first_shift, up_weight, up_bias, down_weight, down_bias, second_gain, second_shift,
):
    section = lax.axis_index("section")
    tensor = lax.axis_index("tensor")
    micro, rows, width = layer_input.shape
    local_heads = attn_weight.shape[2]
    local_units = up_weight.shape[2]
    ranks = lax.axis_size("tensor")
    assert rows == SEQLEN and ranks == 4

    pieces = attn_bias[0].reshape(local_heads, 2, -1)
    own_bias = jnp.stack([pieces[:, 0], jnp.zeros_like(pieces[:, 0]), pieces[:, 1]], axis=1).reshape(-1)
    small = jnp.concatenate([own_bias, up_bias[0]]).reshape(1, -1)
    smalls = gathered(small)
    cut = own_bias.shape[0]
    full_bias = jnp.concatenate([s[0, :cut] for s in smalls])
    unit_bias = jnp.concatenate([s[0, cut:] for s in smalls])
    attn_w = jnp.concatenate(gathered(attn_weight[0].reshape(width, -1)), axis=1)
    proj_w = jnp.concatenate(gathered(proj_weight[0].reshape(-1, width)), axis=0)
    up_w = jnp.concatenate(gathered(up_weight[0]), axis=1)
    down_w = jnp.concatenate(gathered(down_weight[0]), axis=0)
    params = (
        attn_w, full_bias, proj_w, proj_bias[0], first_gain[0], first_shift[0],
        up_w, unit_bias, down_w, down_bias[0], second_gain[0], second_shift[0],
    )
    allowed = lax.dynamic_index_in_dim(key_allowed(region_count, region_mask), tensor, 1, False)

    own_rows = layer_input.reshape(micro * rows, width)
    out_one, _ = forward_layer(own_rows, allowed, params)
    received = lax.ppermute(out_one, "section", [(0, 1)])
    rows_in = jnp.where(section == 0, own_rows, received)
    output, saved = forward_layer(rows_in, allowed, params)
    saved = lax.optimization_barrier(saved)
    cot = cotangent.reshape(micro * rows, width)
    d_first, _ = backward_layer(cot.astype(F32), saved, params, False)
    sent = lax.ppermute(d_first.astype(BF), "section", [(1, 0)])
    grad_in = jnp.where(section == 1, cot, sent).astype(F32)
    d_rows, grads = backward_layer(grad_in, saved, params, True)

    def column_parts(value):
        size = value.shape[1] // ranks
        return [value[:, r * size:(r + 1) * size] for r in range(ranks)]

    def row_parts(value):
        size = value.shape[0] // ranks
        return [value[r * size:(r + 1) * size] for r in range(ranks)]

    def total(parts):
        return chain_sum(scattered(parts), "dp").astype(F32)

    g_down = total(row_parts(grads["down"]))
    g_up = total(column_parts(grads["up"]))
    g_proj = total(row_parts(grads["proj"]))
    g_attn = total(column_parts(grads["attn"]))

    def canonical(vector):
        quarters = vector.reshape(ranks, -1)
        return jnp.concatenate([lax.dynamic_index_in_dim(quarters, q ^ tensor, 0, False) for q in range(ranks)])

    names = ("proj_bias", "gain_one", "shift_one", "down_bias", "gain_two", "shift_two")
    flat = jnp.concatenate([grads[k] for k in names] + [canonical(grads["attn_bias"]), canonical(grads["up_bias"])])
    flat = lax.psum(flat, ("dp", "tensor"))
    rowed = {k: flat[i * width:(i + 1) * width] for i, k in enumerate(names)}
    base = len(names) * width
    bias_sum = lax.dynamic_slice_in_dim(flat, base + tensor * cut, cut).reshape(local_heads, 3, -1)
    grad_attn_bias = jnp.concatenate([bias_sum[:, 0], bias_sum[:, 2]], axis=1)
    g_up_bias = lax.dynamic_slice_in_dim(flat, base + ranks * cut + tensor * local_units, local_units)
    return (
        output.reshape(1, micro, rows, width),
        d_rows.reshape(1, micro, rows, width),
        g_attn.reshape(attn_weight.shape),
        grad_attn_bias[None],
        g_proj.reshape(proj_weight.shape),
        rowed["proj_bias"][None],
        rowed["gain_one"][None],
        rowed["shift_one"][None],
        g_up[None],
        g_up_bias[None],
        g_down[None],
        rowed["down_bias"][None],
        rowed["gain_two"][None],
        rowed["shift_two"][None],
    )


def solution(mesh):
    placed = (
        P(None, ("dp", "tensor"), None),
        P(None, ("dp", "tensor"), None),
        P(None, "dp"),
        P(None, "dp", None),
        P("section", None, "tensor", None),
        P("section", "tensor", None),
        P("section", "tensor", None, None),
        P("section", None),
        P("section", None),
        P("section", None),
        P("section", None, "tensor"),
        P("section", "tensor"),
        P("section", "tensor", None),
        P("section", None),
        P("section", None),
        P("section", None),
    )
    return jax.shard_map(
        body,
        mesh=mesh,
        in_specs=placed,
        out_specs=(
            P("section", None, ("dp", "tensor"), None),
            P("section", None, ("dp", "tensor"), None),
            P("section", None, "tensor", None),
            P("section", "tensor", None),
            P("section", "tensor", None, None),
            P("section", None),
            P("section", None),
            P("section", None),
            P("section", None, "tensor"),
            P("section", "tensor"),
            P("section", "tensor", None),
            P("section", None),
            P("section", None),
            P("section", None),
        ),
        check_vma=False,
    )
```

time: 1870 us -> 973 us (0.52)
  waiting for transfers between devices: 1120 us -> 186 us
  local copies, waits for them, and re-layouts: 135 us -> 298 us
  matrix products: 353 us -> 240 us
  other arithmetic: 134 us -> 109 us
  starting transfers between devices: 25.5 us -> 49.5 us
    reduce_scatter x30 -> x0, waiting for transfers between devices: 657 us -> none  [the longest x10 236 us: forward_layer(): lax.psum_scatter(rows_product(activated, down_w).astype(jnp.bfloat16), 't...]
    all_gather x30 -> x0, waiting for transfers between devices: 345 us -> none  [the longest x10 152 us: forward_layer(): gathered = lax.all_gather(rows_in, 'tensor', axis=0, tiled=True)]
    ppermute x8 -> x41, waiting for transfers between devices: 35.5 us -> 186 us  [the longest x27 93.3 us: swapped(): return lax.ppermute(value, axis, [(i, i ^ bit) for i in range(count)])]
    dot_general x85 -> x25, matrix products: 304 us -> 206 us  [the longest x8 92.3 us: mm(): return jnp.dot(a, b, preferred_element_type=F32)]
    psum x1 -> x0, waiting for transfers between devices: 80 us -> none  [body(): lax.psum(shares[0].astype(jnp.bfloat16), 'dp').astype(jnp.float32)]
    unnamed x404 -> x145, local copies, waits for them, and re-layouts: 26.2 us -> 103 us
    slice x10 -> x3, local copies, waits for them, and re-layouts: 17.8 us -> 66.7 us  [split_heads(): return (pieces[:, :, :, 0], pieces[:, :, :, 1], pieces[:, :, :, 2])]
    reduce_sum x41 -> x9, other arithmetic: 56.8 us -> 14.9 us  [the longest x1 3.67 us: backward_layer(): jnp.sum(d_resid_two, axis=0)]
  transfers between devices with their start and end apart: 69 -> 41, of which waited for: 59 -> 11; matrix products, arithmetic and copies ran while one was open for 20% -> 19% of each run, Pallas kernels for 0% -> 0%
where the time goes in v1:
time: 973 us; the launch traced here: 963 us
  local copies, waits for them, and re-layouts  298 us (31%)
  matrix products  240 us (25%)
  waiting for transfers between devices  186 us (19%)
  other arithmetic  109 us (11%)
  blocking collectives  77.7 us (8%)
  starting transfers between devices  49.5 us (5%)
    unnamed x145, local copies, waits for them, and re-layouts  103 us
    ppermute x27, waiting for transfers between devices, swapped(): return lax.ppermute(value, axis, [(i, i ^ bit) for i in range(count)])  93.3 us
    dot_general x8, matrix products, mm(): return jnp.dot(a, b, preferred_element_type=F32)  92.3 us
    psum x1, blocking collectives, body(): flat = lax.psum(flat, ('dp', 'tensor'))  77.7 us
    dot_general x8, matrix products, mm_t(): return jnp.einsum('nf,df->nd', a, b, preferred_element_type=F32)  74.4 us
    slice x3, local copies, waits for them, and re-layouts, split_heads(): return (pieces[:, :, :, 0], pieces[:, :, :, 1], pieces[:, :, :, 2])  66.7 us
    reshape x3, local copies, waits for them, and re-layouts, split_heads(): pieces = projected.reshape(sequences, SEQLEN, -1, 3, HD)  58.3 us
    ppermute x1, waiting for transfers between devices, body(): sent = lax.ppermute(d_first.astype(BF), 'section', [(1, 0)])  31.2 us
  transfers between devices with their start and end apart: 41, of which 11 were waited for; matrix products, arithmetic and copies ran while one was open for 19% of the time, Pallas kernels for 0%

profile of v1, /device:TPU:0, one launch (start us, length us, event | category | flops | bytes accessed | tf_op | source)
XLA Modules:
  0.0 963.4 jit_solution(11323209984444811324)
XLA Ops:
  8.7 15.6 %collective-permute-done.1 = bf16[768,576]{0,1:T(8,128)(2,1)S(1)} collective-permute-done((bf16[768,576]{0,1:T(8,128)(2,1)}, bf16[768,576]{0,1:T(8,128)(2,1)S(1)}, u32[]{:S(2)}, u32[]{:S(2)}) %collective-permute-start.1) | collective-permute-done | bytes 884768 | tf_op jit(solution)/shard_map/ppermute | solution.py:144
  33.5 21.9 %collective-permute-done.7 = bf16[192,768]{1,0:T(8,128)(2,1)} collective-permute-done((bf16[192,768]{1,0:T(8,128)(2,1)}, bf16[192,768]{1,0:T(8,128)(2,1)}, u32[]{:S(2)}, u32[]{:S(2)}) %collective-permute-start.7) | collective-permute-done | bytes 294944 | tf_op jit(solution)/shard_map/ppermute | solution.py:144
  64.5 19.6 %reshape.270 = bf16[4,208,12,3,64]{4,3,2,1,0:T(4,128)(2,1)} reshape(bf16[832,2304]{1,0:T(8,128)(2,1)} %fusion.37) | data formatting | bytes 7667712 | tf_op jit(solution)/shard_map/reshape | solution.py:62
  84.0 22.2 %fusion.175 = (bf16[4,208,12,1,64]{4,3,2,1,0:T(2,128)(2,1)}, bf16[4,208,12,1,64]{4,3,2,1,0:T(2,128)(2,1)}, bf16[4,208,12,1,64]{4,3,2,1,0:T(2,128)(2,1)}) fusion(bf16[4,208,12,3,64]{4,3,2,1,0:T(4,128)(2,1)} %reshape.270), kind=kLoop, calls=%fused_computation.303 | loop fusion | bytes 7667712 | tf_op jit(solution)/shard_map/slice | solution.py:63
  149.6 29.1 %fusion.3.clone.3.clone.5 = bf16[832,3072]{1,0:T(8,128)(2,1)S(1)} fusion(f32[3072]{0:T(1024)S(1)} %pad_maximum_fusion.5, f32[832,768]{1,0:T(8,128)S(1)} %get-tuple-element.160, f32[768]{0:T(1024)S(1)} %reduce.10, f32[768]{0:T(1024)S(1)} %reduce.9, f32[832]{0:T(1024)S(1)} %add_rsqrt_fusion.5, ...), kind=kOutput, calls=%fused_computation.6.clone.clone.clone.clone.clone.clone.clone.2 | convolution fusion | flops 4116627456 | bytes 12411392 | tf_op jit(solution)/shard_map/dot_general | solution.py:50
  192.8 26.1 %collective-permute-done.15 = bf16[832,768]{1,0:T(8,128)(2,1)} collective-permute-done((bf16[832,768]{1,0:T(8,128)(2,1)}, bf16[832,768]{1,0:T(8,128)(2,1)}, u32[]{:S(2)}, u32[]{:S(2)}) %collective-permute-start.15) | collective-permute-done | bytes 1277984 | tf_op jit(solution)/shard_map/ppermute | solution.py:211
  227.2 19.4 %reshape.271 = bf16[4,208,12,3,64]{4,3,2,1,0:T(4,128)(2,1)} reshape(bf16[832,2304]{1,0:T(8,128)(2,1)} %add_convert_fusion.2) | data formatting | bytes 7667712 | tf_op jit(solution)/shard_map/reshape | solution.py:62
  246.5 22.2 %fusion.174 = (bf16[4,208,12,1,64]{4,3,2,1,0:T(2,128)(2,1)}, bf16[4,208,12,1,64]{4,3,2,1,0:T(2,128)(2,1)}, bf16[4,208,12,1,64]{4,3,2,1,0:T(2,128)(2,1)}) fusion(bf16[4,208,12,3,64]{4,3,2,1,0:T(4,128)(2,1)} %reshape.271), kind=kLoop, calls=%fused_computation.302 | loop fusion | bytes 7667712 | tf_op jit(solution)/shard_map/slice | solution.py:63
  319.6 29.8 %fusion.6 = (bf16[832,3072]{1,0:T(8,128)(2,1)S(1)}, f32[832,3072]{1,0:T(8,128)}) fusion(f32[3072]{0:T(1024)S(1)} %pad_maximum_fusion.5, bf16[832,768]{1,0:T(8,128)(2,1)S(1)} %fusion.51, bf16[768,768]{1,0:T(8,128)(2,1)} %collective-permute-done.11, bf16[768,768]{1,0:T(8,128)(2,1)} %collective-permute-done.10, bf16[768,768]{1,0:T(8,128)(2,1)} %collective-permute-done.9, ...), kind=kOutput, calls=%fused_computation.9 | convolution fusion | flops 4113432576 | bytes 21344256 | tf_op jit(solution)/shard_map/dot_general | solution.py:50
  361.9 23.3 %fusion.7 = f32[832,3072]{1,0:T(8,128)} fusion(f32[832,3072]{1,0:T(8,128)} %get-tuple-element.26), kind=kLoop, calls=%fused_computation.10 | loop fusion | flops 158466048 | bytes 20447232 | tf_op jit(solution)/shard_map/jvp()/erfc | solution.py:38
  385.1 16.8 %add_convert_fusion.9.clone.5 = bf16[832,3072]{1,0:T(8,128)(2,1)} fusion(f32[832,3072]{1,0:T(8,128)} %fusion.7, f32[832,3072]{1,0:T(8,128)} %get-tuple-element.26, bf16[832,768]{1,0:T(8,128)(2,1)} %bitcast.152, f32[832,768]{1,0:T(8,128)S(1)} %get-tuple-element.25, f32[832]{0:T(1024)S(1)} %broadcast_multiply_fusion.7, ...), kind=kOutput, calls=%fused_computation.18.clone.clone.clone.clone.clone.clone.2 | convolution fusion | flops 3986276352 | bytes 34127872 | tf_op jit(solution)/shard_map/nf,df->nd/dot_general | solution.py:54
  427.1 19.3 %reshape.272 = bf16[4,208,12,3,64]{4,3,2,1,0:T(4,128)(2,1)} reshape(bf16[832,2304]{1,0:T(8,128)(2,1)} %add_convert_fusion.2) | data formatting | bytes 7667712 | tf_op jit(solution)/shard_map/reshape | solution.py:62
  446.5 22.3 %fusion.173 = (bf16[4,208,12,1,64]{4,3,2,1,0:T(2,128)(2,1)}, bf16[4,208,12,1,64]{4,3,2,1,0:T(2,128)(2,1)}, bf16[4,208,12,1,64]{4,3,2,1,0:T(2,128)(2,1)}) fusion(bf16[4,208,12,3,64]{4,3,2,1,0:T(4,128)(2,1)} %reshape.272), kind=kLoop, calls=%fused_computation.301 | loop fusion | bytes 7667712 | tf_op jit(solution)/shard_map/slice | solution.py:63
  490.3 11.2 %copy.239 = bf16[4,208,12,1,64]{1,4,2,0,3:T(8,128)(2,1)} copy(bf16[4,208,12,1,64]{4,3,2,1,0:T(2,128)(2,1)} %get-tuple-element.128) | data formatting | bytes 2555904
  516.3 11.6 %multiply_convert_fusion.1 = bf16[4,12,208,208]{2,3,1,0:T(8,128)(2,1)} fusion(f32[4,12,208,208]{2,3,1,0:T(8,128)} %copy-done.2, f32[4,12,208,208]{2,3,1,0:T(8,128)} %get-tuple-element.171, f32[4,12,208]{2,1,0:T(8,128)S(1)} %get-tuple-element.170), kind=kLoop, calls=%fused_computation.15 | loop fusion | flops 6230016 | bytes 20806656 | tf_op jit(solution)/shard_map/convert_element_type | solution.py:118
  562.7 31.2 %collective-permute-done.16 = bf16[832,768]{1,0:T(8,128)(2,1)} collective-permute-done((bf16[832,768]{1,0:T(8,128)(2,1)}, bf16[832,768]{1,0:T(8,128)(2,1)}, u32[]{:S(2)}, u32[]{:S(2)}) %collective-permute-start.16) | collective-permute-done | bytes 1277984 | tf_op jit(solution)/shard_map/ppermute | solution.py:217
  601.2 16.5 %convert_reduce_fusion = (f32[3072]{0:T(1024)}, bf16[832,3072]{1,0:T(8,128)(2,1)}) fusion(f32[832,3072]{1,0:T(8,128)} %fusion.7, f32[832,3072]{1,0:T(8,128)} %get-tuple-element.26, bf16[768,768]{1,0:T(8,128)(2,1)} %copy-done.51, bf16[768,768]{1,0:T(8,128)(2,1)} %collective-permute-done.13, bf16[768,768]{1,0:T(8,128)(2,1)} %copy-done.49, ...), kind=kOutput, calls=%fused_computation.11 | convolution fusion | flops 3986273280 | bytes 32845824 | tf_op jit(solution)/shard_map/nf,df->nd/dot_general | solution.py:54
  656.8 11.7 %multiply_convert_fusion = bf16[4,12,208,208]{2,3,1,0:T(8,128)(2,1)} fusion(f32[4,12,208,208]{2,3,1,0:T(8,128)} %copy-done.2, f32[4,12,208,208]{2,3,1,0:T(8,128)} %get-tuple-element.176, f32[4,12,208]{2,1,0:T(8,128)S(1)} %get-tuple-element.175), kind=kLoop, calls=%fused_computation.12 | loop fusion | flops 6230016 | bytes 20806656 | tf_op jit(solution)/shard_map/convert_element_type | solution.py:118
  723.2 22.2 %collective-permute-done.31 = bf16[768,768]{1,0:T(8,128)(2,1)S(1)} collective-permute-done((bf16[768,768]{1,0:T(8,128)(2,1)S(1)}, bf16[768,768]{1,0:T(8,128)(2,1)S(1)}, u32[]{:S(2)}, u32[]{:S(2)}) %collective-permute-start.31) | collective-permute-done | bytes 1179680 | tf_op jit(solution)/shard_map/ppermute | solution.py:144
  750.7 13.7 %collective-permute-done.19 = bf16[768,576]{0,1:T(8,128)(2,1)S(1)} collective-permute-done((bf16[768,576]{0,1:T(8,128)(2,1)S(1)}, bf16[768,576]{0,1:T(8,128)(2,1)S(1)}, u32[]{:S(2)}, u32[]{:S(2)}) %collective-permute-start.19) | collective-permute-done | bytes 884768 | tf_op jit(solution)/shard_map/ppermute | solution.py:144
  770.6 19.1 %collective-permute-done.37 = bf16[768,768]{1,0:T(8,128)(2,1)} collective-permute-done((bf16[768,768]{1,0:T(8,128)(2,1)S(1)}, bf16[768,768]{1,0:T(8,128)(2,1)}, u32[]{:S(2)}, u32[]{:S(2)}) %collective-permute-start.37) | collective-permute-done | bytes 1179680 | tf_op jit(solution)/shard_map/ppermute | solution.py:144
  808.1 18.2 %collective-permute-done.26 = bf16[192,768]{1,0:T(8,128)(2,1)S(1)} collective-permute-done((bf16[192,768]{1,0:T(8,128)(2,1)S(1)}, bf16[192,768]{1,0:T(8,128)(2,1)S(1)}, u32[]{:S(2)}, u32[]{:S(2)}) %collective-permute-start.26) | collective-permute-done | bytes 294944 | tf_op jit(solution)/shard_map/ppermute | solution.py:156
  850.4 77.7 %psum.7 = f32[9984]{0:T(1024)} all-reduce(f32[9984]{0:T(1024)} %concatenate.38), channel_id=1, replica_groups=mesh['section'=2,'dp'=4,'tensor'=4] {'dp','tensor'}, use_global_device_ids=true, to_apply=%region_34.35 | all-reduce | flops 9984 | bytes 79872 | tf_op jit(solution)/shard_map/psum | solution.py:243
  947.1 14.5 %collective-permute-done.40 = bf16[768,768]{1,0:T(8,128)(2,1)S(1)} collective-permute-done((bf16[768,768]{1,0:T(8,128)(2,1)S(1)}, bf16[768,768]{1,0:T(8,128)(2,1)S(1)}, u32[]{:S(2)}, u32[]{:S(2)}) %collective-permute-start.40) | collective-permute-done | bytes 1179680 | tf_op jit(solution)/shard_map/ppermute | solution.py:162
  (373 shorter events, 426.0 us)
Async XLA Ops:
  5.6 49.8 %collective-permute-start = (bf16[768,576]{0,1:T(8,128)(2,1)}, bf16[768,576]{0,1:T(8,128)(2,1)S(1)}, u32[]{:S(2)}, u32[]{:S(2)}) collective-permute-start(bf16[768,576]{0,1:T(8,128)(2,1)} %bitcast.180), channel_id=1, source_target_pairs={{0,1},{1,0},{2,3},{3,2},{4,5},{5,4},{6,7},{7,6},{8,9},{9,8},{10,11... | collective-permute-start | bytes 2654216 | tf_op jit(solution)/shard_map/ppermute | solution.py:144
  6.0 51.2 %collective-permute-start.10 = (bf16[768,768]{1,0:T(8,128)(2,1)}, bf16[768,768]{1,0:T(8,128)(2,1)}, u32[]{:S(2)}, u32[]{:S(2)}) collective-permute-start(bf16[768,768]{1,0:T(8,128)(2,1)} %bitcast.173), channel_id=1, source_target_pairs={{0,2},{1,3},{2,0},{3,1},{4,6},{5,7},{6,4},{7,5},{8,10},{9,11},{10,... | collective-permute-start | bytes 3538952 | tf_op jit(solution)/shard_map/ppermute | solution.py:144
  24.4 33.0 %collective-permute-start.2 = (bf16[768,576]{0,1:T(8,128)(2,1)S(1)}, bf16[768,576]{0,1:T(8,128)(2,1)S(1)}, u32[]{:S(2)}, u32[]{:S(2)}) collective-permute-start(bf16[768,576]{0,1:T(8,128)(2,1)S(1)} %collective-permute-done.1), channel_id=1, source_target_pairs={{0,1},{1,0},{2,3},{3,2},{4,5},{5,4},{6,7},{7,6},{8,9},{9,8},{10,11... | collective-permute-start | bytes 2654216 | tf_op jit(solution)/shard_map/ppermute | solution.py:144
  33.1 112.3 %collective-permute-start.6 = (bf16[192,768]{1,0:T(8,128)(2,1)}, bf16[192,768]{1,0:T(8,128)(2,1)}, u32[]{:S(2)}, u32[]{:S(2)}) collective-permute-start(bf16[192,768]{1,0:T(8,128)(2,1)} %bitcast.186), channel_id=1, source_target_pairs={{0,1},{1,0},{2,3},{3,2},{4,5},{5,4},{6,7},{7,6},{8,9},{9,8},{10,11... | collective-permute-start | bytes 884744 | tf_op jit(solution)/shard_map/ppermute | solution.py:144
  55.4 94.1 %collective-permute-start.9 = (bf16[768,768]{1,0:T(8,128)(2,1)}, bf16[768,768]{1,0:T(8,128)(2,1)}, u32[]{:S(2)}, u32[]{:S(2)}) collective-permute-start(bf16[768,768]{1,0:T(8,128)(2,1)} %bitcast.174), channel_id=1, source_target_pairs={{0,1},{1,0},{2,3},{3,2},{4,5},{5,4},{6,7},{7,6},{8,9},{9,8},{10,11... | collective-permute-start | bytes 3538952 | tf_op jit(solution)/shard_map/ppermute | solution.py:144
  55.4 90.4 %collective-permute-start.13 = (bf16[768,768]{1,0:T(8,128)(2,1)}, bf16[768,768]{1,0:T(8,128)(2,1)}, u32[]{:S(2)}, u32[]{:S(2)}) collective-permute-start(bf16[768,768]{1,0:T(8,128)(2,1)} %bitcast.167), channel_id=1, source_target_pairs={{0,2},{1,3},{2,0},{3,1},{4,6},{5,7},{6,4},{7,5},{8,10},{9,11},{10,... | collective-permute-start | bytes 3538952 | tf_op jit(solution)/shard_map/ppermute | solution.py:144
  57.2 88.8 %collective-permute-start.8 = (bf16[192,768]{1,0:T(8,128)(2,1)}, bf16[192,768]{1,0:T(8,128)(2,1)}, u32[]{:S(2)}, u32[]{:S(2)}) collective-permute-start(bf16[192,768]{1,0:T(8,128)(2,1)} %collective-permute-done.7), channel_id=1, source_target_pairs={{0,1},{1,0},{2,3},{3,2},{4,5},{5,4},{6,7},{7,6},{8,9},{9,8},{10,11... | collective-permute-start | bytes 884744 | tf_op jit(solution)/shard_map/ppermute | solution.py:144
  57.4 92.2 %collective-permute-start.11 = (bf16[768,768]{1,0:T(8,128)(2,1)}, bf16[768,768]{1,0:T(8,128)(2,1)}, u32[]{:S(2)}, u32[]{:S(2)}) collective-permute-start(bf16[768,768]{1,0:T(8,128)(2,1)} %collective-permute-done.10), channel_id=1, source_target_pairs={{0,1},{1,0},{2,3},{3,2},{4,5},{5,4},{6,7},{7,6},{8,9},{9,8},{10,11... | collective-permute-start | bytes 3538952 | tf_op jit(solution)/shard_map/ppermute | solution.py:144
  145.4 33.3 %collective-permute-start.12 = (bf16[768,768]{1,0:T(8,128)(2,1)}, bf16[768,768]{1,0:T(8,128)(2,1)S(1)}, u32[]{:S(2)}, u32[]{:S(2)}) collective-permute-start(bf16[768,768]{1,0:T(8,128)(2,1)} %bitcast.168), channel_id=1, source_target_pairs={{0,1},{1,0},{2,3},{3,2},{4,5},{5,4},{6,7},{7,6},{8,9},{9,8},{10,11... | collective-permute-start | bytes 3538952 | tf_op jit(solution)/shard_map/ppermute | solution.py:144
  560.9 33.0 %collective-permute-start.16 = (bf16[832,768]{1,0:T(8,128)(2,1)}, bf16[832,768]{1,0:T(8,128)(2,1)}, u32[]{:S(2)}, u32[]{:S(2)}) collective-permute-start(bf16[832,768]{1,0:T(8,128)(2,1)} %add_convert_fusion.5), channel_id=1, source_target_pairs={{16,0},{17,1},{18,2},{19,3},{20,4},{21,5},{22,6},{23,7},{24,8},{25... | collective-permute-start | bytes 3833864 | tf_op jit(solution)/shard_map/ppermute | solution.py:217
  699.1 47.0 %collective-permute-start.17 = (bf16[768,576]{0,1:T(8,128)(2,1)S(1)}, bf16[768,576]{0,1:T(8,128)(2,1)S(1)}, u32[]{:S(2)}, u32[]{:S(2)}) collective-permute-start(bf16[768,576]{0,1:T(8,128)(2,1)S(1)} %get-tuple-element.141), channel_id=1, source_target_pairs={{0,1},{1,0},{2,3},{3,2},{4,5},{5,4},{6,7},{7,6},{8,9},{9,8},{10,11... | collective-permute-start | bytes 2654216 | tf_op jit(solution)/shard_map/ppermute | solution.py:144
  720.9 43.4 %collective-permute-start.19 = (bf16[768,576]{0,1:T(8,128)(2,1)S(1)}, bf16[768,576]{0,1:T(8,128)(2,1)S(1)}, u32[]{:S(2)}, u32[]{:S(2)}) collective-permute-start(bf16[768,576]{0,1:T(8,128)(2,1)S(1)} %slice_add_fusion.4), channel_id=1, source_target_pairs={{0,2},{1,3},{2,0},{3,1},{4,6},{5,7},{6,4},{7,5},{8,10},{9,11},{10,... | collective-permute-start | bytes 2654216 | tf_op jit(solution)/shard_map/ppermute | solution.py:144
  722.4 46.5 %collective-permute-start.24 = (bf16[192,768]{1,0:T(8,128)(2,1)}, bf16[192,768]{1,0:T(8,128)(2,1)}, u32[]{:S(2)}, u32[]{:S(2)}) collective-permute-start(bf16[192,768]{1,0:T(8,128)(2,1)} %get-tuple-element.144), channel_id=1, source_target_pairs={{0,1},{1,0},{2,3},{3,2},{4,5},{5,4},{6,7},{7,6},{8,9},{9,8},{10,11... | collective-permute-start | bytes 884744 | tf_op jit(solution)/shard_map/ppermute | solution.py:144
  722.6 47.4 %collective-permute-start.35 = (bf16[768,768]{1,0:T(8,128)(2,1)}, bf16[768,768]{1,0:T(8,128)(2,1)}, u32[]{:S(2)}, u32[]{:S(2)}) collective-permute-start(bf16[768,768]{1,0:T(8,128)(2,1)} %get-tuple-element.137), channel_id=1, source_target_pairs={{0,1},{1,0},{2,3},{3,2},{4,5},{5,4},{6,7},{7,6},{8,9},{9,8},{10,11... | collective-permute-start | bytes 3538952 | tf_op jit(solution)/shard_map/ppermute | solution.py:144
  745.4 44.3 %collective-permute-start.37 = (bf16[768,768]{1,0:T(8,128)(2,1)S(1)}, bf16[768,768]{1,0:T(8,128)(2,1)}, u32[]{:S(2)}, u32[]{:S(2)}) collective-permute-start(bf16[768,768]{1,0:T(8,128)(2,1)S(1)} %slice_add_fusion), channel_id=1, source_target_pairs={{0,2},{1,3},{2,0},{3,1},{4,6},{5,7},{6,4},{7,5},{8,10},{9,11},{10,... | collective-permute-start | bytes 3538952 | tf_op jit(solution)/shard_map/ppermute | solution.py:144
  746.0 54.1 %collective-permute-start.32 = (bf16[768,768]{1,0:T(8,128)(2,1)S(1)}, bf16[768,768]{1,0:T(8,128)(2,1)}, u32[]{:S(2)}, u32[]{:S(2)}) collective-permute-start(bf16[768,768]{1,0:T(8,128)(2,1)S(1)} %fusion.121), channel_id=1, source_target_pairs={{0,4},{12,8},{1,5},{13,9},{2,6},{14,10},{3,7},{15,11},{16,20},{28,... | collective-permute-start | bytes 3538952 | tf_op jit(solution)/shard_map/ppermute | solution.py:156
  768.9 34.5 %collective-permute-start.23 = (bf16[192,768]{1,0:T(8,128)(2,1)}, bf16[192,768]{1,0:T(8,128)(2,1)S(1)}, u32[]{:S(2)}, u32[]{:S(2)}) collective-permute-start(bf16[192,768]{1,0:T(8,128)(2,1)} %get-tuple-element.143), channel_id=1, source_target_pairs={{0,1},{1,0},{2,3},{3,2},{4,5},{5,4},{6,7},{7,6},{8,9},{9,8},{10,11... | collective-permute-start | bytes 884744 | tf_op jit(solution)/shard_map/ppermute | solution.py:144
  770.0 33.4 %collective-permute-start.25 = (bf16[192,768]{1,0:T(8,128)(2,1)S(1)}, bf16[192,768]{1,0:T(8,128)(2,1)S(1)}, u32[]{:S(2)}, u32[]{:S(2)}) collective-permute-start(bf16[192,768]{1,0:T(8,128)(2,1)S(1)} %slice_add_fusion.6), channel_id=1, source_target_pairs={{0,2},{1,3},{2,0},{3,1},{4,6},{5,7},{6,4},{7,5},{8,10},{9,11},{10,... | collective-permute-start | bytes 884744 | tf_op jit(solution)/shard_map/ppermute | solution.py:144
  791.9 41.1 %collective-permute-start.38 = (bf16[768,768]{1,0:T(8,128)(2,1)S(1)}, bf16[768,768]{1,0:T(8,128)(2,1)}, u32[]{:S(2)}, u32[]{:S(2)}) collective-permute-start(bf16[768,768]{1,0:T(8,128)(2,1)S(1)} %fusion.120), channel_id=1, source_target_pairs={{0,4},{12,8},{1,5},{13,9},{2,6},{14,10},{3,7},{15,11},{16,20},{28,... | collective-permute-start | bytes 3538952 | tf_op jit(solution)/shard_map/ppermute | solution.py:156
  801.7 34.7 %collective-permute-start.33 = (bf16[768,768]{1,0:T(8,128)(2,1)S(1)}, bf16[768,768]{1,0:T(8,128)(2,1)}, u32[]{:S(2)}, u32[]{:S(2)}) collective-permute-start(bf16[768,768]{1,0:T(8,128)(2,1)S(1)} %add_select_fusion.1), channel_id=1, source_target_pairs={{4,8},{8,4},{5,9},{9,5},{6,10},{10,6},{7,11},{11,7},{20,24},{24,20... | collective-permute-start | bytes 3538952 | tf_op jit(solution)/shard_map/ppermute | solution.py:159
  827.1 101.9 %collective-permute-start.27 = (bf16[192,768]{1,0:T(8,128)(2,1)}, bf16[192,768]{1,0:T(8,128)(2,1)}, u32[]{:S(2)}, u32[]{:S(2)}) collective-permute-start(bf16[192,768]{1,0:T(8,128)(2,1)} %add_select_fusion.3), channel_id=1, source_target_pairs={{4,8},{8,4},{5,9},{9,5},{6,10},{10,6},{7,11},{11,7},{20,24},{24,20... | collective-permute-start | bytes 884744 | tf_op jit(solution)/shard_map/ppermute | solution.py:159
  831.2 111.7 %collective-permute-start.22 = (bf16[768,576]{0,1:T(8,128)(2,1)}, bf16[768,576]{0,1:T(8,128)(2,1)}, u32[]{:S(2)}, u32[]{:S(2)}) collective-permute-start(bf16[768,576]{0,1:T(8,128)(2,1)} %add.326), channel_id=1, source_target_pairs={{4,0},{8,12},{5,1},{9,13},{6,2},{10,14},{7,3},{11,15},{20,16},{24,... | collective-permute-start | bytes 2654216 | tf_op jit(solution)/shard_map/ppermute | solution.py:162
  834.7 96.8 %collective-permute-start.39 = (bf16[768,768]{1,0:T(8,128)(2,1)S(1)}, bf16[768,768]{1,0:T(8,128)(2,1)}, u32[]{:S(2)}, u32[]{:S(2)}) collective-permute-start(bf16[768,768]{1,0:T(8,128)(2,1)S(1)} %add_select_fusion), channel_id=1, source_target_pairs={{4,8},{8,4},{5,9},{9,5},{6,10},{10,6},{7,11},{11,7},{20,24},{24,20... | collective-permute-start | bytes 3538952 | tf_op jit(solution)/shard_map/ppermute | solution.py:159
  837.9 107.6 %collective-permute-start.34 = (bf16[768,768]{1,0:T(8,128)(2,1)S(1)}, bf16[768,768]{1,0:T(8,128)(2,1)S(1)}, u32[]{:S(2)}, u32[]{:S(2)}) collective-permute-start(bf16[768,768]{1,0:T(8,128)(2,1)S(1)} %add.340), channel_id=1, source_target_pairs={{4,0},{8,12},{5,1},{9,13},{6,2},{10,14},{7,3},{11,15},{20,16},{24,... | collective-permute-start | bytes 3538952 | tf_op jit(solution)/shard_map/ppermute | solution.py:162
  (83 other events, 1506.3 us)

commit v2 on v1

v2 whole, which is shorter than its diff:
```python
import functools

import jax
import jax.numpy as jnp
from jax import lax
from jax.experimental import pallas as pl
from jax.experimental.pallas import tpu as pltpu
from jax.sharding import PartitionSpec as P

HD = 64
SEQLEN = 208
norm_eps = 1e-06
masked_value = -1000000000.0
BF = jnp.bfloat16
F32 = jnp.float32
NT = (((1,), (1,)), ((), ()))
TN = (((0,), (0,)), ((), ()))
MIB = 1 << 20
PARTS = 3
EXTRA = 32


def dot(a, b):
    return jnp.dot(a, b, preferred_element_type=F32)


def dot_nt(a, b):
    return lax.dot_general(a, b, NT, preferred_element_type=F32)


def dot_tn(a, b):
    return lax.dot_general(a, b, TN, preferred_element_type=F32)


def normed(residual):
    center = residual - jnp.mean(residual, axis=-1, keepdims=True)
    rstd = lax.rsqrt(jnp.mean(center * center, axis=-1, keepdims=True) + norm_eps)
    return center * rstd, rstd


def norm_back(grad, n, rstd, gain):
    g = grad * gain
    return rstd * (g - jnp.mean(g, axis=-1, keepdims=True) - n * jnp.mean(g * n, axis=-1, keepdims=True))


def gelu_parts(u, slope):
    size = jnp.abs(u)
    t = pl.reciprocal(1.0 + 0.23164189 * size, approx=True)
    poly = t * (0.127414796 + t * (-0.142248368 + t * (0.7107068705 + t * (-0.7265760135 + t * 0.5307027145))))
    bell = jnp.exp2(u * (u * -0.7213475204444817))
    tail = poly * bell
    act = jnp.maximum(u, 0.0) - size * tail
    if not slope:
        return act, None
    return act, jnp.where(u < 0, tail, 1.0 - tail) + u * (bell * 0.3989422804014327)


def fixed(a):
    return pl.BlockSpec(a.shape, lambda q: (0,) * len(a.shape))


def quarter(a):
    return pl.BlockSpec((1,) + tuple(a.shape[1:]), lambda q: (q,) + (0,) * (len(a.shape) - 1))


def call(kernel, name, count, ins, outs, scratch, flops, limit=24):
    spec = lambda pair: (quarter if pair[1] else fixed)(pair[0])
    size = sum(a.size * a.dtype.itemsize for a, _ in (*ins, *outs))
    return pl.pallas_call(
        kernel,
        grid=(count,),
        in_specs=[spec(p) for p in ins],
        out_specs=[spec(p) for p in outs],
        out_shape=[a for a, _ in outs],
        scratch_shapes=scratch,
        compiler_params=pltpu.CompilerParams(vmem_limit_bytes=limit * MIB),
        cost_estimate=pl.CostEstimate(flops=2 * flops, bytes_accessed=size, transcendentals=0),
        name=name,
    )(*[a for a, _ in ins])


def shape(*dims, t=BF):
    return jax.ShapeDtypeStruct(dims, t)


def units_of(p, seqs):
    for s in range(seqs):
        for h in range(p.shape[1] // (3 * HD)):
            yield s, h


def head_rows(p, s, h, part):
    at = (3 * h + part) * HD
    return p[s * SEQLEN:(s + 1) * SEQLEN, at:at + HD]


def attn_fwd_kernel(save, first, seqs, x_ref, ok_ref, base_ref, ab_ref, wt_ref, pw_ref, r1_ref, *saved):
    q = pl.program_id(0)
    x = x_ref[...]

    @pl.when(q == 0)
    def _():
        r1_ref[...] = x.astype(F32) + base_ref[...] if first else base_ref[...]

    cols = ab_ref.shape[2]
    p = (dot_nt(x, wt_ref[0, :cols]) + ab_ref[0]).astype(BF)
    blocks = list(units_of(p, seqs))
    oks = [ok_ref[s] > 0 for s in range(seqs)]
    scores = [dot_nt(head_rows(p, s, h, 1), head_rows(p, s, h, 0) * 0.125) for s, h in blocks]
    probs = []
    for (s, h), st in zip(blocks, scores):
        st = jnp.where(oks[s], st, masked_value)
        e = jnp.exp(st - jnp.max(st, axis=0, keepdims=True))
        probs.append((e * (1.0 / jnp.sum(e, axis=0, keepdims=True))).astype(BF))
    cts = [dot_tn(head_rows(p, s, h, 2), a).astype(BF) for (s, h), a in zip(blocks, probs)]
    per = len(blocks) // seqs
    c = jnp.concatenate([jnp.concatenate(cts[s * per:(s + 1) * per], axis=0).T for s in range(seqs)], axis=0)
    r1_ref[...] += dot(c, pw_ref[0])
    if save:
        saved[0][0] = p
        saved[1][0] = c
        for (s, h), a in zip(blocks, probs):
            saved[2][0, s, h] = a


def attn_fwd(x, ok, base, ab, wt, pw, save, first):
    rows, width = x.shape
    count, _, cols = ab.shape
    seqs, heads = rows // SEQLEN, cols // (3 * HD)
    outs = [(shape(rows, width, t=F32), False)]
    if save:
        outs += [(shape(count, rows, cols), True), (shape(count, rows, heads * HD), True),
                 (shape(count, seqs, heads, SEQLEN, SEQLEN), True)]
    flops = count * 2 * rows * (width * cols + heads * HD * (2 * SEQLEN + width))
    ins = [(x, False), (ok, False), (base, False), (ab, True), (wt, True), (pw, True)]
    return call(functools.partial(attn_fwd_kernel, save, first, seqs), "attn_fwd", count, ins, outs, [], flops)


def ffn_fwd_kernel(save, first, last, x_ref, acc_in, vec_ref, ub_ref, up_ref, down_ref, *outs):
    q = pl.program_id(0)
    outs, (hb_ref, acc_ref) = outs[:-2], outs[-2:]

    @pl.when(q == 0)
    def _():
        if first:
            h = normed(x_ref[...])[0] * vec_ref[0:1] + vec_ref[1:2]
            hb_ref[...] = h.astype(BF)
            acc_ref[...] = h + vec_ref[2:3]
        else:
            hb_ref[...] = x_ref[...]
            acc_ref[...] = acc_in[...]

    hb = hb_ref[...]
    units = up_ref.shape[2]
    step = units // PARTS
    us = [dot(hb, up_ref[0, :, j * step:(j + 1) * step]) for j in range(PARTS)]
    es, slopes = [], []
    for j, u in enumerate(us):
        act, slope = gelu_parts(u + ub_ref[0, :, j * step:(j + 1) * step], save)
        es.append(act.astype(BF))
        if save:
            outs[2][0, :, j * step:(j + 1) * step] = slope.astype(BF)
    e = jnp.concatenate(es, axis=1)
    if save:
        outs[1][0] = e
    acc_ref[...] += dot(e, down_ref[0])

    @pl.when(q == pl.num_programs(0) - 1)
    def _():
        acc = acc_ref[...]
        if last:
            outs[0][...] = (normed(acc)[0] * vec_ref[3:4] + vec_ref[4:5]).astype(BF)
            if save:
                outs[3][...] = acc
                outs[4][...] = hb
        else:
            outs[0][...] = acc
            outs[1][...] = hb


def ffn_fwd(x, acc, vec, ub, up, down, save, first, last):
    rows, width = x.shape
    count, _, units = ub.shape
    outs = [(shape(rows, width, t=BF if last else F32), False)]
    if save:
        outs += [(shape(count, rows, units), True)] * 2 + [(shape(rows, width, t=F32), False), (shape(rows, width), False)]
    if not last:
        outs += [(shape(rows, width), False)]
    ins = [(x, False), (acc, False), (vec, False), (ub, True), (up, True), (down, True)]
    scratch = [pltpu.VMEM((rows, width), BF), pltpu.VMEM((rows, width), F32)]
    return call(functools.partial(ffn_fwd_kernel, save, first, last), "ffn_fwd", count, ins, outs, scratch,
                count * 4 * rows * width * units)


def ffn_bwd_kernel(full, dy_ref, r2_ref, r1_ref, vec_ref, slope_ref, up_ref, down_ref, *outs):
    q = pl.program_id(0)
    outs, (df_ref, dh_ref, sum_ref) = outs[:-3], outs[-3:]
    total = lambda v: jnp.sum(v, axis=0, keepdims=True)

    @pl.when(q == 0)
    def _():
        dy = dy_ref[...].astype(F32)
        n2, s2 = normed(r2_ref[...])
        dr2 = norm_back(dy, n2, s2, vec_ref[3:4])
        df_ref[...] = dr2.astype(BF)
        dh_ref[...] = dr2
        if full:
            sum_ref[0:1] = total(dr2)
            sum_ref[1:2] = total(dy * n2)
            sum_ref[2:3] = total(dy)

    df = df_ref[...]
    units = up_ref.shape[2]
    step = units // PARTS
    des = [dot_nt(df, down_ref[0, j * step:(j + 1) * step]) for j in range(PARTS)]
    dus = [(de * slope_ref[0, :, j * step:(j + 1) * step].astype(F32)).astype(BF) for j, de in enumerate(des)]
    du = jnp.concatenate(dus, axis=1)
    dh_ref[...] += dot_nt(du, up_ref[0])
    if full:
        outs[3][0] = du
        outs[4][0] = total(du.astype(F32))

    @pl.when(q == pl.num_programs(0) - 1)
    def _():
        dh = dh_ref[...]
        n1, s1 = normed(r1_ref[...])
        dr1 = norm_back(dh, n1, s1, vec_ref[0:1])
        outs[0][...] = dr1
        outs[1][...] = dr1.astype(BF)
        if full:
            outs[2][...] = df
            outs[5][0:1] = total(dr1)
            outs[5][1:2] = total(dh * n1)
            outs[5][2:3] = total(dh)
            outs[5][3:6] = sum_ref[0:3]
            outs[5][6:8] = jnp.zeros_like(outs[5][6:8])


def ffn_bwd(dy, r2, r1, vec, slope, up, down, full):
    rows, width = r1.shape
    count, _, units = slope.shape
    outs = [(shape(rows, width, t=F32), False), (shape(rows, width), False)]
    if full:
        outs += [(shape(rows, width), False), (shape(count, rows, units), True),
                 (shape(count, 1, units, t=F32), True), (shape(8, width, t=F32), False)]
    ins = [(dy, False), (r2, False), (r1, False), (vec, False), (slope, True), (up, True), (down, True)]
    scratch = [pltpu.VMEM((rows, width), BF), pltpu.VMEM((rows, width), F32), pltpu.VMEM((8, width), F32)]
    return call(functools.partial(ffn_bwd_kernel, full), "ffn_bwd", count, ins, outs, scratch,
                count * 4 * rows * width * units)


def attn_bwd_kernel(full, seqs, dg_ref, dr1_ref, p_ref, a_ref, wt_ref, pw_ref, *outs):
    q = pl.program_id(0)
    outs, dx_ref = outs[:-1], outs[-1]

    @pl.when(q == 0)
    def _():
        dx_ref[...] = dr1_ref[...]

    dc = dot_nt(dg_ref[...], pw_ref[0]).astype(BF)
    p = p_ref[0]
    blocks = list(units_of(p, seqs))
    dcs = [dc[s * SEQLEN:(s + 1) * SEQLEN, h * HD:(h + 1) * HD] for s, h in blocks]
    das = [dot_nt(head_rows(p, s, h, 2), d) for (s, h), d in zip(blocks, dcs)]
    dss = []
    for (s, h), da in zip(blocks, das):
        a = a_ref[0, s, h].astype(F32)
        dss.append((a * (da - jnp.sum(da * a, axis=0, keepdims=True))).astype(BF))
    pieces = []
    for (s, h), d, ds in zip(blocks, dcs, dss):
        dq = dot_tn(ds, head_rows(p, s, h, 1)) * 0.125
        dk = dot(ds, head_rows(p, s, h, 0)) * 0.125
        dv = dot(a_ref[0, s, h], d)
        pieces += [dq.astype(BF), dk.astype(BF), dv.astype(BF)]
    per = len(pieces) // seqs
    dp = jnp.concatenate([jnp.concatenate(pieces[s * per:(s + 1) * per], axis=1) for s in range(seqs)], axis=0)
    dx_ref[...] += dot(dp, wt_ref[0, :dp.shape[1]])
    if full:
        outs[1][0] = dp
        outs[2][0] = jnp.sum(dp.astype(F32), axis=0, keepdims=True)

    @pl.when(q == pl.num_programs(0) - 1)
    def _():
        outs[0][...] = dx_ref[...].astype(outs[0].dtype)


def attn_bwd(dg, dr1, p, a, wt, pw, full):
    rows, width = dg.shape
    count, _, cols = p.shape
    seqs, heads = rows // SEQLEN, cols // (3 * HD)
    outs = [(shape(rows, width, t=F32 if full else BF), False)]
    if full:
        outs += [(shape(count, rows, cols), True), (shape(count, 1, cols, t=F32), True)]
    ins = [(dg, False), (dr1, False), (p, True), (a, True), (wt, True), (pw, True)]
    flops = count * 2 * rows * (width * cols + heads * HD * (4 * SEQLEN + width))
    return call(functools.partial(attn_bwd_kernel, full, seqs), "attn_bwd", count, ins, outs,
                [pltpu.VMEM((rows, width), F32)], flops)


def wgrad_kernel(pairs, added, *refs):
    total = None
    for g in range(pairs):
        a, b = refs[2 * g], refs[2 * g + 1]
        a = a[0] if len(a.shape) == 3 else a[...]
        b = b[0] if len(b.shape) == 3 else b[...]
        part = dot_tn(a, b)
        total = part if total is None else total + part
    if added:
        total = total + refs[2 * pairs][0].astype(F32)
    refs[-1][0] = total.astype(BF)


def wgrad(pairs, odd, more=None):
    def spec(a):
        if a.ndim == 2:
            return pl.BlockSpec(a.shape, lambda i: (0, 0))
        return pl.BlockSpec((1,) + a.shape[1:], lambda i: (2 * i + odd, 0, 0))

    flat = [a for pair in pairs for a in pair]
    dims = (2, pairs[0][0].shape[-1], pairs[0][1].shape[-1])
    block = pl.BlockSpec((1,) + dims[1:], lambda i: (i, 0, 0))
    extra = [] if more is None else [more]
    rows = sum(a.shape[-2] for a, _ in pairs)
    return pl.pallas_call(
        functools.partial(wgrad_kernel, len(pairs), more is not None),
        grid=(2,),
        in_specs=[spec(a) for a in flat] + [block] * len(extra),
        out_specs=block,
        out_shape=shape(*dims),
        compiler_params=pltpu.CompilerParams(vmem_limit_bytes=24 * MIB),
        cost_estimate=pl.CostEstimate(flops=8 * rows * dims[1] * dims[2], bytes_accessed=8 * MIB, transcendentals=0),
        name="wgrad",
    )(*flat, *extra)


def swapped(value, axis, bit):
    count = lax.axis_size(axis)
    return lax.ppermute(value, axis, [(i, i ^ bit) for i in range(count)])


def near(value):
    return swapped(value, "tensor", 1)


def over_y(value):
    return swapped(value, "tensor", 2)


def chain_steps(count):
    half = count // 2
    inward = [[(s, s + 1), (count - 1 - s, count - 2 - s)] for s in range(half - 1)]
    outward = [[(s, s - 1), (count - 1 - s, count - s)] for s in range(half - 1, 0, -1)]
    return inward, [(half - 1, half), (half, half - 1)], outward


def chain_sum(value, axis):
    count = lax.axis_size(axis)
    if count == 1:
        return value
    if count % 2:
        return lax.psum(value, axis)
    here = lax.axis_index(axis)
    inward, cross, outward = chain_steps(count)
    for step in inward:
        value = value + lax.ppermute(value, axis, step)
    value = value + lax.ppermute(value, axis, cross)
    for step in outward:
        got = lax.ppermute(value, axis, step)
        takes = (here == step[0][1]) | (here == step[1][1])
        value = jnp.where(takes, got, value)
    return value


def after(value, *others):
    return lax.optimization_barrier((value, *others))[0]


def key_allowed(region_count, region_mask, caption):
    regions = region_mask.shape[-1]
    slot_index = jnp.arange(caption + regions, dtype=jnp.int32) - caption
    caption_ones = jnp.ones(region_mask.shape[:-1] + (caption,), jnp.int32)
    present = jnp.concatenate([caption_ones, region_mask], axis=-1) > 0
    return present & (slot_index < region_count[..., None])


def three_parts(vector):
    high = lax.reduce_precision(vector, 8, 7)
    mid = lax.reduce_precision(vector - high, 8, 7)
    return [high, mid, vector - high - mid]


def body(
    layer_input, cotangent, region_count, region_mask, attn_weight, attn_bias, proj_weight, proj_bias,
    first_gain, first_shift, up_weight, up_bias, down_weight, down_bias, second_gain, second_shift,
):
    section = lax.axis_index("section")
    tensor = lax.axis_index("tensor")
    micro, rows, width = layer_input.shape
    heads = attn_weight.shape[2]
    cols = heads * attn_weight.shape[3]
    units = up_weight.shape[2]
    assert rows == SEQLEN and lax.axis_size("tensor") == 4
    dp_pairs = lax.axis_size("dp") % 2 == 0
    odd = lax.axis_index("dp") % 2 == 1

    pieces = attn_bias[0].reshape(heads, 2, -1)
    own_bias = jnp.stack([pieces[:, 0], jnp.zeros_like(pieces[:, 0]), pieces[:, 1]], axis=1).reshape(-1)
    own_bias = jnp.pad(own_bias, (0, width - cols))
    tail = jnp.stack(three_parts(own_bias) + three_parts(up_bias[0])).astype(BF)
    tail = after(jnp.pad(tail, ((0, EXTRA - 6), (0, 0))))
    attn_own = attn_weight[0].transpose(1, 2, 0).reshape(cols, width)
    attn_own = jnp.concatenate([attn_own, tail], axis=0)
    proj_own = proj_weight[0].reshape(-1, width)
    up_own = up_weight[0]
    down_own = down_weight[0]

    def part(own):
        half = own.shape[0] // 2
        return jnp.where(odd, own[half:], own[:half]) if dp_pairs else own

    def along_dp(mine):
        return swapped(mine, "dp", 1) if dp_pairs else mine

    def both_halves(mine, pair):
        if not dp_pairs:
            return mine
        return jnp.where(odd, jnp.concatenate([pair, mine]), jnp.concatenate([mine, pair]))

    def pair_of(a, b):
        return jnp.stack([a, b])

    ok = lax.dynamic_index_in_dim(key_allowed(region_count, region_mask, rows - region_mask.shape[-1]), tensor, 1, False)
    ok = ok.astype(jnp.int32)[:, :, None]
    vec = jnp.concatenate([first_gain, first_shift, down_bias, second_gain, second_shift], axis=0)
    groups = 2 if micro % 2 == 0 else 1
    per = micro // groups
    size = per * rows
    cut = lambda value: [value.reshape(micro * rows, -1)[g * size:(g + 1) * size] for g in range(groups)]
    oks = [ok[g * per:(g + 1) * per] for g in range(groups)]
    x_own, cots = cut(layer_input), cut(cotangent)

    attn_mine = over_y(part(attn_own))
    attn_near = near(attn_own)
    proj_mine = over_y(after(part(proj_own), attn_near))
    proj_near = near(proj_own)
    up_mine = over_y(after(part(up_own), attn_mine))
    attn_pair = along_dp(attn_mine)
    up_near = near(after(up_own, proj_near))
    down_mine = over_y(after(part(down_own), proj_mine))
    proj_pair = along_dp(proj_mine)
    down_near = near(after(down_own, up_near))
    up_pair = along_dp(up_mine)
    down_pair = along_dp(down_mine)

    def biases(stack):
        three = stack[:, cols:cols + 6].astype(F32)
        return jnp.sum(three[:, :3], axis=1, keepdims=True)[:, :, :cols], jnp.sum(three[:, 3:], axis=1, keepdims=True)

    attn_0 = pair_of(attn_own, attn_near)
    proj_0 = pair_of(proj_own, proj_near)
    up_0 = pair_of(up_own, up_near)
    down_0 = pair_of(down_own, down_near)
    ab_0, ub_0 = biases(attn_0)
    r1s = [attn_fwd(x_own[g], oks[g], proj_bias, ab_0, attn_0, proj_0, False, True)[0] for g in range(groups)]
    attn_far = both_halves(attn_mine, attn_pair)
    attn_1 = pair_of(attn_far, near(attn_far))
    proj_far = both_halves(proj_mine, proj_pair)
    proj_1 = pair_of(proj_far, near(proj_far))
    ab_1, ub_1 = biases(attn_1)
    r1s = [attn_fwd(x_own[g], oks[g], r1s[g], ab_1, attn_1, proj_1, False, False)[0] for g in range(groups)]
    halves = [ffn_fwd(r1s[g], vec, vec, ub_0, up_0, down_0, False, True, False) for g in range(groups)]
    up_far = both_halves(up_mine, up_pair)
    up_1 = pair_of(up_far, near(up_far))
    down_far = both_halves(down_mine, down_pair)
    down_1 = pair_of(down_far, near(down_far))
    firsts, hops = [], []
    for g in range(groups):
        tok = firsts[-1:]
        acc, hb = halves[g]
        firsts.append(ffn_fwd(hb, after(acc, *tok), vec, ub_1, up_1, down_1, False, False, True)[0])
        hops.append(lax.ppermute(firsts[g], "section", [(0, 1)]))

    tok = firsts[-1]
    attn_w = jnp.concatenate([after(attn_0, tok), attn_1])
    proj_w = jnp.concatenate([after(proj_0, tok), proj_1])
    up_w = jnp.concatenate([after(up_0, tok), up_1])
    down_w = jnp.concatenate([after(down_0, tok), down_1])
    ab = jnp.concatenate([ab_0, ab_1])
    ub = jnp.concatenate([ub_0, ub_1])

    kept, outputs, backs = [], [], []
    tok = (up_w, down_w)
    for g in range(groups):
        x = jnp.where(section == 0, after(x_own[g], *tok), hops[g])
        r1, p, c, a = attn_fwd(x, oks[g], proj_bias, ab, attn_w, proj_w, True, True)
        y, e, slope, r2, hb = ffn_fwd(r1, vec, vec, ub, up_w, down_w, True, True, True)
        dr1, dg = ffn_bwd(cots[g], r2, r1, vec, slope, up_w, down_w, False)
        (d_first,) = attn_bwd(dg, dr1, p, a, attn_w, proj_w, False)
        backs.append(lax.ppermute(d_first, "section", [(1, 0)]))
        kept.append((x, r1, p, c, a, e, slope, r2, hb))
        outputs.append(y)
        tok = (d_first,)

    def ffn_part(g, *before):
        x, r1, p, c, a, e, slope, r2, hb = kept[g]
        dy = jnp.where(section == 1, after(cots[g], *before), backs[g])
        return ffn_bwd(dy, r2, r1, vec, slope, up_w, down_w, True)

    def attn_part(g, dg, dr1):
        x, r1, p, c, a, e, slope, r2, hb = kept[g]
        return attn_bwd(dg, dr1, p, a, attn_w, proj_w, True)

    ffn_parts, attn_parts = [], []
    for g in range(groups):
        ffn_parts.append(ffn_part(g, *tok))
        if g < groups - 1:
            attn_parts.append(attn_part(g, ffn_parts[g][1], ffn_parts[g][0]))
            tok = (attn_parts[g][0],)
    all_of = lambda a, b: [(a(g), b(g)) for g in range(groups)]
    down_terms = all_of(lambda g: kept[g][5], lambda g: ffn_parts[g][2])
    up_terms = all_of(lambda g: kept[g][8], lambda g: ffn_parts[g][3])
    proj_terms = all_of(lambda g: kept[g][3], lambda g: ffn_parts[g][1])

    def following(terms, *before):
        return [(after(terms[0][0], *before), terms[0][1])] + terms[1:]

    out_d = wgrad(down_terms, 1)
    got_d = near(out_d)
    out_u = wgrad(following(up_terms, out_d), 1)
    got_u = near(out_u)
    held_d = wgrad(following(down_terms, out_u), 0, got_d)
    held_u = wgrad(following(up_terms, held_d), 0, got_u)
    out_p = wgrad(following(proj_terms, held_u), 1)
    got_p = near(out_p)
    g = groups - 1
    attn_parts.append(attn_part(g, after(ffn_parts[g][1], out_p), ffn_parts[g][0]))
    attn_terms = all_of(lambda g: attn_parts[g][1], lambda g: kept[g][0])
    out_a = wgrad(attn_terms, 1)
    got_a = near(out_a)
    held_p = wgrad(following(proj_terms, out_a), 0, got_p)
    held_a = wgrad(following(attn_terms, held_p), 0, got_a)
    half, half_u, half_a = units // 2, width // 2, cols // 2
    owned = [(held_d, 0, half), (held_d, half, units), (held_u, 0, half_u), (held_u, half_u, width),
             (held_a, 0, half_a), (held_a, half_a, cols), (held_p, 0, held_p.shape[1])]
    count = len(owned)
    sent, mine = {}, {}
    for k, (held, lo, hi) in enumerate(owned):
        ahead = [mine[k - 2]] if k >= 2 else [sent[k - 1]] if False else []
        sent[k] = over_y(after(held[1, lo:hi], *ahead))
        base = after(held, attn_parts[-1][0], *([mine[k - 1]] if k else []))
        mine[k] = base[0, lo:hi] + sent[k]

    bias_sums = sum(part[2] for part in attn_parts)
    unit_sums = sum(part[4] for part in ffn_parts)
    row_sums = sum(part[5] for part in ffn_parts)[:6].reshape(1, 1, -1)
    small = jnp.concatenate([bias_sums, unit_sums, jnp.broadcast_to(row_sums, (4, 1, 6 * width))], axis=2)
    small = jnp.stack([small[0], small[2]]) + near(jnp.stack([small[1], small[3]]))
    small_sent = over_y(small[1])

    if lax.axis_size("dp") == 4:
        here = lax.axis_index("dp")
        middle = (here == 1) | (here == 2)
        (inward,), cross, (outward,) = chain_steps(4)
        totals = []
        mine[count] = small[0] + small_sent
        firsts_in, crossed = {}, {}
        for k in range(count + 1):
            prior = [crossed[k - 2]] if k >= 2 else []
            got = lax.ppermute(mine[k], "dp", inward)
            firsts_in[k] = after(mine[k], *prior) + got
            got = lax.ppermute(firsts_in[k], "dp", cross)
            crossed[k] = firsts_in[k] + got
            got = lax.ppermute(crossed[k], "dp", outward)
            totals.append(jnp.where(middle, crossed[k], got))
        small = totals.pop()
    else:
        totals = [chain_sum(mine[k], "dp") for k in range(count)]
        small = chain_sum(small[0] + small_sent, "dp")
    totals = [t.astype(F32) for t in totals]
    small = small[0]
    g_attn = jnp.concatenate(totals[4:6], axis=0).reshape(heads, -1, width).transpose(2, 0, 1)
    bias_sum = small[:cols].reshape(heads, 3, -1)
    grad_attn_bias = jnp.concatenate([bias_sum[:, 0], bias_sum[:, 2]], axis=1)
    rowed = small[cols + units:].reshape(6, 1, width)
    return (
        jnp.concatenate(outputs).reshape(1, micro, rows, width),
        jnp.concatenate([part[0] for part in attn_parts]).reshape(1, micro, rows, width),
        g_attn[None],
        grad_attn_bias[None],
        totals[6].reshape(proj_weight.shape),
        rowed[0],
        rowed[1],
        rowed[2],
        jnp.concatenate(totals[2:4], axis=0)[None],
        small[None, cols:cols + units],
        jnp.concatenate(totals[0:2], axis=0)[None],
        rowed[3],
        rowed[4],
        rowed[5],
    )


def solution(mesh):
    rows = P(None, ("dp", "tensor"), None)
    layer = P("section", None)
    placed = (
        rows, rows, P(None, "dp"), P(None, "dp", None),
        P("section", None, "tensor", None), P("section", "tensor", None), P("section", "tensor", None, None),
        layer, layer, layer, P("section", None, "tensor"), P("section", "tensor"), P("section", "tensor", None),
        layer, layer, layer,
    )
    both = P("section", None, ("dp", "tensor"), None)
    return jax.shard_map(
        body,
        mesh=mesh,
        in_specs=placed,
        out_specs=(both, both) + placed[4:],
        check_vma=False,
    )
```

time: 973 us -> 462 us (0.47)
  local copies, waits for them, and re-layouts: 298 us -> 34 us
  matrix products: 240 us -> 0 us
  Pallas kernels: 0 us -> 150 us
  blocking collectives: 77.7 us -> 0 us
  other arithmetic: 109 us -> 34.1 us
  starting transfers between devices: 49.5 us -> 82.6 us
  waiting for transfers between devices: 186 us -> 154 us
    dot_general x33 -> x0, matrix products: 240 us -> none  [the longest x8 92.3 us: mm(): return jnp.dot(a, b, preferred_element_type=F32)]
    pallas_call x0 -> x28, Pallas kernels: none -> 150 us  [the longest x20 124 us: call(): pl.pallas_call(kernel, grid=(count,), in_specs=[spec(p) for p in ins], ou...]
    reshape x13 -> x1, local copies, waits for them, and re-layouts: 81 us -> 0.08 us  [body(): bias_sum = small[:cols].reshape(heads, 3, -1)]
    unnamed x145 -> x191, local copies, waits for them, and re-layouts: 103 us -> 25 us
    psum x1 -> x0, blocking collectives: 77.7 us -> none  [body(): flat = lax.psum(flat, ('dp', 'tensor'))]
    slice x16 -> x10, local copies, waits for them, and re-layouts: 69.5 us -> 3.82 us  [the longest x2 2.84 us: body(): value.reshape(micro * rows, -1)[g * size:(g + 1) * size]]
    convert_element_type x5 -> x0, local copies, waits for them, and re-layouts: 28.4 us -> none  [the longest x3 26 us: backward_layer(): jnp.stack([d_queries, d_keys, d_values], axis=3).reshape(projected.shape)]
    ppermute x14 -> x28, starting transfers between devices: 34.9 us -> 60.2 us  [the longest x8 36 us: body(): got = lax.ppermute(mine[k], 'dp', inward)]
  transfers between devices with their start and end apart: 41 -> 57, of which waited for: 11 -> 18; matrix products, arithmetic and copies ran while one was open for 19% -> 9% of each run, Pallas kernels for 0% -> 27%
where the time goes in v2:
time: 462 us; the launch traced here: 457 us
  waiting for transfers between devices  154 us (33%)
  Pallas kernels  150 us (32%)
  starting transfers between devices  82.6 us (18%)
  other arithmetic  34.1 us (7%)
  local copies, waits for them, and re-layouts  34 us (7%)
    pallas_call x20, Pallas kernels, call(): pl.pallas_call(kernel, grid=(count,), in_specs=[spec(p) for p in ins], ou...  124 us
    ppermute x29, waiting for transfers between devices, swapped(): return lax.ppermute(value, axis, [(i, i ^ bit) for i in range(count)])  81.6 us
    ppermute x8, waiting for transfers between devices, body(): got = lax.ppermute(crossed[k], 'dp', outward)  38.5 us
    ppermute x8, starting transfers between devices, body(): got = lax.ppermute(mine[k], 'dp', inward)  36 us
    pallas_call x8, Pallas kernels, wgrad(): pl.pallas_call(functools.partial(wgrad_kernel, len(pairs), more is not No...  26.1 us
    unnamed x191, local copies, waits for them, and re-layouts  25 us
    ppermute x2, waiting for transfers between devices, body(): hops.append(lax.ppermute(firsts[g], 'section', [(0, 1)]))  23.5 us
    ppermute x29, starting transfers between devices, swapped(): return lax.ppermute(value, axis, [(i, i ^ bit) for i in range(count)])  22.4 us
  transfers between devices with their start and end apart: 57, of which 18 were waited for; matrix products, arithmetic and copies ran while one was open for 9% of the time, Pallas kernels for 27%

profile of v2, /device:TPU:0, one launch (start us, length us, event | category | flops | bytes accessed | tf_op | source)
XLA Modules:
  0.0 457.4 jit_solution(7908188192588318210)
XLA Ops:
  25.6 6.1 %collective-permute-done.4 = bf16[304,768]{1,0:T(8,128)(2,1)} collective-permute-done((bf16[304,768]{1,0:T(8,128)(2,1)S(1)}, bf16[304,768]{1,0:T(8,128)(2,1)}, u32[]{:S(2)}, u32[]{:S(2)}) %collective-permute-start.4) | collective-permute-done | bytes 466976 | tf_op jit(solution)/shard_map/ppermute | solution.py:338
  52.5 10.6 %collective-permute-done.11 = bf16[384,768]{1,0:T(8,128)(2,1)S(1)} collective-permute-done((bf16[384,768]{1,0:T(8,128)(2,1)S(1)}, bf16[384,768]{1,0:T(8,128)(2,1)S(1)}, u32[]{:S(2)}, u32[]{:S(2)}) %collective-permute-start.11) | collective-permute-done | bytes 589856 | tf_op jit(solution)/shard_map/ppermute | solution.py:338
  73.7 7.3 %collective-permute-done.14 = bf16[384,768]{1,0:T(8,128)(2,1)S(1)} collective-permute-done((bf16[384,768]{1,0:T(8,128)(2,1)S(1)}, bf16[384,768]{1,0:T(8,128)(2,1)S(1)}, u32[]{:S(2)}, u32[]{:S(2)}) %collective-permute-start.14) | collective-permute-done | bytes 589856 | tf_op jit(solution)/shard_map/ppermute | solution.py:338
  107.9 23.5 %collective-permute-done.16 = bf16[416,768]{1,0:T(8,128)(2,1)S(1)} collective-permute-done((bf16[416,768]{1,0:T(8,128)(2,1)S(1)}, bf16[416,768]{1,0:T(8,128)(2,1)S(1)}, u32[]{:S(2)}, u32[]{:S(2)}) %collective-permute-start.16) | collective-permute-done | bytes 639008 | tf_op jit(solution)/shard_map/ppermute | solution.py:481
  131.5 7.0 %attn_fwd.10 = (f32[416,768]{1,0:T(8,128)S(1)}, bf16[4,416,576]{2,1,0:T(8,128)(2,1)S(1)}, bf16[4,416,192]{2,1,0:T(8,128)(2,1)S(1)}, bf16[4,2,3,208,208]{4,3,2,1,0:T(8,128)(2,1)S(1)}) custom-call(bf16[416,768]{1,0:T(8,128)(2,1)S(1)} %broadcast_select_fusion.3.x_ref.refs_1_, s32[2,208,1]{2,1,0:T(8,128)S(1)} %slice.267.ok_ref, f32[1,768]{1,0:T(1,128)S(1)} %copy-done.28, ...), custom_call_target="tpu_custom_call" | custom-call | flops 4457496576 | bytes 11478656 | tf_op jit(solution)/shard_map/attn_fwd/pallas_call | solution.py:69
  139.4 9.5 %ffn_fwd.10 = (bf16[416,768]{1,0:T(8,128)(2,1)S(1)}, bf16[4,416,768]{2,1,0:T(8,128)(2,1)S(1)}, bf16[4,416,768]{2,1,0:T(8,128)(2,1)S(1)}, f32[416,768]{1,0:T(8,128)S(1)}, bf16[416,768]{1,0:T(8,128)(2,1)S(1)}) custom-call(f32[416,768]{1,0:T(8,128)S(1)} %get-tuple-element.112.x_ref.r1_ref, f32[5,768]{1,0:T(8,128)S(1)} %concatenate.181.acc_in.vec_ref, ...), custom_call_target="tpu_custom_call" | custom-call | flops 7851737088 | bytes 18425856 | tf_op jit(solution)/shard_map/ffn_fwd/pallas_call | solution.py:69
  149.0 6.9 %ffn_bwd.4 = (f32[416,768]{1,0:T(8,128)S(1)}, bf16[416,768]{1,0:T(8,128)(2,1)S(1)}) custom-call(bf16[416,768]{1,0:T(8,128)(2,1)S(1)} %bitcast.98, f32[416,768]{1,0:T(8,128)S(1)} %get-tuple-element.114.r2_ref, f32[416,768]{1,0:T(8,128)S(1)} %get-tuple-element.112.x_ref.r1_ref, f32[5,768]{1,0:T(8,128)S(1)} %concatenate.181.acc_in.vec_ref, ...), custom_call_target="tpu_custom_call" | custom-call | flops 7851737088 | bytes 17120256 | tf_op jit(solution)/shard_map/ffn_bwd/pallas_call | solution.py:69
  155.9 7.7 %attn_bwd.4 = bf16[416,768]{1,0:T(8,128)(2,1)S(1)} custom-call(bf16[416,768]{1,0:T(8,128)(2,1)S(1)} %get-tuple-element.116.dg_ref, f32[416,768]{1,0:T(8,128)S(1)} %get-tuple-element.117.dr1_ref, bf16[4,416,576]{2,1,0:T(8,128)(2,1)S(1)} %get-tuple-element.118.p_ref, bf16[4,2,3,208,208]{4,3,2,1,0:T(8,128)(2,1)S(1)} %get-tuple-element.119.a_ref, ...), custom_call_target="tpu_custom_call" | custom-call | flops 4989124608 | bytes 11464704 | tf_op jit(solution)/shard_map/attn_bwd/pallas_call | solution.py:69
  165.0 7.1 %attn_fwd.11 = (f32[416,768]{1,0:T(8,128)S(1)}, bf16[4,416,576]{2,1,0:T(8,128)(2,1)S(1)}, bf16[4,416,192]{2,1,0:T(8,128)(2,1)S(1)}, bf16[4,2,3,208,208]{4,3,2,1,0:T(8,128)(2,1)S(1)}) custom-call(bf16[416,768]{1,0:T(8,128)(2,1)S(1)} %broadcast_select_fusion.2.x_ref.refs_3_, s32[2,208,1]{2,1,0:T(8,128)S(1)} %slice.266.ok_ref, f32[1,768]{1,0:T(1,128)S(1)} %copy-done.28, ...), custom_call_target="tpu_custom_call" | custom-call | flops 4457496576 | bytes 11478656 | tf_op jit(solution)/shard_map/attn_fwd/pallas_call | solution.py:69
  173.6 9.5 %ffn_fwd.11 = (bf16[416,768]{1,0:T(8,128)(2,1)S(1)}, bf16[4,416,768]{2,1,0:T(8,128)(2,1)S(1)}, bf16[4,416,768]{2,1,0:T(8,128)(2,1)S(1)}, f32[416,768]{1,0:T(8,128)S(1)}, bf16[416,768]{1,0:T(8,128)(2,1)S(1)}) custom-call(f32[416,768]{1,0:T(8,128)S(1)} %get-tuple-element.121.x_ref.r1_ref, f32[5,768]{1,0:T(8,128)S(1)} %concatenate.181.acc_in.vec_ref, ...), custom_call_target="tpu_custom_call" | custom-call | flops 7851737088 | bytes 18425856 | tf_op jit(solution)/shard_map/ffn_fwd/pallas_call | solution.py:69
  183.2 6.8 %ffn_bwd.5 = (f32[416,768]{1,0:T(8,128)S(1)}, bf16[416,768]{1,0:T(8,128)(2,1)S(1)}) custom-call(bf16[416,768]{1,0:T(8,128)(2,1)S(1)} %bitcast.96, f32[416,768]{1,0:T(8,128)S(1)} %get-tuple-element.123.r2_ref, f32[416,768]{1,0:T(8,128)S(1)} %get-tuple-element.121.x_ref.r1_ref, f32[5,768]{1,0:T(8,128)S(1)} %concatenate.181.acc_in.vec_ref, ...), custom_call_target="tpu_custom_call" | custom-call | flops 7851737088 | bytes 17120256 | tf_op jit(solution)/shard_map/ffn_bwd/pallas_call | solution.py:69
  190.1 7.7 %attn_bwd.5 = bf16[416,768]{1,0:T(8,128)(2,1)S(1)} custom-call(bf16[416,768]{1,0:T(8,128)(2,1)S(1)} %get-tuple-element.125.dg_ref, f32[416,768]{1,0:T(8,128)S(1)} %get-tuple-element.126.dr1_ref, bf16[4,416,576]{2,1,0:T(8,128)(2,1)S(1)} %copy-done.58, bf16[4,2,3,208,208]{4,3,2,1,0:T(8,128)(2,1)S(1)} %copy-done.45, ...), custom_call_target="tpu_custom_call" | custom-call | flops 4989124608 | bytes 11464704 | tf_op jit(solution)/shard_map/attn_bwd/pallas_call | solution.py:69
  200.5 7.6 %ffn_bwd.6 = (f32[416,768]{1,0:T(8,128)S(1)}, bf16[416,768]{1,0:T(8,128)(2,1)S(1)}, bf16[416,768]{1,0:T(8,128)(2,1)S(1)}, bf16[4,416,768]{2,1,0:T(8,128)(2,1)S(1...) custom-call(bf16[416,768]{1,0:T(8,128)(2,1)S(1)} %broadcast_select_fusion.1.dy_ref, f32[416,768]{1,0:T(8,128)S(1)} %copy-done.73, ...), custom_call_target="tpu_custom_call" | custom-call | flops 7851737088 | bytes 20352000 | tf_op jit(solution)/shard_map/ffn_bwd/pallas_call | solution.py:69
  211.8 7.7 %attn_bwd.6 = (f32[416,768]{1,0:T(8,128)S(1)}, bf16[4,416,576]{2,1,0:T(8,128)(2,1)S(1)}, f32[4,1,576]{2,1,0:T(1,128)S(1)}) custom-call(bf16[416,768]{1,0:T(8,128)(2,1)S(1)} %get-tuple-element.130.dg_ref.refs_1_, f32[416,768]{1,0:T(8,128)S(1)} %get-tuple-element.131.dr1_ref, bf16[4,416,576]{2,1,0:T(8,128)(2,1)S(1)} %copy-done.61, ...), custom_call_target="tpu_custom_call" | custom-call | flops 4989124608 | bytes 14029824 | tf_op jit(solution)/shard_map/attn_bwd/pallas_call | solution.py:69
  225.1 7.3 %ffn_bwd.7 = (f32[416,768]{1,0:T(8,128)S(1)}, bf16[416,768]{1,0:T(8,128)(2,1)S(1)}, bf16[416,768]{1,0:T(8,128)(2,1)S(1)}, bf16[4,416,768]{2,1,0:T(8,128)(2,1)S(1...) custom-call(bf16[416,768]{1,0:T(8,128)(2,1)S(1)} %broadcast_select_fusion.dy_ref, f32[416,768]{1,0:T(8,128)S(1)} %copy-done.75, ...), custom_call_target="tpu_custom_call" | custom-call | flops 7851737088 | bytes 20352000 | tf_op jit(solution)/shard_map/ffn_bwd/pallas_call | solution.py:69
  262.6 7.7 %attn_bwd.7 = (f32[416,768]{1,0:T(8,128)S(1)}, bf16[4,416,576]{2,1,0:T(8,128)(2,1)S(1)}, f32[4,1,576]{2,1,0:T(1,128)S(1)}) custom-call(bf16[416,768]{1,0:T(8,128)(2,1)S(1)} %copy-done.26, f32[416,768]{1,0:T(8,128)S(1)} %copy-done.63, bf16[4,416,576]{2,1,0:T(8,128)(2,1)S(1)} %copy-done.59, bf16[4,2,3,208,208]{4,3,2,1,0:T(8,128)(2,1)S(1)} %copy-done.46, ...), custom_call_target="tpu_custom_call" | custom-call | flops 4989124608 | bytes 14029824 | tf_op jit(solution)/shard_map/attn_bwd/pallas_call | solution.py:69
  286.1 25.8 %collective-permute-done.24 = bf16[384,768]{1,0:T(8,128)(2,1)S(1)} collective-permute-done((bf16[384,768]{1,0:T(8,128)(2,1)S(1)}, bf16[384,768]{1,0:T(8,128)(2,1)S(1)}, u32[]{:S(2)}, u32[]{:S(2)}) %collective-permute-start.24) | collective-permute-done | bytes 589856 | tf_op jit(solution)/shard_map/ppermute | solution.py:338
  320.1 21.4 %collective-permute-done.26 = bf16[384,768]{1,0:T(8,128)(2,1)S(1)} collective-permute-done((bf16[384,768]{1,0:T(8,128)(2,1)S(1)}, bf16[384,768]{1,0:T(8,128)(2,1)S(1)}, u32[]{:S(2)}, u32[]{:S(2)}) %collective-permute-start.26) | collective-permute-done | bytes 589856 | tf_op jit(solution)/shard_map/ppermute | solution.py:338
  358.2 9.9 %collective-permute-done.39 = bf16[384,768]{1,0:T(8,128)(2,1)S(1)} collective-permute-done((bf16[384,768]{1,0:T(8,128)(2,1)S(1)}, bf16[384,768]{1,0:T(8,128)(2,1)S(1)}, u32[]{:S(2)}, u32[]{:S(2)}) %collective-permute-start.39) | collective-permute-done | bytes 589856 | tf_op jit(solution)/shard_map/ppermute | solution.py:569
  373.5 11.0 %collective-permute-start.41 = (bf16[288,768]{1,0:T(8,128)(2,1)S(1)}, bf16[288,768]{1,0:T(8,128)(2,1)S(1)}, u32[]{:S(2)}, u32[]{:S(2)}) collective-permute-start(bf16[288,768]{1,0:T(8,128)(2,1)S(1)} %bitcast_add_fusion.4), channel_id=1, source_target_pairs={{0,4},{12,8},{1,5},{13,9},{2,6},{14,10},{3,7},{15,11},{16,20},{28,... | collective-permute-start | bytes 1327112 | tf_op jit(solution)/shard_map/ppermute | solution.py:569
  400.9 8.8 %collective-permute-start.46 = (f32[1,5952]{1,0:T(1,128)S(1)}, f32[1,5952]{1,0:T(1,128)S(1)}, u32[]{:S(2)}, u32[]{:S(2)}) collective-permute-start(f32[1,5952]{1,0:T(1,128)S(1)} %fusion.8), channel_id=1, source_target_pairs={{0,4},{12,8},{1,5},{13,9},{2,6},{14,10},{3,7},{15,11},{16,20},{28,... | collective-permute-start | bytes 71432 | tf_op jit(solution)/shard_map/ppermute | solution.py:569
  420.4 6.7 %collective-permute-done.53 = bf16[384,768]{1,0:T(8,128)(2,1)S(1)} collective-permute-done((bf16[384,768]{1,0:T(8,128)(2,1)S(1)}, bf16[384,768]{1,0:T(8,128)(2,1)S(1)}, u32[]{:S(2)}, u32[]{:S(2)}) %collective-permute-start.53) | collective-permute-done | bytes 589856 | tf_op jit(solution)/shard_map/ppermute | solution.py:573
  436.5 8.8 %collective-permute-done.43 = bf16[288,768]{1,0:T(8,128)(2,1)S(1)} collective-permute-done((bf16[288,768]{1,0:T(8,128)(2,1)S(1)}, bf16[288,768]{1,0:T(8,128)(2,1)S(1)}, u32[]{:S(2)}, u32[]{:S(2)}) %collective-permute-start.43) | collective-permute-done | bytes 442400 | tf_op jit(solution)/shard_map/ppermute | solution.py:573
  445.4 7.5 %collective-permute-done.35 = bf16[288,768]{1,0:T(8,128)(2,1)S(1)} collective-permute-done((bf16[288,768]{1,0:T(8,128)(2,1)S(1)}, bf16[288,768]{1,0:T(8,128)(2,1)S(1)}, u32[]{:S(2)}, u32[]{:S(2)}) %collective-permute-start.35) | collective-permute-done | bytes 442400 | tf_op jit(solution)/shard_map/ppermute | solution.py:573
  (430 shorter events, 214.2 us)
Async XLA Ops:
  8.7 24.5 %collective-permute-start.2 = (bf16[608,768]{1,0:T(8,128)(2,1)}, bf16[608,768]{1,0:T(8,128)(2,1)}, u32[]{:S(2)}, u32[]{:S(2)}) collective-permute-start(bf16[608,768]{1,0:T(8,128)(2,1)} %get-tuple-element.197), channel_id=1, source_target_pairs={{0,1},{1,0},{2,3},{3,2},{4,5},{5,4},{6,7},{7,6},{8,9},{9,8},{10,11... | collective-permute-start | bytes 2801672 | tf_op jit(solution)/shard_map/ppermute | solution.py:338
  23.0 28.9 %collective-permute-start.1 = (bf16[768,768]{1,0:T(8,128)(2,1)S(1)}, bf16[768,768]{1,0:T(8,128)(2,1)S(1)}, u32[]{:S(2)}, u32[]{:S(2)}) collective-permute-start(bf16[768,768]{1,0:T(8,128)(2,1)S(1)} %bitcast.115), channel_id=1, source_target_pairs={{0,1},{1,0},{2,3},{3,2},{4,5},{5,4},{6,7},{7,6},{8,9},{9,8},{10,11... | collective-permute-start | bytes 3538952 | tf_op jit(solution)/shard_map/ppermute | solution.py:338
  24.0 24.4 %collective-permute-start.10 = (bf16[384,768]{1,0:T(8,128)(2,1)S(1)}, bf16[384,768]{1,0:T(8,128)(2,1)S(1)}, u32[]{:S(2)}, u32[]{:S(2)}) collective-permute-start(bf16[384,768]{1,0:T(8,128)(2,1)S(1)} %copy-done.83), channel_id=1, source_target_pairs={{0,2},{1,3},{2,0},{3,1},{4,6},{5,7},{6,4},{7,5},{8,10},{9,11},{10,... | collective-permute-start | bytes 1769480 | tf_op jit(solution)/shard_map/ppermute | solution.py:338
  33.1 33.3 %collective-permute-start.5 = (bf16[608,768]{1,0:T(8,128)(2,1)S(1)}, bf16[608,768]{1,0:T(8,128)(2,1)S(1)}, u32[]{:S(2)}, u32[]{:S(2)}) collective-permute-start(bf16[608,768]{1,0:T(8,128)(2,1)S(1)} %maximum_select_fusion.5), channel_id=1, source_target_pairs={{0,1},{1,0},{2,3},{3,2},{4,5},{5,4},{6,7},{7,6},{8,9},{9,8},{10,11... | collective-permute-start | bytes 2801672 | tf_op jit(solution)/shard_map/ppermute | solution.py:338
  51.9 30.1 %collective-permute-start.9 = (bf16[768,768]{1,0:T(8,128)(2,1)S(1)}, bf16[768,768]{1,0:T(8,128)(2,1)S(1)}, u32[]{:S(2)}, u32[]{:S(2)}) collective-permute-start(bf16[768,768]{1,0:T(8,128)(2,1)S(1)} %bitcast.116), channel_id=1, source_target_pairs={{0,1},{1,0},{2,3},{3,2},{4,5},{5,4},{6,7},{7,6},{8,9},{9,8},{10,11... | collective-permute-start | bytes 3538952 | tf_op jit(solution)/shard_map/ppermute | solution.py:338
  63.6 27.5 %collective-permute-start.12 = (bf16[768,768]{1,0:T(8,128)(2,1)S(1)}, bf16[768,768]{1,0:T(8,128)(2,1)S(1)}, u32[]{:S(2)}, u32[]{:S(2)}) collective-permute-start(bf16[768,768]{1,0:T(8,128)(2,1)S(1)} %maximum_select_fusion.1), channel_id=1, source_target_pairs={{0,1},{1,0},{2,3},{3,2},{4,5},{5,4},{6,7},{7,6},{8,9},{9,8},{10,11... | collective-permute-start | bytes 3538952 | tf_op jit(solution)/shard_map/ppermute | solution.py:338
  100.0 64.9 %collective-permute-start.17 = (bf16[416,768]{1,0:T(8,128)(2,1)S(1)}, bf16[416,768]{1,0:T(8,128)(2,1)}, u32[]{:S(2)}, u32[]{:S(2)}) collective-permute-start(bf16[416,768]{1,0:T(8,128)(2,1)S(1)} %ffn_fwd.9), channel_id=1, source_target_pairs={{0,16},{1,17},{2,18},{3,19},{4,20},{5,21},{6,22},{7,23},{8,24},{9,... | collective-permute-start | bytes 1916936 | tf_op jit(solution)/shard_map/ppermute | solution.py:481
  104.3 27.1 %collective-permute-start.16 = (bf16[416,768]{1,0:T(8,128)(2,1)S(1)}, bf16[416,768]{1,0:T(8,128)(2,1)S(1)}, u32[]{:S(2)}, u32[]{:S(2)}) collective-permute-start(bf16[416,768]{1,0:T(8,128)(2,1)S(1)} %ffn_fwd.8), channel_id=1, source_target_pairs={{0,16},{1,17},{2,18},{3,19},{4,20},{5,21},{6,22},{7,23},{8,24},{9,... | collective-permute-start | bytes 1916936 | tf_op jit(solution)/shard_map/ppermute | solution.py:481
  163.6 35.7 %collective-permute-start.18 = (bf16[416,768]{1,0:T(8,128)(2,1)S(1)}, bf16[416,768]{1,0:T(8,128)(2,1)}, u32[]{:S(2)}, u32[]{:S(2)}) collective-permute-start(bf16[416,768]{1,0:T(8,128)(2,1)S(1)} %attn_bwd.4), channel_id=1, source_target_pairs={{16,0},{17,1},{18,2},{19,3},{20,4},{21,5},{22,6},{23,7},{24,8},{25... | collective-permute-start | bytes 1916936 | tf_op jit(solution)/shard_map/ppermute | solution.py:499
  197.8 24.2 %collective-permute-start.19 = (bf16[416,768]{1,0:T(8,128)(2,1)S(1)}, bf16[416,768]{1,0:T(8,128)(2,1)S(1)}, u32[]{:S(2)}, u32[]{:S(2)}) collective-permute-start(bf16[416,768]{1,0:T(8,128)(2,1)S(1)} %attn_bwd.5), channel_id=1, source_target_pairs={{16,0},{17,1},{18,2},{19,3},{20,4},{21,5},{22,6},{23,7},{24,8},{25... | collective-permute-start | bytes 1916936 | tf_op jit(solution)/shard_map/ppermute | solution.py:499
  259.6 57.1 %collective-permute-start.22 = (bf16[2,192,768]{2,1,0:T(8,128)(2,1)}, bf16[2,192,768]{2,1,0:T(8,128)(2,1)}, u32[]{:S(2)}, u32[]{:S(2)}) collective-permute-start(bf16[2,192,768]{2,1,0:T(8,128)(2,1)} %wgrad.12), channel_id=1, source_target_pairs={{0,1},{1,0},{2,3},{3,2},{4,5},{5,4},{6,7},{7,6},{8,9},{9,8},{10,11... | collective-permute-start | bytes 1769480 | tf_op jit(solution)/shard_map/ppermute | solution.py:338
  283.4 67.8 %collective-permute-start.23 = (bf16[2,576,768]{2,1,0:T(8,128)(2,1)S(1)}, bf16[2,576,768]{2,1,0:T(8,128)(2,1)S(1)}, u32[]{:S(2)}, u32[]{:S(2)}) collective-permute-start(bf16[2,576,768]{2,1,0:T(8,128)(2,1)S(1)} %wgrad.13), channel_id=1, source_target_pairs={{0,1},{1,0},{2,3},{3,2},{4,5},{5,4},{6,7},{7,6},{8,9},{9,8},{10,11... | collective-permute-start | bytes 5308424 | tf_op jit(solution)/shard_map/ppermute | solution.py:338
  283.9 28.0 %collective-permute-start.25 = (bf16[384,768]{1,0:T(8,128)(2,1)S(1)}, bf16[384,768]{1,0:T(8,128)(2,1)S(1)}, u32[]{:S(2)}, u32[]{:S(2)}) collective-permute-start(bf16[384,768]{1,0:T(8,128)(2,1)S(1)} %copy-done.84), channel_id=1, source_target_pairs={{0,2},{1,3},{2,0},{3,1},{4,6},{5,7},{6,4},{7,5},{8,10},{9,11},{10,... | collective-permute-start | bytes 1769480 | tf_op jit(solution)/shard_map/ppermute | solution.py:338
  285.4 26.4 %collective-permute-start.24 = (bf16[384,768]{1,0:T(8,128)(2,1)S(1)}, bf16[384,768]{1,0:T(8,128)(2,1)S(1)}, u32[]{:S(2)}, u32[]{:S(2)}) collective-permute-start(bf16[384,768]{1,0:T(8,128)(2,1)S(1)} %copy-done.85), channel_id=1, source_target_pairs={{0,2},{1,3},{2,0},{3,1},{4,6},{5,7},{6,4},{7,5},{8,10},{9,11},{10,... | collective-permute-start | bytes 1769480 | tf_op jit(solution)/shard_map/ppermute | solution.py:338
  312.0 31.0 %collective-permute-start.37 = (bf16[384,768]{1,0:T(8,128)(2,1)S(1)}, bf16[384,768]{1,0:T(8,128)(2,1)S(1)}, u32[]{:S(2)}, u32[]{:S(2)}) collective-permute-start(bf16[384,768]{1,0:T(8,128)(2,1)S(1)} %bitcast_add_fusion.2), channel_id=1, source_target_pairs={{0,4},{12,8},{1,5},{13,9},{2,6},{14,10},{3,7},{15,11},{16,20},{28,... | collective-permute-start | bytes 1769480 | tf_op jit(solution)/shard_map/ppermute | solution.py:569
  314.6 30.4 %collective-permute-start.27 = (bf16[384,768]{1,0:T(8,128)(2,1)S(1)}, bf16[384,768]{1,0:T(8,128)(2,1)S(1)}, u32[]{:S(2)}, u32[]{:S(2)}) collective-permute-start(bf16[384,768]{1,0:T(8,128)(2,1)S(1)} %copy-done.81), channel_id=1, source_target_pairs={{0,2},{1,3},{2,0},{3,1},{4,6},{5,7},{6,4},{7,5},{8,10},{9,11},{10,... | collective-permute-start | bytes 1769480 | tf_op jit(solution)/shard_map/ppermute | solution.py:338
  316.1 25.3 %collective-permute-start.26 = (bf16[384,768]{1,0:T(8,128)(2,1)S(1)}, bf16[384,768]{1,0:T(8,128)(2,1)S(1)}, u32[]{:S(2)}, u32[]{:S(2)}) collective-permute-start(bf16[384,768]{1,0:T(8,128)(2,1)S(1)} %copy-done.82), channel_id=1, source_target_pairs={{0,2},{1,3},{2,0},{3,1},{4,6},{5,7},{6,4},{7,5},{8,10},{9,11},{10,... | collective-permute-start | bytes 1769480 | tf_op jit(solution)/shard_map/ppermute | solution.py:338
  316.7 29.2 %collective-permute-start.29 = (bf16[384,768]{1,0:T(8,128)(2,1)S(1)}, bf16[384,768]{1,0:T(8,128)(2,1)S(1)}, u32[]{:S(2)}, u32[]{:S(2)}) collective-permute-start(bf16[384,768]{1,0:T(8,128)(2,1)S(1)} %bitcast_add_fusion.3), channel_id=1, source_target_pairs={{0,4},{12,8},{1,5},{13,9},{2,6},{14,10},{3,7},{15,11},{16,20},{28,... | collective-permute-start | bytes 1769480 | tf_op jit(solution)/shard_map/ppermute | solution.py:569
  343.0 26.5 %collective-permute-start.31 = (bf16[384,768]{1,0:T(8,128)(2,1)S(1)}, bf16[384,768]{1,0:T(8,128)(2,1)S(1)}, u32[]{:S(2)}, u32[]{:S(2)}) collective-permute-start(bf16[384,768]{1,0:T(8,128)(2,1)S(1)} %bitcast_add_fusion.1), channel_id=1, source_target_pairs={{0,4},{12,8},{1,5},{13,9},{2,6},{14,10},{3,7},{15,11},{16,20},{28,... | collective-permute-start | bytes 1769480 | tf_op jit(solution)/shard_map/ppermute | solution.py:569
  356.7 31.9 %collective-permute-start.56 = (bf16[384,768]{1,0:T(8,128)(2,1)S(1)}, bf16[384,768]{1,0:T(8,128)(2,1)S(1)}, u32[]{:S(2)}, u32[]{:S(2)}) collective-permute-start(bf16[384,768]{1,0:T(8,128)(2,1)S(1)} %add.118), channel_id=1, source_target_pairs={{4,0},{8,12},{5,1},{9,13},{6,2},{10,14},{7,3},{11,15},{20,16},{24,... | collective-permute-start | bytes 1769480 | tf_op jit(solution)/shard_map/ppermute | solution.py:573
  368.1 29.8 %collective-permute-start.55 = (bf16[384,768]{1,0:T(8,128)(2,1)S(1)}, bf16[384,768]{1,0:T(8,128)(2,1)S(1)}, u32[]{:S(2)}, u32[]{:S(2)}) collective-permute-start(bf16[384,768]{1,0:T(8,128)(2,1)S(1)} %add.111), channel_id=1, source_target_pairs={{4,0},{8,12},{5,1},{9,13},{6,2},{10,14},{7,3},{11,15},{20,16},{24,... | collective-permute-start | bytes 1769480 | tf_op jit(solution)/shard_map/ppermute | solution.py:573
  373.5 27.4 %collective-permute-start.41 = (bf16[288,768]{1,0:T(8,128)(2,1)S(1)}, bf16[288,768]{1,0:T(8,128)(2,1)S(1)}, u32[]{:S(2)}, u32[]{:S(2)}) collective-permute-start(bf16[288,768]{1,0:T(8,128)(2,1)S(1)} %bitcast_add_fusion.4), channel_id=1, source_target_pairs={{0,4},{12,8},{1,5},{13,9},{2,6},{14,10},{3,7},{15,11},{16,20},{28,... | collective-permute-start | bytes 1327112 | tf_op jit(solution)/shard_map/ppermute | solution.py:569
  390.9 27.9 %collective-permute-start.54 = (bf16[384,768]{1,0:T(8,128)(2,1)S(1)}, bf16[384,768]{1,0:T(8,128)(2,1)S(1)}, u32[]{:S(2)}, u32[]{:S(2)}) collective-permute-start(bf16[384,768]{1,0:T(8,128)(2,1)S(1)} %add.120), channel_id=1, source_target_pairs={{4,0},{8,12},{5,1},{9,13},{6,2},{10,14},{7,3},{11,15},{20,16},{24,... | collective-permute-start | bytes 1769480 | tf_op jit(solution)/shard_map/ppermute | solution.py:573
  397.9 29.2 %collective-permute-start.53 = (bf16[384,768]{1,0:T(8,128)(2,1)S(1)}, bf16[384,768]{1,0:T(8,128)(2,1)S(1)}, u32[]{:S(2)}, u32[]{:S(2)}) collective-permute-start(bf16[384,768]{1,0:T(8,128)(2,1)S(1)} %add.113), channel_id=1, source_target_pairs={{4,0},{8,12},{5,1},{9,13},{6,2},{10,14},{7,3},{11,15},{20,16},{24,... | collective-permute-start | bytes 1769480 | tf_op jit(solution)/shard_map/ppermute | solution.py:573
  (127 other events, 1511.8 us)

commit v3 on v2

--- a/solution.py
+++ b/solution.py
@@ -74,7 +74,7 @@
         out_shape=[a for a, _ in outs],
         scratch_shapes=scratch,
         compiler_params=pltpu.CompilerParams(vmem_limit_bytes=limit * MIB),
-        cost_estimate=pl.CostEstimate(flops=2 * flops, bytes_accessed=size, transcendentals=0),
+        cost_estimate=pl.CostEstimate(flops=1, bytes_accessed=1, transcendentals=0),
         name=name,
     )(*[a for a, _ in ins])
 
@@ -297,7 +297,7 @@
                 [pltpu.VMEM((rows, width), F32)], flops)
 
 
-def wgrad_kernel(pairs, added, *refs):
+def wgrad_kernel(pairs, *refs):
     total = None
     for g in range(pairs):
         a, b = refs[2 * g], refs[2 * g + 1]
@@ -305,12 +305,12 @@
         b = b[0] if len(b.shape) == 3 else b[...]
         part = dot_tn(a, b)
         total = part if total is None else total + part
-    if added:
-        total = total + refs[2 * pairs][0].astype(F32)
+    for more in refs[2 * pairs:-1]:
+        total = total + more[0].astype(F32)
     refs[-1][0] = total.astype(BF)
 
 
-def wgrad(pairs, odd, more=None):
+def wgrad(pairs, odd, *more):
     def spec(a):
         if a.ndim == 2:
             return pl.BlockSpec(a.shape, lambda i: (0, 0))
@@ -319,18 +319,25 @@
     flat = [a for pair in pairs for a in pair]
     dims = (2, pairs[0][0].shape[-1], pairs[0][1].shape[-1])
     block = pl.BlockSpec((1,) + dims[1:], lambda i: (i, 0, 0))
-    extra = [] if more is None else [more]
-    rows = sum(a.shape[-2] for a, _ in pairs)
     return pl.pallas_call(
-        functools.partial(wgrad_kernel, len(pairs), more is not None),
+        functools.partial(wgrad_kernel, len(pairs)),
         grid=(2,),
-        in_specs=[spec(a) for a in flat] + [block] * len(extra),
+        in_specs=[spec(a) for a in flat] + [block] * len(more),
         out_specs=block,
         out_shape=shape(*dims),
         compiler_params=pltpu.CompilerParams(vmem_limit_bytes=24 * MIB),
-        cost_estimate=pl.CostEstimate(flops=8 * rows * dims[1] * dims[2], bytes_accessed=8 * MIB, transcendentals=0),
+        cost_estimate=pl.CostEstimate(flops=1, bytes_accessed=1, transcendentals=0),
         name="wgrad",
-    )(*flat, *extra)
+    )(*flat, *more)
+
+
+STEPS = (
+    "out a", "out p", "take d", "held a", "held p", "cross d0", "in d1", "cross d1",
+    "take u", "outw d0", "cross u0", "in u1", "outw d1", "fin d0", "take a", "cross u1",
+    "outw u0", "cross a0", "in a1", "fin d1", "outw u1", "take s", "take p", "cross a1",
+    "outw a0", "fin u0", "cross s0", "cross p0", "fin u1", "outw a1", "outw s0", "outw p0",
+    "fin a0", "fin a1", "fin s0", "fin p0",
+)
 
 
 def swapped(value, axis, bit):
@@ -441,14 +448,14 @@
 
     attn_mine = over_y(part(attn_own))
     attn_near = near(attn_own)
-    proj_mine = over_y(after(part(proj_own), attn_near))
+    proj_mine = over_y(part(proj_own))
     proj_near = near(proj_own)
     up_mine = over_y(after(part(up_own), attn_mine))
     attn_pair = along_dp(attn_mine)
-    up_near = near(after(up_own, proj_near))
+    up_near = near(up_own)
     down_mine = over_y(after(part(down_own), proj_mine))
     proj_pair = along_dp(proj_mine)
-    down_near = near(after(down_own, up_near))
+    down_near = near(down_own)
     up_pair = along_dp(up_mine)
     down_pair = along_dp(down_mine)
 
@@ -478,7 +485,7 @@
         tok = firsts[-1:]
         acc, hb = halves[g]
         firsts.append(ffn_fwd(hb, after(acc, *tok), vec, ub_1, up_1, down_1, False, False, True)[0])
-        hops.append(lax.ppermute(firsts[g], "section", [(0, 1)]))
+        hops.append(lax.ppermute(after(firsts[g], *hops[-1:]), "section", [(0, 1)]))
 
     tok = firsts[-1]
     attn_w = jnp.concatenate([after(attn_0, tok), attn_1])
@@ -511,71 +518,87 @@
         return attn_bwd(dg, dr1, p, a, attn_w, proj_w, True)
 
     ffn_parts, attn_parts = [], []
+    down_pre, up_pre = [[], []], [[], []]
+
+    def following(terms, *before):
+        return [(after(terms[0][0], *before), terms[0][1])] + terms[1:]
+
     for g in range(groups):
         ffn_parts.append(ffn_part(g, *tok))
         if g < groups - 1:
-            attn_parts.append(attn_part(g, ffn_parts[g][1], ffn_parts[g][0]))
-            tok = (attn_parts[g][0],)
+            down_term = (kept[g][5], ffn_parts[g][2])
+            up_term = (kept[g][8], ffn_parts[g][3])
+            for odd_share in (1, 0):
+                down_pre[odd_share] = [wgrad([down_term], odd_share, *down_pre[odd_share])]
+                up_pre[odd_share] = [wgrad([up_term], odd_share, *up_pre[odd_share])]
+            tok = (*down_pre[0], *down_pre[1], *up_pre[0], *up_pre[1])
+    g = groups - 1
+    down_terms, up_terms = [(kept[g][5], ffn_parts[g][2])], [(kept[g][8], ffn_parts[g][3])]
     all_of = lambda a, b: [(a(g), b(g)) for g in range(groups)]
-    down_terms = all_of(lambda g: kept[g][5], lambda g: ffn_parts[g][2])
-    up_terms = all_of(lambda g: kept[g][8], lambda g: ffn_parts[g][3])
     proj_terms = all_of(lambda g: kept[g][3], lambda g: ffn_parts[g][1])
 
-    def following(terms, *before):
-        return [(after(terms[0][0], *before), terms[0][1])] + terms[1:]
-
-    out_d = wgrad(down_terms, 1)
+    out_d = wgrad(down_terms, 1, *down_pre[1])
     got_d = near(out_d)
-    out_u = wgrad(following(up_terms, out_d), 1)
+    out_u = wgrad(following(up_terms, out_d), 1, *up_pre[1])
     got_u = near(out_u)
-    held_d = wgrad(following(down_terms, out_u), 0, got_d)
-    held_u = wgrad(following(up_terms, held_d), 0, got_u)
-    out_p = wgrad(following(proj_terms, held_u), 1)
-    got_p = near(out_p)
-    g = groups - 1
-    attn_parts.append(attn_part(g, after(ffn_parts[g][1], out_p), ffn_parts[g][0]))
+    held_d = wgrad(following(down_terms, out_u), 0, *down_pre[0], got_d)
+    held_u = wgrad(following(up_terms, held_d), 0, *up_pre[0], got_u)
+    tok = (held_u,)
+    for g in range(groups):
+        attn_parts.append(attn_part(g, after(ffn_parts[g][1], *tok), ffn_parts[g][0]))
+        tok = (attn_parts[g][0],)
     attn_terms = all_of(lambda g: attn_parts[g][1], lambda g: kept[g][0])
-    out_a = wgrad(attn_terms, 1)
-    got_a = near(out_a)
-    held_p = wgrad(following(proj_terms, out_a), 0, got_p)
-    held_a = wgrad(following(attn_terms, held_p), 0, got_a)
     half, half_u, half_a = units // 2, width // 2, cols // 2
-    owned = [(held_d, 0, half), (held_d, half, units), (held_u, 0, half_u), (held_u, half_u, width),
-             (held_a, 0, half_a), (held_a, half_a, cols), (held_p, 0, held_p.shape[1])]
-    count = len(owned)
-    sent, mine = {}, {}
-    for k, (held, lo, hi) in enumerate(owned):
-        ahead = [mine[k - 2]] if k >= 2 else [sent[k - 1]] if False else []
-        sent[k] = over_y(after(held[1, lo:hi], *ahead))
-        base = after(held, attn_parts[-1][0], *([mine[k - 1]] if k else []))
-        mine[k] = base[0, lo:hi] + sent[k]
 
     bias_sums = sum(part[2] for part in attn_parts)
     unit_sums = sum(part[4] for part in ffn_parts)
     row_sums = sum(part[5] for part in ffn_parts)[:6].reshape(1, 1, -1)
     small = jnp.concatenate([bias_sums, unit_sums, jnp.broadcast_to(row_sums, (4, 1, 6 * width))], axis=2)
     small = jnp.stack([small[0], small[2]]) + near(jnp.stack([small[1], small[3]]))
-    small_sent = over_y(small[1])
-
-    if lax.axis_size("dp") == 4:
-        here = lax.axis_index("dp")
-        middle = (here == 1) | (here == 2)
-        (inward,), cross, (outward,) = chain_steps(4)
-        totals = []
-        mine[count] = small[0] + small_sent
-        firsts_in, crossed = {}, {}
-        for k in range(count + 1):
-            prior = [crossed[k - 2]] if k >= 2 else []
-            got = lax.ppermute(mine[k], "dp", inward)
-            firsts_in[k] = after(mine[k], *prior) + got
-            got = lax.ppermute(firsts_in[k], "dp", cross)
-            crossed[k] = firsts_in[k] + got
-            got = lax.ppermute(crossed[k], "dp", outward)
-            totals.append(jnp.where(middle, crossed[k], got))
-        small = totals.pop()
-    else:
-        totals = [chain_sum(mine[k], "dp") for k in range(count)]
-        small = chain_sum(small[0] + small_sent, "dp")
+    count_of = {"d": 2, "u": 2, "a": 2, "p": 1, "s": 1}
+    helds = {"d": held_d, "u": held_u, "s": small}
+    sent = {"d": over_y(held_d[1]), "u": over_y(held_u[1]), "s": over_y(small[1])}
+    chain = lax.axis_size("dp") == 4
+    middle = (lax.axis_index("dp") == 1) | (lax.axis_index("dp") == 2)
+    inward, cross, outward = chain_steps(lax.axis_size("dp")) if chain else (None, None, None)
+    tok = (attn_parts[-1][0],)
+    mine, got, totals = {}, {}, {}
+    for step in STEPS:
+        what, key = step.split()
+        if what == "out":
+            terms = {"a": attn_terms, "p": proj_terms}[key]
+            share = wgrad(following(terms, *tok), 1)
+            got[key] = near(share)
+            tok = (share,)
+        elif what == "held":
+            terms = {"a": attn_terms, "p": proj_terms}[key]
+            helds[key] = wgrad(following(terms, *tok), 0, got[key])
+            sent[key] = over_y(helds[key][1])
+            tok = (helds[key],)
+        elif what == "take":
+            held = after(helds[key], *tok)
+            part = held.shape[1] // count_of[key]
+            for i in range(count_of[key]):
+                k = key + str(i)
+                mine[k] = held[0, i * part:(i + 1) * part] + sent[key][i * part:(i + 1) * part]
+                tok = (mine[k],)
+                if chain and "in " + k not in STEPS:
+                    got[k] = lax.ppermute(mine[k], "dp", inward[0])
+                elif not chain:
+                    totals[k] = chain_sum(mine[k], "dp")
+        elif not chain:
+            continue
+        elif what == "in":
+            got[key] = lax.ppermute(after(mine[key], *tok), "dp", inward[0])
+        elif what == "fin":
+            totals[key] = jnp.where(middle, after(mine[key], *tok), got[key])
+            tok = (totals[key],)
+        else:
+            mine[key] = after(mine[key], *tok) + got[key]
+            tok = (mine[key],)
+            got[key] = lax.ppermute(mine[key], "dp", cross if what == "cross" else outward[0])
+    small = totals["s0"]
+    totals = [totals[k] for k in ("d0", "d1", "u0", "u1", "a0", "a1", "p0")]
     totals = [t.astype(F32) for t in totals]
     small = small[0]
     g_attn = jnp.concatenate(totals[4:6], axis=0).reshape(heads, -1, width).transpose(2, 0, 1)
@@ -593,7 +616,7 @@
         rowed[2],
         jnp.concatenate(totals[2:4], axis=0)[None],
         small[None, cols:cols + units],
-        jnp.concatenate(totals[0:2], axis=0)[None],
+        jnp.concatenate(totals[:2], axis=0)[None],
         rowed[3],
         rowed[4],
         rowed[5],

time: 462 us -> 390 us (0.84)
  waiting for transfers between devices: 154 us -> 76.3 us
  local copies, waits for them, and re-layouts: 34 us -> 26.2 us
  other arithmetic: 34.1 us -> 41.2 us
    ppermute x29 -> x26, waiting for transfers between devices: 81.6 us -> 29.9 us  [swapped(): return lax.ppermute(value, axis, [(i, i ^ bit) for i in range(count)])]
    ppermute x26, waiting for transfers between devices: 72 us -> 46.3 us  [the longest x16 15 us: body(): lax.ppermute(mine[key], 'dp', cross if what == 'cross' else outward[0])]
    ppermute x26, starting transfers between devices: 57.5 us -> 66.1 us  [the longest x3 22.3 us: body(): got[key] = lax.ppermute(after(mine[key], *tok), 'dp', inward[0])]
    unnamed x191 -> x195, local copies, waits for them, and re-layouts: 25 us -> 18.9 us
    add x24 -> x21, other arithmetic: 2.13 us -> 7.33 us  [the longest x5 4.12 us: body(): held[0, i * part:(i + 1) * part] + sent[key][i * part:(i + 1) * part]]
    ppermute x29 -> x26, starting transfers between devices: 22.4 us -> 17.7 us  [swapped(): return lax.ppermute(value, axis, [(i, i ^ bit) for i in range(count)])]
    pallas_call x8 -> x12, Pallas kernels: 26.1 us -> 24.6 us  [wgrad(): pl.pallas_call(functools.partial(wgrad_kernel, len(pairs)), grid=(2,), in...]
  transfers between devices with their start and end apart: 57 -> 54, of which waited for: 18 -> 22; matrix products, arithmetic and copies ran while one was open for 9% -> 12% of each run, Pallas kernels for 27% -> 36%
where the time goes in v3:
time: 390 us; the launch traced here: 384 us
  Pallas kernels  150 us (38%)
  starting transfers between devices  86.4 us (22%)
  waiting for transfers between devices  76.3 us (20%)
  other arithmetic  41.2 us (11%)
  local copies, waits for them, and re-layouts  26.2 us (7%)
    pallas_call x20, Pallas kernels, call(): pl.pallas_call(kernel, grid=(count,), in_specs=[spec(p) for p in ins], ou...  126 us
    ppermute x26, waiting for transfers between devices, swapped(): return lax.ppermute(value, axis, [(i, i ^ bit) for i in range(count)])  29.9 us
    pallas_call x12, Pallas kernels, wgrad(): pl.pallas_call(functools.partial(wgrad_kernel, len(pairs)), grid=(2,), in...  24.6 us
    ppermute x3, starting transfers between devices, body(): got[key] = lax.ppermute(after(mine[key], *tok), 'dp', inward[0])  22.3 us
    ppermute x5, starting transfers between devices, body(): got[k] = lax.ppermute(mine[k], 'dp', inward[0])  20 us
    unnamed x195, local copies, waits for them, and re-layouts  18.9 us
    ppermute x26, starting transfers between devices, swapped(): return lax.ppermute(value, axis, [(i, i ^ bit) for i in range(count)])  17.7 us
    ppermute x16, starting transfers between devices, body(): lax.ppermute(mine[key], 'dp', cross if what == 'cross' else outward[0])  16 us
  transfers between devices with their start and end apart: 54, of which 22 were waited for; matrix products, arithmetic and copies ran while one was open for 12% of the time, Pallas kernels for 36%

profile of v3, /device:TPU:0, one launch (start us, length us, event | category | flops | bytes accessed | tf_op | source)
XLA Modules:
  0.0 383.7 jit_solution(600300923288306172)
XLA Ops:
  26.7 7.6 %collective-permute-done.13 = bf16[384,768]{1,0:T(8,128)(2,1)} collective-permute-done((bf16[384,768]{1,0:T(8,128)(2,1)}, bf16[384,768]{1,0:T(8,128)(2,1)}, u32[]{:S(2)}, u32[]{:S(2)}) %collective-permute-start.13) | collective-permute-done | bytes 589856 | tf_op jit(solution)/shard_map/ppermute | solution.py:345
  39.1 7.0 %collective-permute-done.10 = bf16[384,768]{1,0:T(8,128)(2,1)S(1)} collective-permute-done((bf16[384,768]{1,0:T(8,128)(2,1)}, bf16[384,768]{1,0:T(8,128)(2,1)S(1)}, u32[]{:S(2)}, u32[]{:S(2)}) %collective-permute-start.10) | collective-permute-done | bytes 589856 | tf_op jit(solution)/shard_map/ppermute | solution.py:345
  78.0 4.5 %ffn_fwd.8 = bf16[416,768]{1,0:T(8,128)(2,1)S(1)} custom-call(bf16[416,768]{1,0:T(8,128)(2,1)S(1)} %get-tuple-element.112.x_ref, f32[416,768]{1,0:T(8,128)S(1)} %get-tuple-element.113.acc_in, f32[5,768]{1,0:T(8,128)S(1)} %concatenate.181.acc_in.vec_ref, f32[2,1,768]{2,1,0:T(1,128)S(1)} %broadcast_in_dim.48.ub_ref, ...), custom_call_target="tpu_custom_call" | custom-call | flops 1 | bytes 1 | tf_op jit(solution)/shard_map/ffn_fwd/pallas_call | solution.py:69
  95.7 4.5 %collective-permute-done.16 = bf16[416,768]{1,0:T(8,128)(2,1)S(1)} collective-permute-done((bf16[416,768]{1,0:T(8,128)(2,1)S(1)}, bf16[416,768]{1,0:T(8,128)(2,1)S(1)}, u32[]{:S(2)}, u32[]{:S(2)}) %collective-permute-start.16) | collective-permute-done | bytes 639008 | tf_op jit(solution)/shard_map/ppermute | solution.py:488
  100.2 4.4 %collective-permute-start.17 = (bf16[416,768]{1,0:T(8,128)(2,1)S(1)}, bf16[416,768]{1,0:T(8,128)(2,1)S(1)}, u32[]{:S(2)}, u32[]{:S(2)}) collective-permute-start(bf16[416,768]{1,0:T(8,128)(2,1)S(1)} %ffn_fwd.9), channel_id=1, source_target_pairs={{0,16},{1,17},{2,18},{3,19},{4,20},{5,21},{6,22},{7,23},{8,24},{9,... | collective-permute-start | bytes 1916936 | tf_op jit(solution)/shard_map/ppermute | solution.py:488
  105.9 7.0 %attn_fwd.10 = (f32[416,768]{1,0:T(8,128)S(1)}, bf16[4,416,576]{2,1,0:T(8,128)(2,1)S(1)}, bf16[4,416,192]{2,1,0:T(8,128)(2,1)S(1)}, bf16[4,2,3,208,208]{4,3,2,1,0:T(8,128)(2,1)S(1)}) custom-call(bf16[416,768]{1,0:T(8,128)(2,1)S(1)} %broadcast_select_fusion.3.x_ref.refs_1_, s32[2,208,1]{2,1,0:T(8,128)S(1)} %slice.279.ok_ref, f32[1,768]{1,0:T(1,128)S(1)} %copy-done.73, ...), custom_call_target="tpu_custom_call" | custom-call | flops 1 | bytes 1 | tf_op jit(solution)/shard_map/attn_fwd/pallas_call | solution.py:69
  112.9 9.6 %ffn_fwd.10 = (bf16[416,768]{1,0:T(8,128)(2,1)S(1)}, bf16[4,416,768]{2,1,0:T(8,128)(2,1)S(1)}, bf16[4,416,768]{2,1,0:T(8,128)(2,1)S(1)}, f32[416,768]{1,0:T(8,128)S(1)}, bf16[416,768]{1,0:T(8,128)(2,1)S(1)}) custom-call(f32[416,768]{1,0:T(8,128)S(1)} %get-tuple-element.122.x_ref.r1_ref, f32[5,768]{1,0:T(8,128)S(1)} %concatenate.181.acc_in.vec_ref, ...), custom_call_target="tpu_custom_call" | custom-call | flops 1 | bytes 1 | tf_op jit(solution)/shard_map/ffn_fwd/pallas_call | solution.py:69
  123.3 6.8 %ffn_bwd.4 = (f32[416,768]{1,0:T(8,128)S(1)}, bf16[416,768]{1,0:T(8,128)(2,1)S(1)}) custom-call(bf16[416,768]{1,0:T(8,128)(2,1)S(1)} %bitcast.101, f32[416,768]{1,0:T(8,128)S(1)} %get-tuple-element.124.r2_ref, f32[416,768]{1,0:T(8,128)S(1)} %get-tuple-element.122.x_ref.r1_ref, f32[5,768]{1,0:T(8,128)S(1)} %concatenate.181.acc_in.vec_ref, ...), custom_call_target="tpu_custom_call" | custom-call | flops 1 | bytes 1 | tf_op jit(solution)/shard_map/ffn_bwd/pallas_call | solution.py:69
  130.2 8.5 %attn_bwd.4 = bf16[416,768]{1,0:T(8,128)(2,1)} custom-call(bf16[416,768]{1,0:T(8,128)(2,1)S(1)} %get-tuple-element.126.dg_ref, f32[416,768]{1,0:T(8,128)S(1)} %get-tuple-element.127.dr1_ref, bf16[4,416,576]{2,1,0:T(8,128)(2,1)S(1)} %get-tuple-element.128.p_ref, bf16[4,2,3,208,208]{4,3,2,1,0:T(8,128)(2,1)S(1)} %get-tuple-element.129.a_ref, ...), custom_call_target="tpu_custom_call" | custom-call | flops 1 | bytes 1 | tf_op jit(solution)/shard_map/attn_bwd/pallas_call | solution.py:69
  140.1 7.1 %attn_fwd.11 = (f32[416,768]{1,0:T(8,128)S(1)}, bf16[4,416,576]{2,1,0:T(8,128)(2,1)S(1)}, bf16[4,416,192]{2,1,0:T(8,128)(2,1)S(1)}, bf16[4,2,3,208,208]{4,3,2,1,0:T(8,128)(2,1)S(1)}) custom-call(bf16[416,768]{1,0:T(8,128)(2,1)S(1)} %broadcast_select_fusion.2.x_ref.refs_3_, s32[2,208,1]{2,1,0:T(8,128)S(1)} %slice.278.ok_ref, f32[1,768]{1,0:T(1,128)S(1)} %copy-done.73, ...), custom_call_target="tpu_custom_call" | custom-call | flops 1 | bytes 1 | tf_op jit(solution)/shard_map/attn_fwd/pallas_call | solution.py:69
  148.2 9.6 %ffn_fwd.11 = (bf16[416,768]{1,0:T(8,128)(2,1)S(1)}, bf16[4,416,768]{2,1,0:T(8,128)(2,1)S(1)}, bf16[4,416,768]{2,1,0:T(8,128)(2,1)S(1)}, f32[416,768]{1,0:T(8,128)S(1)}, bf16[416,768]{1,0:T(8,128)(2,1)S(1)}) custom-call(f32[416,768]{1,0:T(8,128)S(1)} %get-tuple-element.132.x_ref.r1_ref, f32[5,768]{1,0:T(8,128)S(1)} %concatenate.181.acc_in.vec_ref, ...), custom_call_target="tpu_custom_call" | custom-call | flops 1 | bytes 1 | tf_op jit(solution)/shard_map/ffn_fwd/pallas_call | solution.py:69
  157.9 6.8 %ffn_bwd.5 = (f32[416,768]{1,0:T(8,128)S(1)}, bf16[416,768]{1,0:T(8,128)(2,1)S(1)}) custom-call(bf16[416,768]{1,0:T(8,128)(2,1)S(1)} %bitcast.98, f32[416,768]{1,0:T(8,128)S(1)} %get-tuple-element.134.r2_ref, f32[416,768]{1,0:T(8,128)S(1)} %get-tuple-element.132.x_ref.r1_ref, f32[5,768]{1,0:T(8,128)S(1)} %concatenate.181.acc_in.vec_ref, ...), custom_call_target="tpu_custom_call" | custom-call | flops 1 | bytes 1 | tf_op jit(solution)/shard_map/ffn_bwd/pallas_call | solution.py:69
  164.8 8.6 %attn_bwd.5 = bf16[416,768]{1,0:T(8,128)(2,1)} custom-call(bf16[416,768]{1,0:T(8,128)(2,1)S(1)} %get-tuple-element.136.dg_ref, f32[416,768]{1,0:T(8,128)S(1)} %get-tuple-element.137.dr1_ref, bf16[4,416,576]{2,1,0:T(8,128)(2,1)S(1)} %copy-done.38, bf16[4,2,3,208,208]{4,3,2,1,0:T(8,128)(2,1)S(1)} %copy-done.23, ...), custom_call_target="tpu_custom_call" | custom-call | flops 1 | bytes 1 | tf_op jit(solution)/shard_map/attn_bwd/pallas_call | solution.py:69
  182.6 7.6 %ffn_bwd.6 = (f32[416,768]{1,0:T(8,128)S(1)}, bf16[416,768]{1,0:T(8,128)(2,1)S(1)}, bf16[416,768]{1,0:T(8,128)(2,1)S(1)}, bf16[4,416,768]{2,1,0:T(8,128)(2,1)S(1...) custom-call(bf16[416,768]{1,0:T(8,128)(2,1)S(1)} %broadcast_select_fusion.1.dy_ref, f32[416,768]{1,0:T(8,128)S(1)} %copy-done.48, ...), custom_call_target="tpu_custom_call" | custom-call | flops 1 | bytes 1 | tf_op jit(solution)/shard_map/ffn_bwd/pallas_call | solution.py:69
  198.8 7.3 %ffn_bwd.7 = (f32[416,768]{1,0:T(8,128)S(1)}, bf16[416,768]{1,0:T(8,128)(2,1)S(1)}, bf16[416,768]{1,0:T(8,128)(2,1)S(1)}, bf16[4,416,768]{2,1,0:T(8,128)(2,1)S(1...) custom-call(bf16[416,768]{1,0:T(8,128)(2,1)S(1)} %broadcast_select_fusion.dy_ref, f32[416,768]{1,0:T(8,128)S(1)} %copy-done.50, ...), custom_call_target="tpu_custom_call" | custom-call | flops 1 | bytes 1 | tf_op jit(solution)/shard_map/ffn_bwd/pallas_call | solution.py:69
  221.3 7.9 %attn_bwd.6 = (f32[416,768]{1,0:T(8,128)S(1)}, bf16[4,416,576]{2,1,0:T(8,128)(2,1)S(1)}, f32[4,1,576]{2,1,0:T(1,128)S(1)}) custom-call(bf16[416,768]{1,0:T(8,128)(2,1)S(1)} %copy-done.44, f32[416,768]{1,0:T(8,128)S(1)} %copy-done.66, bf16[4,416,576]{2,1,0:T(8,128)(2,1)S(1)} %copy-done.36, bf16[4,2,3,208,208]{4,3,2,1,0:T(8,128)(2,1)S(1)} %copy-done.21, ...), custom_call_target="tpu_custom_call" | custom-call | flops 1 | bytes 1 | tf_op jit(solution)/shard_map/attn_bwd/pallas_call | solution.py:69
  229.3 7.7 %attn_bwd.7 = (f32[416,768]{1,0:T(8,128)S(1)}, bf16[4,416,576]{2,1,0:T(8,128)(2,1)S(1)}, f32[4,1,576]{2,1,0:T(1,128)S(1)}) custom-call(bf16[416,768]{1,0:T(8,128)(2,1)S(1)} %get-tuple-element.158.dg_ref.refs_3_, f32[416,768]{1,0:T(8,128)S(1)} %copy-done.68, bf16[4,416,576]{2,1,0:T(8,128)(2,1)S(1)} %copy-done.39, bf16[4,2,3,208,208]{4,3,2,1,0:T(8,128)(2,1)S(1)} %copy-done.24, ...), custom_call_target="tpu_custom_call" | custom-call | flops 1 | bytes 1 | tf_op jit(solution)/shard_map/attn_bwd/pallas_call | solution.py:69
  271.0 11.4 %collective-permute-done.26 = bf16[384,768]{1,0:T(8,128)(2,1)S(1)} collective-permute-done((bf16[384,768]{1,0:T(8,128)(2,1)S(1)}, bf16[384,768]{1,0:T(8,128)(2,1)S(1)}, u32[]{:S(2)}, u32[]{:S(2)}) %collective-permute-start.26) | collective-permute-done | bytes 589856 | tf_op jit(solution)/shard_map/ppermute | solution.py:592
  291.4 8.2 %collective-permute-done.29 = bf16[384,768]{1,0:T(8,128)(2,1)S(1)} collective-permute-done((bf16[384,768]{1,0:T(8,128)(2,1)S(1)}, bf16[384,768]{1,0:T(8,128)(2,1)S(1)}, u32[]{:S(2)}, u32[]{:S(2)}) %collective-permute-start.29) | collective-permute-done | bytes 589856 | tf_op jit(solution)/shard_map/ppermute | solution.py:586
  299.7 4.4 %collective-permute-start.33 = (bf16[384,768]{1,0:T(8,128)(2,1)S(1)}, bf16[384,768]{1,0:T(8,128)(2,1)S(1)}, u32[]{:S(2)}, u32[]{:S(2)}) collective-permute-start(bf16[384,768]{1,0:T(8,128)(2,1)S(1)} %get-tuple-element.179), channel_id=1, source_target_pairs={{0,4},{12,8},{1,5},{13,9},{2,6},{14,10},{3,7},{15,11},{16,20},{28,... | collective-permute-start | bytes 1769480 | tf_op jit(solution)/shard_map/ppermute | solution.py:592
  326.2 14.9 %collective-permute-start.41 = (bf16[288,768]{1,0:T(8,128)(2,1)S(1)}, bf16[288,768]{1,0:T(8,128)(2,1)S(1)}, u32[]{:S(2)}, u32[]{:S(2)}) collective-permute-start(bf16[288,768]{1,0:T(8,128)(2,1)S(1)} %get-tuple-element.193), channel_id=1, source_target_pairs={{0,4},{12,8},{1,5},{13,9},{2,6},{14,10},{3,7},{15,11},{16,20},{28,... | collective-permute-start | bytes 1327112 | tf_op jit(solution)/shard_map/ppermute | solution.py:592
  342.7 4.9 %collective-permute-start.45 = (bf16[192,768]{1,0:T(8,128)(2,1)S(1)}, bf16[192,768]{1,0:T(8,128)(2,1)S(1)}, u32[]{:S(2)}, u32[]{:S(2)}) collective-permute-start(bf16[192,768]{1,0:T(8,128)(2,1)S(1)} %bitcast_add_fusion), channel_id=1, source_target_pairs={{0,4},{12,8},{1,5},{13,9},{2,6},{14,10},{3,7},{15,11},{16,20},{28,... | collective-permute-start | bytes 884744 | tf_op jit(solution)/shard_map/ppermute | solution.py:586
  349.8 4.4 %collective-permute-start.44 = (f32[1,5952]{1,0:T(1,128)S(1)}, f32[1,5952]{1,0:T(1,128)S(1)}, u32[]{:S(2)}, u32[]{:S(2)}) collective-permute-start(f32[1,5952]{1,0:T(1,128)S(1)} %bitcast_add_fusion.1), channel_id=1, source_target_pairs={{0,4},{12,8},{1,5},{13,9},{2,6},{14,10},{3,7},{15,11},{16,20},{28,... | collective-permute-start | bytes 71432 | tf_op jit(solution)/shard_map/ppermute | solution.py:586
  370.7 6.8 %collective-permute-done.51 = bf16[288,768]{1,0:T(8,128)(2,1)S(1)} collective-permute-done((bf16[288,768]{1,0:T(8,128)(2,1)S(1)}, bf16[288,768]{1,0:T(8,128)(2,1)S(1)}, u32[]{:S(2)}, u32[]{:S(2)}) %collective-permute-start.51) | collective-permute-done | bytes 442400 | tf_op jit(solution)/shard_map/ppermute | solution.py:599
  (431 shorter events, 203.0 us)
Async XLA Ops:
  0.7 23.0 %collective-permute-start.2 = (bf16[192,768]{1,0:T(8,128)(2,1)}, bf16[192,768]{1,0:T(8,128)(2,1)}, u32[]{:S(2)}, u32[]{:S(2)}) collective-permute-start(bf16[192,768]{1,0:T(8,128)(2,1)} %bitcast.123), channel_id=1, source_target_pairs={{0,1},{1,0},{2,3},{3,2},{4,5},{5,4},{6,7},{7,6},{8,9},{9,8},{10,11... | collective-permute-start | bytes 884744 | tf_op jit(solution)/shard_map/ppermute | solution.py:345
  9.1 29.8 %collective-permute-start.1 = (bf16[608,768]{1,0:T(8,128)(2,1)}, bf16[608,768]{1,0:T(8,128)(2,1)}, u32[]{:S(2)}, u32[]{:S(2)}) collective-permute-start(bf16[608,768]{1,0:T(8,128)(2,1)} %get-tuple-element.223), channel_id=1, source_target_pairs={{0,1},{1,0},{2,3},{3,2},{4,5},{5,4},{6,7},{7,6},{8,9},{9,8},{10,11... | collective-permute-start | bytes 2801672 | tf_op jit(solution)/shard_map/ppermute | solution.py:345
  15.0 19.3 %collective-permute-start.13 = (bf16[384,768]{1,0:T(8,128)(2,1)}, bf16[384,768]{1,0:T(8,128)(2,1)}, u32[]{:S(2)}, u32[]{:S(2)}) collective-permute-start(bf16[384,768]{1,0:T(8,128)(2,1)} %select_bitcast_fusion), channel_id=1, source_target_pairs={{0,2},{1,3},{2,0},{3,1},{4,6},{5,7},{6,4},{7,5},{8,10},{9,11},{10,... | collective-permute-start | bytes 1769480 | tf_op jit(solution)/shard_map/ppermute | solution.py:345
  23.6 22.4 %collective-permute-start.10 = (bf16[384,768]{1,0:T(8,128)(2,1)}, bf16[384,768]{1,0:T(8,128)(2,1)S(1)}, u32[]{:S(2)}, u32[]{:S(2)}) collective-permute-start(bf16[384,768]{1,0:T(8,128)(2,1)} %select_bitcast_fusion.1), channel_id=1, source_target_pairs={{0,2},{1,3},{2,0},{3,1},{4,6},{5,7},{6,4},{7,5},{8,10},{9,11},{10,... | collective-permute-start | bytes 1769480 | tf_op jit(solution)/shard_map/ppermute | solution.py:345
  26.6 36.9 %collective-permute-start.9 = (bf16[768,768]{1,0:T(8,128)(2,1)}, bf16[768,768]{1,0:T(8,128)(2,1)S(1)}, u32[]{:S(2)}, u32[]{:S(2)}) collective-permute-start(bf16[768,768]{1,0:T(8,128)(2,1)} %bitcast.111), channel_id=1, source_target_pairs={{0,1},{1,0},{2,3},{3,2},{4,5},{5,4},{6,7},{7,6},{8,9},{9,8},{10,11... | collective-permute-start | bytes 3538952 | tf_op jit(solution)/shard_map/ppermute | solution.py:345
  34.3 29.4 %collective-permute-start = (bf16[768,768]{1,0:T(8,128)(2,1)S(1)}, bf16[768,768]{1,0:T(8,128)(2,1)S(1)}, u32[]{:S(2)}, u32[]{:S(2)}) collective-permute-start(bf16[768,768]{1,0:T(8,128)(2,1)S(1)} %bitcast.112), channel_id=1, source_target_pairs={{0,1},{1,0},{2,3},{3,2},{4,5},{5,4},{6,7},{7,6},{8,9},{9,8},{10,11... | collective-permute-start | bytes 3538952 | tf_op jit(solution)/shard_map/ppermute | solution.py:345
  38.9 25.1 %collective-permute-start.5 = (bf16[608,768]{1,0:T(8,128)(2,1)S(1)}, bf16[608,768]{1,0:T(8,128)(2,1)S(1)}, u32[]{:S(2)}, u32[]{:S(2)}) collective-permute-start(bf16[608,768]{1,0:T(8,128)(2,1)S(1)} %maximum_select_fusion.5), channel_id=1, source_target_pairs={{0,1},{1,0},{2,3},{3,2},{4,5},{5,4},{6,7},{7,6},{8,9},{9,8},{10,11... | collective-permute-start | bytes 2801672 | tf_op jit(solution)/shard_map/ppermute | solution.py:345
  52.4 25.2 %collective-permute-start.15 = (bf16[768,768]{1,0:T(8,128)(2,1)S(1)}, bf16[768,768]{1,0:T(8,128)(2,1)S(1)}, u32[]{:S(2)}, u32[]{:S(2)}) collective-permute-start(bf16[768,768]{1,0:T(8,128)(2,1)S(1)} %maximum_select_fusion.3), channel_id=1, source_target_pairs={{0,1},{1,0},{2,3},{3,2},{4,5},{5,4},{6,7},{7,6},{8,9},{9,8},{10,11... | collective-permute-start | bytes 3538952 | tf_op jit(solution)/shard_map/ppermute | solution.py:345
  100.2 39.8 %collective-permute-start.17 = (bf16[416,768]{1,0:T(8,128)(2,1)S(1)}, bf16[416,768]{1,0:T(8,128)(2,1)S(1)}, u32[]{:S(2)}, u32[]{:S(2)}) collective-permute-start(bf16[416,768]{1,0:T(8,128)(2,1)S(1)} %ffn_fwd.9), channel_id=1, source_target_pairs={{0,16},{1,17},{2,18},{3,19},{4,20},{5,21},{6,22},{7,23},{8,24},{9,... | collective-permute-start | bytes 1916936 | tf_op jit(solution)/shard_map/ppermute | solution.py:488
  138.7 36.0 %collective-permute-start.18 = (bf16[416,768]{1,0:T(8,128)(2,1)}, bf16[416,768]{1,0:T(8,128)(2,1)}, u32[]{:S(2)}, u32[]{:S(2)}) collective-permute-start(bf16[416,768]{1,0:T(8,128)(2,1)} %attn_bwd.4), channel_id=1, source_target_pairs={{16,0},{17,1},{18,2},{19,3},{20,4},{21,5},{22,6},{23,7},{24,8},{25... | collective-permute-start | bytes 1916936 | tf_op jit(solution)/shard_map/ppermute | solution.py:506
  173.4 23.8 %collective-permute-start.19 = (bf16[416,768]{1,0:T(8,128)(2,1)}, bf16[416,768]{1,0:T(8,128)(2,1)}, u32[]{:S(2)}, u32[]{:S(2)}) collective-permute-start(bf16[416,768]{1,0:T(8,128)(2,1)} %attn_bwd.5), channel_id=1, source_target_pairs={{16,0},{17,1},{18,2},{19,3},{20,4},{21,5},{22,6},{23,7},{24,8},{25... | collective-permute-start | bytes 1916936 | tf_op jit(solution)/shard_map/ppermute | solution.py:506
  216.9 28.3 %collective-permute-start.22 = (bf16[768,768]{1,0:T(8,128)(2,1)}, bf16[768,768]{1,0:T(8,128)(2,1)}, u32[]{:S(2)}, u32[]{:S(2)}) collective-permute-start(bf16[768,768]{1,0:T(8,128)(2,1)} %slice_bitcast_fusion.1), channel_id=1, source_target_pairs={{0,2},{1,3},{2,0},{3,1},{4,6},{5,7},{6,4},{7,5},{8,10},{9,11},{10,... | collective-permute-start | bytes 3538952 | tf_op jit(solution)/shard_map/ppermute | solution.py:345
  244.9 18.7 %collective-permute-start.24 = (bf16[2,192,768]{2,1,0:T(8,128)(2,1)}, bf16[2,192,768]{2,1,0:T(8,128)(2,1)}, u32[]{:S(2)}, u32[]{:S(2)}) collective-permute-start(bf16[2,192,768]{2,1,0:T(8,128)(2,1)} %wgrad.21), channel_id=1, source_target_pairs={{0,1},{1,0},{2,3},{3,2},{4,5},{5,4},{6,7},{7,6},{8,9},{9,8},{10,11... | collective-permute-start | bytes 1769480 | tf_op jit(solution)/shard_map/ppermute | solution.py:345
  247.7 18.0 %collective-permute-start.25 = (bf16[384,768]{1,0:T(8,128)(2,1)}, bf16[384,768]{1,0:T(8,128)(2,1)}, u32[]{:S(2)}, u32[]{:S(2)}) collective-permute-start(bf16[384,768]{1,0:T(8,128)(2,1)} %get-tuple-element.170), channel_id=1, source_target_pairs={{0,4},{12,8},{1,5},{13,9},{2,6},{14,10},{3,7},{15,11},{16,20},{28,... | collective-permute-start | bytes 1769480 | tf_op jit(solution)/shard_map/ppermute | solution.py:586
  255.5 28.1 %collective-permute-start.27 = (bf16[768,768]{1,0:T(8,128)(2,1)}, bf16[768,768]{1,0:T(8,128)(2,1)}, u32[]{:S(2)}, u32[]{:S(2)}) collective-permute-start(bf16[768,768]{1,0:T(8,128)(2,1)} %slice_bitcast_fusion), channel_id=1, source_target_pairs={{0,2},{1,3},{2,0},{3,1},{4,6},{5,7},{6,4},{7,5},{8,10},{9,11},{10,... | collective-permute-start | bytes 3538952 | tf_op jit(solution)/shard_map/ppermute | solution.py:345
  270.3 19.6 %collective-permute-start.28 = (bf16[384,768]{1,0:T(8,128)(2,1)S(1)}, bf16[384,768]{1,0:T(8,128)(2,1)S(1)}, u32[]{:S(2)}, u32[]{:S(2)}) collective-permute-start(bf16[384,768]{1,0:T(8,128)(2,1)S(1)} %add.107), channel_id=1, source_target_pairs={{4,8},{8,4},{5,9},{9,5},{6,10},{10,6},{7,11},{11,7},{20,24},{24,20... | collective-permute-start | bytes 1769480 | tf_op jit(solution)/shard_map/ppermute | solution.py:599
  288.6 22.1 %collective-permute-start.32 = (bf16[576,768]{1,0:T(8,128)(2,1)S(1)}, bf16[576,768]{1,0:T(8,128)(2,1)S(1)}, u32[]{:S(2)}, u32[]{:S(2)}) collective-permute-start(bf16[576,768]{1,0:T(8,128)(2,1)S(1)} %slice_bitcast_fusion.2), channel_id=1, source_target_pairs={{0,2},{1,3},{2,0},{3,1},{4,6},{5,7},{6,4},{7,5},{8,10},{9,11},{10,... | collective-permute-start | bytes 2654216 | tf_op jit(solution)/shard_map/ppermute | solution.py:345
  304.4 20.4 %collective-permute-start.37 = (bf16[384,768]{1,0:T(8,128)(2,1)S(1)}, bf16[384,768]{1,0:T(8,128)(2,1)S(1)}, u32[]{:S(2)}, u32[]{:S(2)}) collective-permute-start(bf16[384,768]{1,0:T(8,128)(2,1)S(1)} %add.113), channel_id=1, source_target_pairs={{4,0},{8,12},{5,1},{9,13},{6,2},{10,14},{7,3},{11,15},{20,16},{24,... | collective-permute-start | bytes 1769480 | tf_op jit(solution)/shard_map/ppermute | solution.py:599
  317.4 23.9 %collective-permute-start.39 = (f32[1,5952]{1,0:T(1,128)S(1)}, f32[1,5952]{1,0:T(1,128)S(1)}, u32[]{:S(2)}, u32[]{:S(2)}) collective-permute-start(f32[1,5952]{1,0:T(1,128)S(1)} %slice_bitcast_fusion.4), channel_id=1, source_target_pairs={{0,2},{1,3},{2,0},{3,1},{4,6},{5,7},{6,4},{7,5},{8,10},{9,11},{10,... | collective-permute-start | bytes 71432 | tf_op jit(solution)/shard_map/ppermute | solution.py:345
  317.5 25.1 %collective-permute-start.40 = (bf16[192,768]{1,0:T(8,128)(2,1)S(1)}, bf16[192,768]{1,0:T(8,128)(2,1)S(1)}, u32[]{:S(2)}, u32[]{:S(2)}) collective-permute-start(bf16[192,768]{1,0:T(8,128)(2,1)S(1)} %slice_bitcast_fusion.3), channel_id=1, source_target_pairs={{0,2},{1,3},{2,0},{3,1},{4,6},{5,7},{6,4},{7,5},{8,10},{9,11},{10,... | collective-permute-start | bytes 884744 | tf_op jit(solution)/shard_map/ppermute | solution.py:345
  324.0 30.3 %collective-permute-start.42 = (bf16[288,768]{1,0:T(8,128)(2,1)S(1)}, bf16[288,768]{1,0:T(8,128)(2,1)S(1)}, u32[]{:S(2)}, u32[]{:S(2)}) collective-permute-start(bf16[288,768]{1,0:T(8,128)(2,1)S(1)} %add.118), channel_id=1, source_target_pairs={{4,8},{8,4},{5,9},{9,5},{6,10},{10,6},{7,11},{11,7},{20,24},{24,20... | collective-permute-start | bytes 1327112 | tf_op jit(solution)/shard_map/ppermute | solution.py:599
  324.9 30.8 %collective-permute-start.43 = (bf16[384,768]{1,0:T(8,128)(2,1)S(1)}, bf16[384,768]{1,0:T(8,128)(2,1)S(1)}, u32[]{:S(2)}, u32[]{:S(2)}) collective-permute-start(bf16[384,768]{1,0:T(8,128)(2,1)S(1)} %add.117), channel_id=1, source_target_pairs={{4,0},{8,12},{5,1},{9,13},{6,2},{10,14},{7,3},{11,15},{20,16},{24,... | collective-permute-start | bytes 1769480 | tf_op jit(solution)/shard_map/ppermute | solution.py:599
  326.2 23.5 %collective-permute-start.41 = (bf16[288,768]{1,0:T(8,128)(2,1)S(1)}, bf16[288,768]{1,0:T(8,128)(2,1)S(1)}, u32[]{:S(2)}, u32[]{:S(2)}) collective-permute-start(bf16[288,768]{1,0:T(8,128)(2,1)S(1)} %get-tuple-element.193), channel_id=1, source_target_pairs={{0,4},{12,8},{1,5},{13,9},{2,6},{14,10},{3,7},{15,11},{16,20},{28,... | collective-permute-start | bytes 1327112 | tf_op jit(solution)/shard_map/ppermute | solution.py:592
  341.3 18.2 %collective-permute-start.46 = (bf16[384,768]{1,0:T(8,128)(2,1)S(1)}, bf16[384,768]{1,0:T(8,128)(2,1)S(1)}, u32[]{:S(2)}, u32[]{:S(2)}) collective-permute-start(bf16[384,768]{1,0:T(8,128)(2,1)S(1)} %add.123), channel_id=1, source_target_pairs={{4,0},{8,12},{5,1},{9,13},{6,2},{10,14},{7,3},{11,15},{20,16},{24,... | collective-permute-start | bytes 1769480 | tf_op jit(solution)/shard_map/ppermute | solution.py:599
  (126 other events, 1212.7 us)

commit v4 on v3

--- a/solution.py
+++ b/solution.py
@@ -152,8 +152,9 @@
 
     hb = hb_ref[...]
     units = up_ref.shape[2]
-    step = units // PARTS
-    us = [dot(hb, up_ref[0, :, j * step:(j + 1) * step]) for j in range(PARTS)]
+    pieces = 2
+    step = units // pieces
+    us = [dot(hb, up_ref[0, :, j * step:(j + 1) * step]) for j in range(pieces)]
     es, slopes = [], []
     for j, u in enumerate(us):
         act, slope = gelu_parts(u + ub_ref[0, :, j * step:(j + 1) * step], save)
@@ -485,7 +486,7 @@
         tok = firsts[-1:]
         acc, hb = halves[g]
         firsts.append(ffn_fwd(hb, after(acc, *tok), vec, ub_1, up_1, down_1, False, False, True)[0])
-        hops.append(lax.ppermute(after(firsts[g], *hops[-1:]), "section", [(0, 1)]))
+        hops.append(swapped(after(firsts[g], *hops[-1:]), "section", 1))
 
     tok = firsts[-1]
     attn_w = jnp.concatenate([after(attn_0, tok), attn_1])
@@ -503,7 +504,7 @@
         y, e, slope, r2, hb = ffn_fwd(r1, vec, vec, ub, up_w, down_w, True, True, True)
         dr1, dg = ffn_bwd(cots[g], r2, r1, vec, slope, up_w, down_w, False)
         (d_first,) = attn_bwd(dg, dr1, p, a, attn_w, proj_w, False)
-        backs.append(lax.ppermute(d_first, "section", [(1, 0)]))
+        backs.append(swapped(d_first, "section", 1))
         kept.append((x, r1, p, c, a, e, slope, r2, hb))
         outputs.append(y)
         tok = (d_first,)

time: 390 us -> 382 us (0.979)
  starting transfers between devices: 86.4 us -> 80.4 us
    ppermute x4 -> x0, starting transfers between devices: 10.4 us -> none  [the longest x2 7.87 us: body(): hops.append(lax.ppermute(after(firsts[g], *hops[-1:]), 'section', [(0, 1)]))]
    ppermute x26 -> x30, waiting for transfers between devices: 29.9 us -> 36.5 us  [swapped(): return lax.ppermute(value, axis, [(i, i ^ bit) for i in range(count)])]
    ppermute x26 -> x30, starting transfers between devices: 17.7 us -> 22.9 us  [swapped(): return lax.ppermute(value, axis, [(i, i ^ bit) for i in range(count)])]
    ppermute x4 -> x0, waiting for transfers between devices: 4.51 us -> none  [the longest x2 4.5 us: body(): hops.append(lax.ppermute(after(firsts[g], *hops[-1:]), 'section', [(0, 1)]))]
where the time goes in v4:
time: 382 us; the launch traced here: 377 us
  Pallas kernels  149 us (39%)
  starting transfers between devices  80.4 us (21%)
  waiting for transfers between devices  78.6 us (21%)
  other arithmetic  40.6 us (11%)
  local copies, waits for them, and re-layouts  26.3 us (7%)
    pallas_call x20, Pallas kernels, call(): pl.pallas_call(kernel, grid=(count,), in_specs=[spec(p) for p in ins], ou...  124 us
    ppermute x30, waiting for transfers between devices, swapped(): return lax.ppermute(value, axis, [(i, i ^ bit) for i in range(count)])  36.5 us
    pallas_call x12, Pallas kernels, wgrad(): pl.pallas_call(functools.partial(wgrad_kernel, len(pairs)), grid=(2,), in...  24.6 us
    ppermute x30, starting transfers between devices, swapped(): return lax.ppermute(value, axis, [(i, i ^ bit) for i in range(count)])  22.9 us
    ppermute x3, starting transfers between devices, body(): got[key] = lax.ppermute(after(mine[key], *tok), 'dp', inward[0])  22.2 us
    ppermute x5, starting transfers between devices, body(): got[k] = lax.ppermute(mine[k], 'dp', inward[0])  19.3 us
    unnamed x195, local copies, waits for them, and re-layouts  19 us
    ppermute x16, starting transfers between devices, body(): lax.ppermute(mine[key], 'dp', cross if what == 'cross' else outward[0])  16 us
  transfers between devices with their start and end apart: 54, of which 22 were waited for; matrix products, arithmetic and copies ran while one was open for 12% of the time, Pallas kernels for 36%

profile of v4, /device:TPU:0, one launch (start us, length us, event | category | flops | bytes accessed | tf_op | source)
XLA Modules:
  0.0 377.5 jit_solution(15060804901276795614)
XLA Ops:
  26.7 7.6 %collective-permute-done.13 = bf16[384,768]{1,0:T(8,128)(2,1)} collective-permute-done((bf16[384,768]{1,0:T(8,128)(2,1)}, bf16[384,768]{1,0:T(8,128)(2,1)}, u32[]{:S(2)}, u32[]{:S(2)}) %collective-permute-start.13) | collective-permute-done | bytes 589856 | tf_op jit(solution)/shard_map/ppermute | solution.py:346
  39.1 7.0 %collective-permute-done.10 = bf16[384,768]{1,0:T(8,128)(2,1)S(1)} collective-permute-done((bf16[384,768]{1,0:T(8,128)(2,1)}, bf16[384,768]{1,0:T(8,128)(2,1)S(1)}, u32[]{:S(2)}, u32[]{:S(2)}) %collective-permute-start.10) | collective-permute-done | bytes 589856 | tf_op jit(solution)/shard_map/ppermute | solution.py:346
  92.8 6.0 %collective-permute-done.16 = bf16[416,768]{1,0:T(8,128)(2,1)S(1)} collective-permute-done((bf16[416,768]{1,0:T(8,128)(2,1)S(1)}, bf16[416,768]{1,0:T(8,128)(2,1)S(1)}, u32[]{:S(2)}, u32[]{:S(2)}) %collective-permute-start.16) | collective-permute-done | bytes 639008 | tf_op jit(solution)/shard_map/ppermute | solution.py:346
  101.1 7.0 %attn_fwd.10 = (f32[416,768]{1,0:T(8,128)S(1)}, bf16[4,416,576]{2,1,0:T(8,128)(2,1)S(1)}, bf16[4,416,192]{2,1,0:T(8,128)(2,1)S(1)}, bf16[4,2,3,208,208]{4,3,2,1,0:T(8,128)(2,1)S(1)}) custom-call(bf16[416,768]{1,0:T(8,128)(2,1)S(1)} %broadcast_select_fusion.3.x_ref.refs_1_, s32[2,208,1]{2,1,0:T(8,128)S(1)} %slice.279.ok_ref, f32[1,768]{1,0:T(1,128)S(1)} %copy-done.73, ...), custom_call_target="tpu_custom_call" | custom-call | flops 1 | bytes 1 | tf_op jit(solution)/shard_map/attn_fwd/pallas_call | solution.py:69
  108.1 9.5 %ffn_fwd.10 = (bf16[416,768]{1,0:T(8,128)(2,1)S(1)}, bf16[4,416,768]{2,1,0:T(8,128)(2,1)S(1)}, bf16[4,416,768]{2,1,0:T(8,128)(2,1)S(1)}, f32[416,768]{1,0:T(8,128)S(1)}, bf16[416,768]{1,0:T(8,128)(2,1)S(1)}) custom-call(f32[416,768]{1,0:T(8,128)S(1)} %get-tuple-element.122.x_ref.r1_ref, f32[5,768]{1,0:T(8,128)S(1)} %concatenate.181.acc_in.vec_ref, ...), custom_call_target="tpu_custom_call" | custom-call | flops 1 | bytes 1 | tf_op jit(solution)/shard_map/ffn_fwd/pallas_call | solution.py:69
  118.5 6.8 %ffn_bwd.4 = (f32[416,768]{1,0:T(8,128)S(1)}, bf16[416,768]{1,0:T(8,128)(2,1)S(1)}) custom-call(bf16[416,768]{1,0:T(8,128)(2,1)S(1)} %bitcast.101, f32[416,768]{1,0:T(8,128)S(1)} %get-tuple-element.124.r2_ref, f32[416,768]{1,0:T(8,128)S(1)} %get-tuple-element.122.x_ref.r1_ref, f32[5,768]{1,0:T(8,128)S(1)} %concatenate.181.acc_in.vec_ref, ...), custom_call_target="tpu_custom_call" | custom-call | flops 1 | bytes 1 | tf_op jit(solution)/shard_map/ffn_bwd/pallas_call | solution.py:69
  125.4 8.5 %attn_bwd.4 = bf16[416,768]{1,0:T(8,128)(2,1)} custom-call(bf16[416,768]{1,0:T(8,128)(2,1)S(1)} %get-tuple-element.126.dg_ref, f32[416,768]{1,0:T(8,128)S(1)} %get-tuple-element.127.dr1_ref, bf16[4,416,576]{2,1,0:T(8,128)(2,1)S(1)} %get-tuple-element.128.p_ref, bf16[4,2,3,208,208]{4,3,2,1,0:T(8,128)(2,1)S(1)} %get-tuple-element.129.a_ref, ...), custom_call_target="tpu_custom_call" | custom-call | flops 1 | bytes 1 | tf_op jit(solution)/shard_map/attn_bwd/pallas_call | solution.py:69
  134.6 7.0 %attn_fwd.11 = (f32[416,768]{1,0:T(8,128)S(1)}, bf16[4,416,576]{2,1,0:T(8,128)(2,1)S(1)}, bf16[4,416,192]{2,1,0:T(8,128)(2,1)S(1)}, bf16[4,2,3,208,208]{4,3,2,1,0:T(8,128)(2,1)S(1)}) custom-call(bf16[416,768]{1,0:T(8,128)(2,1)S(1)} %broadcast_select_fusion.2.x_ref.refs_3_, s32[2,208,1]{2,1,0:T(8,128)S(1)} %slice.278.ok_ref, f32[1,768]{1,0:T(1,128)S(1)} %copy-done.73, ...), custom_call_target="tpu_custom_call" | custom-call | flops 1 | bytes 1 | tf_op jit(solution)/shard_map/attn_fwd/pallas_call | solution.py:69
  142.5 9.1 %ffn_fwd.11 = (bf16[416,768]{1,0:T(8,128)(2,1)S(1)}, bf16[4,416,768]{2,1,0:T(8,128)(2,1)S(1)}, bf16[4,416,768]{2,1,0:T(8,128)(2,1)S(1)}, f32[416,768]{1,0:T(8,128)S(1)}, bf16[416,768]{1,0:T(8,128)(2,1)S(1)}) custom-call(f32[416,768]{1,0:T(8,128)S(1)} %get-tuple-element.132.x_ref.r1_ref, f32[5,768]{1,0:T(8,128)S(1)} %concatenate.181.acc_in.vec_ref, ...), custom_call_target="tpu_custom_call" | custom-call | flops 1 | bytes 1 | tf_op jit(solution)/shard_map/ffn_fwd/pallas_call | solution.py:69
  151.8 7.0 %ffn_bwd.5 = (f32[416,768]{1,0:T(8,128)S(1)}, bf16[416,768]{1,0:T(8,128)(2,1)S(1)}) custom-call(bf16[416,768]{1,0:T(8,128)(2,1)S(1)} %bitcast.98, f32[416,768]{1,0:T(8,128)S(1)} %get-tuple-element.134.r2_ref, f32[416,768]{1,0:T(8,128)S(1)} %get-tuple-element.132.x_ref.r1_ref, f32[5,768]{1,0:T(8,128)S(1)} %concatenate.181.acc_in.vec_ref, ...), custom_call_target="tpu_custom_call" | custom-call | flops 1 | bytes 1 | tf_op jit(solution)/shard_map/ffn_bwd/pallas_call | solution.py:69
  158.8 8.6 %attn_bwd.5 = bf16[416,768]{1,0:T(8,128)(2,1)} custom-call(bf16[416,768]{1,0:T(8,128)(2,1)S(1)} %get-tuple-element.136.dg_ref, f32[416,768]{1,0:T(8,128)S(1)} %get-tuple-element.137.dr1_ref, bf16[4,416,576]{2,1,0:T(8,128)(2,1)S(1)} %copy-done.38, bf16[4,2,3,208,208]{4,3,2,1,0:T(8,128)(2,1)S(1)} %copy-done.23, ...), custom_call_target="tpu_custom_call" | custom-call | flops 1 | bytes 1 | tf_op jit(solution)/shard_map/attn_bwd/pallas_call | solution.py:69
  176.8 7.3 %ffn_bwd.6 = (f32[416,768]{1,0:T(8,128)S(1)}, bf16[416,768]{1,0:T(8,128)(2,1)S(1)}, bf16[416,768]{1,0:T(8,128)(2,1)S(1)}, bf16[4,416,768]{2,1,0:T(8,128)(2,1)S(1...) custom-call(bf16[416,768]{1,0:T(8,128)(2,1)S(1)} %broadcast_select_fusion.1.dy_ref, f32[416,768]{1,0:T(8,128)S(1)} %copy-done.48, ...), custom_call_target="tpu_custom_call" | custom-call | flops 1 | bytes 1 | tf_op jit(solution)/shard_map/ffn_bwd/pallas_call | solution.py:69
  192.9 7.5 %ffn_bwd.7 = (f32[416,768]{1,0:T(8,128)S(1)}, bf16[416,768]{1,0:T(8,128)(2,1)S(1)}, bf16[416,768]{1,0:T(8,128)(2,1)S(1)}, bf16[4,416,768]{2,1,0:T(8,128)(2,1)S(1...) custom-call(bf16[416,768]{1,0:T(8,128)(2,1)S(1)} %broadcast_select_fusion.dy_ref, f32[416,768]{1,0:T(8,128)S(1)} %copy-done.50, ...), custom_call_target="tpu_custom_call" | custom-call | flops 1 | bytes 1 | tf_op jit(solution)/shard_map/ffn_bwd/pallas_call | solution.py:69
  215.5 7.7 %attn_bwd.6 = (f32[416,768]{1,0:T(8,128)S(1)}, bf16[4,416,576]{2,1,0:T(8,128)(2,1)S(1)}, f32[4,1,576]{2,1,0:T(1,128)S(1)}) custom-call(bf16[416,768]{1,0:T(8,128)(2,1)S(1)} %copy-done.44, f32[416,768]{1,0:T(8,128)S(1)} %copy-done.66, bf16[4,416,576]{2,1,0:T(8,128)(2,1)S(1)} %copy-done.36, bf16[4,2,3,208,208]{4,3,2,1,0:T(8,128)(2,1)S(1)} %copy-done.21, ...), custom_call_target="tpu_custom_call" | custom-call | flops 1 | bytes 1 | tf_op jit(solution)/shard_map/attn_bwd/pallas_call | solution.py:69
  223.3 7.7 %attn_bwd.7 = (f32[416,768]{1,0:T(8,128)S(1)}, bf16[4,416,576]{2,1,0:T(8,128)(2,1)S(1)}, f32[4,1,576]{2,1,0:T(1,128)S(1)}) custom-call(bf16[416,768]{1,0:T(8,128)(2,1)S(1)} %get-tuple-element.158.dg_ref.refs_3_, f32[416,768]{1,0:T(8,128)S(1)} %copy-done.68, bf16[4,416,576]{2,1,0:T(8,128)(2,1)S(1)} %copy-done.39, bf16[4,2,3,208,208]{4,3,2,1,0:T(8,128)(2,1)S(1)} %copy-done.24, ...), custom_call_target="tpu_custom_call" | custom-call | flops 1 | bytes 1 | tf_op jit(solution)/shard_map/attn_bwd/pallas_call | solution.py:69
  241.9 4.5 %collective-permute-start.25 = (bf16[384,768]{1,0:T(8,128)(2,1)}, bf16[384,768]{1,0:T(8,128)(2,1)}, u32[]{:S(2)}, u32[]{:S(2)}) collective-permute-start(bf16[384,768]{1,0:T(8,128)(2,1)} %get-tuple-element.170), channel_id=1, source_target_pairs={{0,4},{12,8},{1,5},{13,9},{2,6},{14,10},{3,7},{15,11},{16,20},{28,... | collective-permute-start | bytes 1769480 | tf_op jit(solution)/shard_map/ppermute | solution.py:587
  264.9 11.1 %collective-permute-done.26 = bf16[384,768]{1,0:T(8,128)(2,1)S(1)} collective-permute-done((bf16[384,768]{1,0:T(8,128)(2,1)S(1)}, bf16[384,768]{1,0:T(8,128)(2,1)S(1)}, u32[]{:S(2)}, u32[]{:S(2)}) %collective-permute-start.26) | collective-permute-done | bytes 589856 | tf_op jit(solution)/shard_map/ppermute | solution.py:593
  285.3 7.7 %collective-permute-done.29 = bf16[384,768]{1,0:T(8,128)(2,1)S(1)} collective-permute-done((bf16[384,768]{1,0:T(8,128)(2,1)S(1)}, bf16[384,768]{1,0:T(8,128)(2,1)S(1)}, u32[]{:S(2)}, u32[]{:S(2)}) %collective-permute-start.29) | collective-permute-done | bytes 589856 | tf_op jit(solution)/shard_map/ppermute | solution.py:587
  293.2 4.4 %collective-permute-start.33 = (bf16[384,768]{1,0:T(8,128)(2,1)S(1)}, bf16[384,768]{1,0:T(8,128)(2,1)S(1)}, u32[]{:S(2)}, u32[]{:S(2)}) collective-permute-start(bf16[384,768]{1,0:T(8,128)(2,1)S(1)} %get-tuple-element.179), channel_id=1, source_target_pairs={{0,4},{12,8},{1,5},{13,9},{2,6},{14,10},{3,7},{15,11},{16,20},{28,... | collective-permute-start | bytes 1769480 | tf_op jit(solution)/shard_map/ppermute | solution.py:593
  312.4 4.8 %collective-permute-done.35 = bf16[288,768]{1,0:T(8,128)(2,1)S(1)} collective-permute-done((bf16[288,768]{1,0:T(8,128)(2,1)S(1)}, bf16[288,768]{1,0:T(8,128)(2,1)S(1)}, u32[]{:S(2)}, u32[]{:S(2)}) %collective-permute-start.35) | collective-permute-done | bytes 442400 | tf_op jit(solution)/shard_map/ppermute | solution.py:587
  319.6 15.0 %collective-permute-start.41 = (bf16[288,768]{1,0:T(8,128)(2,1)S(1)}, bf16[288,768]{1,0:T(8,128)(2,1)S(1)}, u32[]{:S(2)}, u32[]{:S(2)}) collective-permute-start(bf16[288,768]{1,0:T(8,128)(2,1)S(1)} %get-tuple-element.193), channel_id=1, source_target_pairs={{0,4},{12,8},{1,5},{13,9},{2,6},{14,10},{3,7},{15,11},{16,20},{28,... | collective-permute-start | bytes 1327112 | tf_op jit(solution)/shard_map/ppermute | solution.py:593
  336.2 4.6 %collective-permute-start.45 = (bf16[192,768]{1,0:T(8,128)(2,1)S(1)}, bf16[192,768]{1,0:T(8,128)(2,1)S(1)}, u32[]{:S(2)}, u32[]{:S(2)}) collective-permute-start(bf16[192,768]{1,0:T(8,128)(2,1)S(1)} %bitcast_add_fusion), channel_id=1, source_target_pairs={{0,4},{12,8},{1,5},{13,9},{2,6},{14,10},{3,7},{15,11},{16,20},{28,... | collective-permute-start | bytes 884744 | tf_op jit(solution)/shard_map/ppermute | solution.py:587
  343.8 4.4 %collective-permute-start.44 = (f32[1,5952]{1,0:T(1,128)S(1)}, f32[1,5952]{1,0:T(1,128)S(1)}, u32[]{:S(2)}, u32[]{:S(2)}) collective-permute-start(f32[1,5952]{1,0:T(1,128)S(1)} %bitcast_add_fusion.1), channel_id=1, source_target_pairs={{0,4},{12,8},{1,5},{13,9},{2,6},{14,10},{3,7},{15,11},{16,20},{28,... | collective-permute-start | bytes 71432 | tf_op jit(solution)/shard_map/ppermute | solution.py:587
  364.3 7.2 %collective-permute-done.51 = bf16[288,768]{1,0:T(8,128)(2,1)S(1)} collective-permute-done((bf16[288,768]{1,0:T(8,128)(2,1)S(1)}, bf16[288,768]{1,0:T(8,128)(2,1)S(1)}, u32[]{:S(2)}, u32[]{:S(2)}) %collective-permute-start.51) | collective-permute-done | bytes 442400 | tf_op jit(solution)/shard_map/ppermute | solution.py:600
  (431 shorter events, 196.2 us)
Async XLA Ops:
  0.7 23.0 %collective-permute-start.2 = (bf16[192,768]{1,0:T(8,128)(2,1)}, bf16[192,768]{1,0:T(8,128)(2,1)}, u32[]{:S(2)}, u32[]{:S(2)}) collective-permute-start(bf16[192,768]{1,0:T(8,128)(2,1)} %bitcast.123), channel_id=1, source_target_pairs={{0,1},{1,0},{2,3},{3,2},{4,5},{5,4},{6,7},{7,6},{8,9},{9,8},{10,11... | collective-permute-start | bytes 884744 | tf_op jit(solution)/shard_map/ppermute | solution.py:346
  9.1 29.8 %collective-permute-start.1 = (bf16[608,768]{1,0:T(8,128)(2,1)}, bf16[608,768]{1,0:T(8,128)(2,1)}, u32[]{:S(2)}, u32[]{:S(2)}) collective-permute-start(bf16[608,768]{1,0:T(8,128)(2,1)} %get-tuple-element.223), channel_id=1, source_target_pairs={{0,1},{1,0},{2,3},{3,2},{4,5},{5,4},{6,7},{7,6},{8,9},{9,8},{10,11... | collective-permute-start | bytes 2801672 | tf_op jit(solution)/shard_map/ppermute | solution.py:346
  15.0 19.3 %collective-permute-start.13 = (bf16[384,768]{1,0:T(8,128)(2,1)}, bf16[384,768]{1,0:T(8,128)(2,1)}, u32[]{:S(2)}, u32[]{:S(2)}) collective-permute-start(bf16[384,768]{1,0:T(8,128)(2,1)} %select_bitcast_fusion), channel_id=1, source_target_pairs={{0,2},{1,3},{2,0},{3,1},{4,6},{5,7},{6,4},{7,5},{8,10},{9,11},{10,... | collective-permute-start | bytes 1769480 | tf_op jit(solution)/shard_map/ppermute | solution.py:346
  23.6 22.4 %collective-permute-start.10 = (bf16[384,768]{1,0:T(8,128)(2,1)}, bf16[384,768]{1,0:T(8,128)(2,1)S(1)}, u32[]{:S(2)}, u32[]{:S(2)}) collective-permute-start(bf16[384,768]{1,0:T(8,128)(2,1)} %select_bitcast_fusion.1), channel_id=1, source_target_pairs={{0,2},{1,3},{2,0},{3,1},{4,6},{5,7},{6,4},{7,5},{8,10},{9,11},{10,... | collective-permute-start | bytes 1769480 | tf_op jit(solution)/shard_map/ppermute | solution.py:346
  26.6 36.9 %collective-permute-start.9 = (bf16[768,768]{1,0:T(8,128)(2,1)}, bf16[768,768]{1,0:T(8,128)(2,1)S(1)}, u32[]{:S(2)}, u32[]{:S(2)}) collective-permute-start(bf16[768,768]{1,0:T(8,128)(2,1)} %bitcast.111), channel_id=1, source_target_pairs={{0,1},{1,0},{2,3},{3,2},{4,5},{5,4},{6,7},{7,6},{8,9},{9,8},{10,11... | collective-permute-start | bytes 3538952 | tf_op jit(solution)/shard_map/ppermute | solution.py:346
  34.3 29.4 %collective-permute-start = (bf16[768,768]{1,0:T(8,128)(2,1)S(1)}, bf16[768,768]{1,0:T(8,128)(2,1)S(1)}, u32[]{:S(2)}, u32[]{:S(2)}) collective-permute-start(bf16[768,768]{1,0:T(8,128)(2,1)S(1)} %bitcast.112), channel_id=1, source_target_pairs={{0,1},{1,0},{2,3},{3,2},{4,5},{5,4},{6,7},{7,6},{8,9},{9,8},{10,11... | collective-permute-start | bytes 3538952 | tf_op jit(solution)/shard_map/ppermute | solution.py:346
  38.9 25.1 %collective-permute-start.5 = (bf16[608,768]{1,0:T(8,128)(2,1)S(1)}, bf16[608,768]{1,0:T(8,128)(2,1)S(1)}, u32[]{:S(2)}, u32[]{:S(2)}) collective-permute-start(bf16[608,768]{1,0:T(8,128)(2,1)S(1)} %maximum_select_fusion.5), channel_id=1, source_target_pairs={{0,1},{1,0},{2,3},{3,2},{4,5},{5,4},{6,7},{7,6},{8,9},{9,8},{10,11... | collective-permute-start | bytes 2801672 | tf_op jit(solution)/shard_map/ppermute | solution.py:346
  52.4 25.0 %collective-permute-start.15 = (bf16[768,768]{1,0:T(8,128)(2,1)S(1)}, bf16[768,768]{1,0:T(8,128)(2,1)S(1)}, u32[]{:S(2)}, u32[]{:S(2)}) collective-permute-start(bf16[768,768]{1,0:T(8,128)(2,1)S(1)} %maximum_select_fusion.3), channel_id=1, source_target_pairs={{0,1},{1,0},{2,3},{3,2},{4,5},{5,4},{6,7},{7,6},{8,9},{9,8},{10,11... | collective-permute-start | bytes 3538952 | tf_op jit(solution)/shard_map/ppermute | solution.py:346
  98.9 35.6 %collective-permute-start.17 = (bf16[416,768]{1,0:T(8,128)(2,1)S(1)}, bf16[416,768]{1,0:T(8,128)(2,1)S(1)}, u32[]{:S(2)}, u32[]{:S(2)}) collective-permute-start(bf16[416,768]{1,0:T(8,128)(2,1)S(1)} %ffn_fwd.9), channel_id=1, source_target_pairs={{0,16},{16,0},{1,17},{17,1},{2,18},{18,2},{3,19},{19,3},{4,20},{20... | collective-permute-start | bytes 1916936 | tf_op jit(solution)/shard_map/ppermute | solution.py:346
  134.0 35.0 %collective-permute-start.18 = (bf16[416,768]{1,0:T(8,128)(2,1)}, bf16[416,768]{1,0:T(8,128)(2,1)}, u32[]{:S(2)}, u32[]{:S(2)}) collective-permute-start(bf16[416,768]{1,0:T(8,128)(2,1)} %attn_bwd.4), channel_id=1, source_target_pairs={{0,16},{16,0},{1,17},{17,1},{2,18},{18,2},{3,19},{19,3},{4,20},{20... | collective-permute-start | bytes 1916936 | tf_op jit(solution)/shard_map/ppermute | solution.py:346
  167.4 23.8 %collective-permute-start.19 = (bf16[416,768]{1,0:T(8,128)(2,1)}, bf16[416,768]{1,0:T(8,128)(2,1)}, u32[]{:S(2)}, u32[]{:S(2)}) collective-permute-start(bf16[416,768]{1,0:T(8,128)(2,1)} %attn_bwd.5), channel_id=1, source_target_pairs={{0,16},{16,0},{1,17},{17,1},{2,18},{18,2},{3,19},{19,3},{4,20},{20... | collective-permute-start | bytes 1916936 | tf_op jit(solution)/shard_map/ppermute | solution.py:346
  211.1 28.3 %collective-permute-start.22 = (bf16[768,768]{1,0:T(8,128)(2,1)}, bf16[768,768]{1,0:T(8,128)(2,1)}, u32[]{:S(2)}, u32[]{:S(2)}) collective-permute-start(bf16[768,768]{1,0:T(8,128)(2,1)} %slice_bitcast_fusion.1), channel_id=1, source_target_pairs={{0,2},{1,3},{2,0},{3,1},{4,6},{5,7},{6,4},{7,5},{8,10},{9,11},{10,... | collective-permute-start | bytes 3538952 | tf_op jit(solution)/shard_map/ppermute | solution.py:346
  238.9 18.9 %collective-permute-start.24 = (bf16[2,192,768]{2,1,0:T(8,128)(2,1)}, bf16[2,192,768]{2,1,0:T(8,128)(2,1)}, u32[]{:S(2)}, u32[]{:S(2)}) collective-permute-start(bf16[2,192,768]{2,1,0:T(8,128)(2,1)} %wgrad.21), channel_id=1, source_target_pairs={{0,1},{1,0},{2,3},{3,2},{4,5},{5,4},{6,7},{7,6},{8,9},{9,8},{10,11... | collective-permute-start | bytes 1769480 | tf_op jit(solution)/shard_map/ppermute | solution.py:346
  249.9 27.9 %collective-permute-start.27 = (bf16[768,768]{1,0:T(8,128)(2,1)}, bf16[768,768]{1,0:T(8,128)(2,1)}, u32[]{:S(2)}, u32[]{:S(2)}) collective-permute-start(bf16[768,768]{1,0:T(8,128)(2,1)} %slice_bitcast_fusion), channel_id=1, source_target_pairs={{0,2},{1,3},{2,0},{3,1},{4,6},{5,7},{6,4},{7,5},{8,10},{9,11},{10,... | collective-permute-start | bytes 3538952 | tf_op jit(solution)/shard_map/ppermute | solution.py:346
  264.2 19.6 %collective-permute-start.28 = (bf16[384,768]{1,0:T(8,128)(2,1)S(1)}, bf16[384,768]{1,0:T(8,128)(2,1)S(1)}, u32[]{:S(2)}, u32[]{:S(2)}) collective-permute-start(bf16[384,768]{1,0:T(8,128)(2,1)S(1)} %add.107), channel_id=1, source_target_pairs={{4,8},{8,4},{5,9},{9,5},{6,10},{10,6},{7,11},{11,7},{20,24},{24,20... | collective-permute-start | bytes 1769480 | tf_op jit(solution)/shard_map/ppermute | solution.py:600
  282.3 22.1 %collective-permute-start.32 = (bf16[576,768]{1,0:T(8,128)(2,1)S(1)}, bf16[576,768]{1,0:T(8,128)(2,1)S(1)}, u32[]{:S(2)}, u32[]{:S(2)}) collective-permute-start(bf16[576,768]{1,0:T(8,128)(2,1)S(1)} %slice_bitcast_fusion.2), channel_id=1, source_target_pairs={{0,2},{1,3},{2,0},{3,1},{4,6},{5,7},{6,4},{7,5},{8,10},{9,11},{10,... | collective-permute-start | bytes 2654216 | tf_op jit(solution)/shard_map/ppermute | solution.py:346
  297.9 20.2 %collective-permute-start.37 = (bf16[384,768]{1,0:T(8,128)(2,1)S(1)}, bf16[384,768]{1,0:T(8,128)(2,1)S(1)}, u32[]{:S(2)}, u32[]{:S(2)}) collective-permute-start(bf16[384,768]{1,0:T(8,128)(2,1)S(1)} %add.113), channel_id=1, source_target_pairs={{4,0},{8,12},{5,1},{9,13},{6,2},{10,14},{7,3},{11,15},{20,16},{24,... | collective-permute-start | bytes 1769480 | tf_op jit(solution)/shard_map/ppermute | solution.py:600
  310.0 24.7 %collective-permute-start.39 = (f32[1,5952]{1,0:T(1,128)S(1)}, f32[1,5952]{1,0:T(1,128)S(1)}, u32[]{:S(2)}, u32[]{:S(2)}) collective-permute-start(f32[1,5952]{1,0:T(1,128)S(1)} %slice_bitcast_fusion.4), channel_id=1, source_target_pairs={{0,2},{1,3},{2,0},{3,1},{4,6},{5,7},{6,4},{7,5},{8,10},{9,11},{10,... | collective-permute-start | bytes 71432 | tf_op jit(solution)/shard_map/ppermute | solution.py:346
  310.9 25.2 %collective-permute-start.40 = (bf16[192,768]{1,0:T(8,128)(2,1)S(1)}, bf16[192,768]{1,0:T(8,128)(2,1)S(1)}, u32[]{:S(2)}, u32[]{:S(2)}) collective-permute-start(bf16[192,768]{1,0:T(8,128)(2,1)S(1)} %slice_bitcast_fusion.3), channel_id=1, source_target_pairs={{0,2},{1,3},{2,0},{3,1},{4,6},{5,7},{6,4},{7,5},{8,10},{9,11},{10,... | collective-permute-start | bytes 884744 | tf_op jit(solution)/shard_map/ppermute | solution.py:346
  317.3 31.0 %collective-permute-start.42 = (bf16[288,768]{1,0:T(8,128)(2,1)S(1)}, bf16[288,768]{1,0:T(8,128)(2,1)S(1)}, u32[]{:S(2)}, u32[]{:S(2)}) collective-permute-start(bf16[288,768]{1,0:T(8,128)(2,1)S(1)} %add.118), channel_id=1, source_target_pairs={{4,8},{8,4},{5,9},{9,5},{6,10},{10,6},{7,11},{11,7},{20,24},{24,20... | collective-permute-start | bytes 1327112 | tf_op jit(solution)/shard_map/ppermute | solution.py:600
  318.2 31.6 %collective-permute-start.43 = (bf16[384,768]{1,0:T(8,128)(2,1)S(1)}, bf16[384,768]{1,0:T(8,128)(2,1)S(1)}, u32[]{:S(2)}, u32[]{:S(2)}) collective-permute-start(bf16[384,768]{1,0:T(8,128)(2,1)S(1)} %add.117), channel_id=1, source_target_pairs={{4,0},{8,12},{5,1},{9,13},{6,2},{10,14},{7,3},{11,15},{20,16},{24,... | collective-permute-start | bytes 1769480 | tf_op jit(solution)/shard_map/ppermute | solution.py:600
  319.6 24.3 %collective-permute-start.41 = (bf16[288,768]{1,0:T(8,128)(2,1)S(1)}, bf16[288,768]{1,0:T(8,128)(2,1)S(1)}, u32[]{:S(2)}, u32[]{:S(2)}) collective-permute-start(bf16[288,768]{1,0:T(8,128)(2,1)S(1)} %get-tuple-element.193), channel_id=1, source_target_pairs={{0,4},{12,8},{1,5},{13,9},{2,6},{14,10},{3,7},{15,11},{16,20},{28,... | collective-permute-start | bytes 1327112 | tf_op jit(solution)/shard_map/ppermute | solution.py:593
  334.8 18.2 %collective-permute-start.46 = (bf16[384,768]{1,0:T(8,128)(2,1)S(1)}, bf16[384,768]{1,0:T(8,128)(2,1)S(1)}, u32[]{:S(2)}, u32[]{:S(2)}) collective-permute-start(bf16[384,768]{1,0:T(8,128)(2,1)S(1)} %add.123), channel_id=1, source_target_pairs={{4,0},{8,12},{5,1},{9,13},{6,2},{10,14},{7,3},{11,15},{20,16},{24,... | collective-permute-start | bytes 1769480 | tf_op jit(solution)/shard_map/ppermute | solution.py:600
  353.1 18.4 %collective-permute-start.51 = (bf16[288,768]{1,0:T(8,128)(2,1)S(1)}, bf16[288,768]{1,0:T(8,128)(2,1)S(1)}, u32[]{:S(2)}, u32[]{:S(2)}) collective-permute-start(bf16[288,768]{1,0:T(8,128)(2,1)S(1)} %add.130), channel_id=1, source_target_pairs={{4,0},{8,12},{5,1},{9,13},{6,2},{10,14},{7,3},{11,15},{20,16},{24,... | collective-permute-start | bytes 1327112 | tf_op jit(solution)/shard_map/ppermute | solution.py:600
  (126 other events, 1197.9 us)

commit v5 on v4

--- a/solution.py
+++ b/solution.py
@@ -44,15 +44,17 @@
 
 
 def gelu_parts(u, slope):
-    size = jnp.abs(u)
-    t = pl.reciprocal(1.0 + 0.23164189 * size, approx=True)
-    poly = t * (0.127414796 + t * (-0.142248368 + t * (0.7107068705 + t * (-0.7265760135 + t * 0.5307027145))))
-    bell = jnp.exp2(u * (u * -0.7213475204444817))
+    short = u.astype(BF)
+    size = jnp.abs(short)
+    t = pl.reciprocal(1.0 + 0.23164189 * jnp.abs(u), approx=True).astype(BF)
+    terms = [BF(c) for c in (0.127414796, -0.142248368, 0.7107068705, -0.7265760135, 0.5307027145)]
+    poly = t * (terms[0] + t * (terms[1] + t * (terms[2] + t * (terms[3] + t * terms[4]))))
+    bell = jnp.exp2(u * (u * -0.7213475204444817)).astype(BF)
     tail = poly * bell
-    act = jnp.maximum(u, 0.0) - size * tail
+    act = jnp.maximum(short, BF(0.0)) - size * tail
     if not slope:
         return act, None
-    return act, jnp.where(u < 0, tail, 1.0 - tail) + u * (bell * 0.3989422804014327)
+    return act, jnp.where(short < 0, tail, BF(1.0) - tail) + short * (bell * BF(0.3989422804014327))
 
 
 def fixed(a):

time: 382 us -> 379 us (level)
  transfers between devices with their start and end apart: 54 -> 54, of which waited for: 22 -> 22; matrix products, arithmetic and copies ran while one was open for 12% -> 12% of each run, Pallas kernels for 36% -> 35%
where the time goes in v5:
time: 379 us; the launch traced here: 374 us
  Pallas kernels  146 us (39%)
  starting transfers between devices  81.1 us (21%)
  waiting for transfers between devices  78 us (21%)
  other arithmetic  40.6 us (11%)
  local copies, waits for them, and re-layouts  26.2 us (7%)
    pallas_call x20, Pallas kernels, call(): pl.pallas_call(kernel, grid=(count,), in_specs=[spec(p) for p in ins], ou...  120 us
    ppermute x30, waiting for transfers between devices, swapped(): return lax.ppermute(value, axis, [(i, i ^ bit) for i in range(count)])  36.3 us
    pallas_call x12, Pallas kernels, wgrad(): pl.pallas_call(functools.partial(wgrad_kernel, len(pairs)), grid=(2,), in...  25 us
    ppermute x30, starting transfers between devices, swapped(): return lax.ppermute(value, axis, [(i, i ^ bit) for i in range(count)])  22.9 us
    ppermute x3, starting transfers between devices, body(): got[key] = lax.ppermute(after(mine[key], *tok), 'dp', inward[0])  22.8 us
    ppermute x5, starting transfers between devices, body(): got[k] = lax.ppermute(mine[k], 'dp', inward[0])  19.5 us
    unnamed x195, local copies, waits for them, and re-layouts  18.9 us
    ppermute x16, starting transfers between devices, body(): lax.ppermute(mine[key], 'dp', cross if what == 'cross' else outward[0])  16 us
  transfers between devices with their start and end apart: 54, of which 22 were waited for; matrix products, arithmetic and copies ran while one was open for 12% of the time, Pallas kernels for 35%

profile of v5, /device:TPU:0, one launch (start us, length us, event | category | flops | bytes accessed | tf_op | source)
XLA Modules:
  0.0 374.4 jit_solution(8561424575775825360)
XLA Ops:
  26.7 7.6 %collective-permute-done.13 = bf16[384,768]{1,0:T(8,128)(2,1)} collective-permute-done((bf16[384,768]{1,0:T(8,128)(2,1)}, bf16[384,768]{1,0:T(8,128)(2,1)}, u32[]{:S(2)}, u32[]{:S(2)}) %collective-permute-start.13) | collective-permute-done | bytes 589856 | tf_op jit(solution)/shard_map/ppermute | solution.py:348
  39.1 7.0 %collective-permute-done.10 = bf16[384,768]{1,0:T(8,128)(2,1)S(1)} collective-permute-done((bf16[384,768]{1,0:T(8,128)(2,1)}, bf16[384,768]{1,0:T(8,128)(2,1)S(1)}, u32[]{:S(2)}, u32[]{:S(2)}) %collective-permute-start.10) | collective-permute-done | bytes 589856 | tf_op jit(solution)/shard_map/ppermute | solution.py:348
  92.1 6.6 %collective-permute-done.16 = bf16[416,768]{1,0:T(8,128)(2,1)S(1)} collective-permute-done((bf16[416,768]{1,0:T(8,128)(2,1)S(1)}, bf16[416,768]{1,0:T(8,128)(2,1)S(1)}, u32[]{:S(2)}, u32[]{:S(2)}) %collective-permute-start.16) | collective-permute-done | bytes 639008 | tf_op jit(solution)/shard_map/ppermute | solution.py:348
  100.9 7.0 %attn_fwd.10 = (f32[416,768]{1,0:T(8,128)S(1)}, bf16[4,416,576]{2,1,0:T(8,128)(2,1)S(1)}, bf16[4,416,192]{2,1,0:T(8,128)(2,1)S(1)}, bf16[4,2,3,208,208]{4,3,2,1,0:T(8,128)(2,1)S(1)}) custom-call(bf16[416,768]{1,0:T(8,128)(2,1)S(1)} %broadcast_select_fusion.3.x_ref.refs_1_, s32[2,208,1]{2,1,0:T(8,128)S(1)} %slice.279.ok_ref, f32[1,768]{1,0:T(1,128)S(1)} %copy-done.73, ...), custom_call_target="tpu_custom_call" | custom-call | flops 1 | bytes 1 | tf_op jit(solution)/shard_map/attn_fwd/pallas_call | solution.py:71
  107.9 7.9 %ffn_fwd.10 = (bf16[416,768]{1,0:T(8,128)(2,1)S(1)}, bf16[4,416,768]{2,1,0:T(8,128)(2,1)S(1)}, bf16[4,416,768]{2,1,0:T(8,128)(2,1)S(1)}, f32[416,768]{1,0:T(8,128)S(1)}, bf16[416,768]{1,0:T(8,128)(2,1)S(1)}) custom-call(f32[416,768]{1,0:T(8,128)S(1)} %get-tuple-element.122.x_ref.r1_ref, f32[5,768]{1,0:T(8,128)S(1)} %concatenate.181.acc_in.vec_ref, ...), custom_call_target="tpu_custom_call" | custom-call | flops 1 | bytes 1 | tf_op jit(solution)/shard_map/ffn_fwd/pallas_call | solution.py:71
  116.6 7.0 %ffn_bwd.4 = (f32[416,768]{1,0:T(8,128)S(1)}, bf16[416,768]{1,0:T(8,128)(2,1)S(1)}) custom-call(bf16[416,768]{1,0:T(8,128)(2,1)S(1)} %bitcast.101, f32[416,768]{1,0:T(8,128)S(1)} %get-tuple-element.124.r2_ref, f32[416,768]{1,0:T(8,128)S(1)} %get-tuple-element.122.x_ref.r1_ref, f32[5,768]{1,0:T(8,128)S(1)} %concatenate.181.acc_in.vec_ref, ...), custom_call_target="tpu_custom_call" | custom-call | flops 1 | bytes 1 | tf_op jit(solution)/shard_map/ffn_bwd/pallas_call | solution.py:71
  123.7 8.5 %attn_bwd.4 = bf16[416,768]{1,0:T(8,128)(2,1)} custom-call(bf16[416,768]{1,0:T(8,128)(2,1)S(1)} %get-tuple-element.126.dg_ref, f32[416,768]{1,0:T(8,128)S(1)} %get-tuple-element.127.dr1_ref, bf16[4,416,576]{2,1,0:T(8,128)(2,1)S(1)} %get-tuple-element.128.p_ref, bf16[4,2,3,208,208]{4,3,2,1,0:T(8,128)(2,1)S(1)} %get-tuple-element.129.a_ref, ...), custom_call_target="tpu_custom_call" | custom-call | flops 1 | bytes 1 | tf_op jit(solution)/shard_map/attn_bwd/pallas_call | solution.py:71
  132.9 7.0 %attn_fwd.11 = (f32[416,768]{1,0:T(8,128)S(1)}, bf16[4,416,576]{2,1,0:T(8,128)(2,1)S(1)}, bf16[4,416,192]{2,1,0:T(8,128)(2,1)S(1)}, bf16[4,2,3,208,208]{4,3,2,1,0:T(8,128)(2,1)S(1)}) custom-call(bf16[416,768]{1,0:T(8,128)(2,1)S(1)} %broadcast_select_fusion.2.x_ref.refs_3_, s32[2,208,1]{2,1,0:T(8,128)S(1)} %slice.278.ok_ref, f32[1,768]{1,0:T(1,128)S(1)} %copy-done.73, ...), custom_call_target="tpu_custom_call" | custom-call | flops 1 | bytes 1 | tf_op jit(solution)/shard_map/attn_fwd/pallas_call | solution.py:71
  140.8 7.9 %ffn_fwd.11 = (bf16[416,768]{1,0:T(8,128)(2,1)S(1)}, bf16[4,416,768]{2,1,0:T(8,128)(2,1)S(1)}, bf16[4,416,768]{2,1,0:T(8,128)(2,1)S(1)}, f32[416,768]{1,0:T(8,128)S(1)}, bf16[416,768]{1,0:T(8,128)(2,1)S(1)}) custom-call(f32[416,768]{1,0:T(8,128)S(1)} %get-tuple-element.132.x_ref.r1_ref, f32[5,768]{1,0:T(8,128)S(1)} %concatenate.181.acc_in.vec_ref, ...), custom_call_target="tpu_custom_call" | custom-call | flops 1 | bytes 1 | tf_op jit(solution)/shard_map/ffn_fwd/pallas_call | solution.py:71
  148.8 6.8 %ffn_bwd.5 = (f32[416,768]{1,0:T(8,128)S(1)}, bf16[416,768]{1,0:T(8,128)(2,1)S(1)}) custom-call(bf16[416,768]{1,0:T(8,128)(2,1)S(1)} %bitcast.98, f32[416,768]{1,0:T(8,128)S(1)} %get-tuple-element.134.r2_ref, f32[416,768]{1,0:T(8,128)S(1)} %get-tuple-element.132.x_ref.r1_ref, f32[5,768]{1,0:T(8,128)S(1)} %concatenate.181.acc_in.vec_ref, ...), custom_call_target="tpu_custom_call" | custom-call | flops 1 | bytes 1 | tf_op jit(solution)/shard_map/ffn_bwd/pallas_call | solution.py:71
  155.7 8.8 %attn_bwd.5 = bf16[416,768]{1,0:T(8,128)(2,1)} custom-call(bf16[416,768]{1,0:T(8,128)(2,1)S(1)} %get-tuple-element.136.dg_ref, f32[416,768]{1,0:T(8,128)S(1)} %get-tuple-element.137.dr1_ref, bf16[4,416,576]{2,1,0:T(8,128)(2,1)S(1)} %copy-done.38, bf16[4,2,3,208,208]{4,3,2,1,0:T(8,128)(2,1)S(1)} %copy-done.23, ...), custom_call_target="tpu_custom_call" | custom-call | flops 1 | bytes 1 | tf_op jit(solution)/shard_map/attn_bwd/pallas_call | solution.py:71
  173.9 7.3 %ffn_bwd.6 = (f32[416,768]{1,0:T(8,128)S(1)}, bf16[416,768]{1,0:T(8,128)(2,1)S(1)}, bf16[416,768]{1,0:T(8,128)(2,1)S(1)}, bf16[4,416,768]{2,1,0:T(8,128)(2,1)S(1...) custom-call(bf16[416,768]{1,0:T(8,128)(2,1)S(1)} %broadcast_select_fusion.1.dy_ref, f32[416,768]{1,0:T(8,128)S(1)} %copy-done.48, ...), custom_call_target="tpu_custom_call" | custom-call | flops 1 | bytes 1 | tf_op jit(solution)/shard_map/ffn_bwd/pallas_call | solution.py:71
  189.9 7.3 %ffn_bwd.7 = (f32[416,768]{1,0:T(8,128)S(1)}, bf16[416,768]{1,0:T(8,128)(2,1)S(1)}, bf16[416,768]{1,0:T(8,128)(2,1)S(1)}, bf16[4,416,768]{2,1,0:T(8,128)(2,1)S(1...) custom-call(bf16[416,768]{1,0:T(8,128)(2,1)S(1)} %broadcast_select_fusion.dy_ref, f32[416,768]{1,0:T(8,128)S(1)} %copy-done.50, ...), custom_call_target="tpu_custom_call" | custom-call | flops 1 | bytes 1 | tf_op jit(solution)/shard_map/ffn_bwd/pallas_call | solution.py:71
  212.4 7.7 %attn_bwd.6 = (f32[416,768]{1,0:T(8,128)S(1)}, bf16[4,416,576]{2,1,0:T(8,128)(2,1)S(1)}, f32[4,1,576]{2,1,0:T(1,128)S(1)}) custom-call(bf16[416,768]{1,0:T(8,128)(2,1)S(1)} %copy-done.44, f32[416,768]{1,0:T(8,128)S(1)} %copy-done.66, bf16[4,416,576]{2,1,0:T(8,128)(2,1)S(1)} %copy-done.36, bf16[4,2,3,208,208]{4,3,2,1,0:T(8,128)(2,1)S(1)} %copy-done.21, ...), custom_call_target="tpu_custom_call" | custom-call | flops 1 | bytes 1 | tf_op jit(solution)/shard_map/attn_bwd/pallas_call | solution.py:71
  220.2 7.7 %attn_bwd.7 = (f32[416,768]{1,0:T(8,128)S(1)}, bf16[4,416,576]{2,1,0:T(8,128)(2,1)S(1)}, f32[4,1,576]{2,1,0:T(1,128)S(1)}) custom-call(bf16[416,768]{1,0:T(8,128)(2,1)S(1)} %get-tuple-element.158.dg_ref.refs_3_, f32[416,768]{1,0:T(8,128)S(1)} %copy-done.68, bf16[4,416,576]{2,1,0:T(8,128)(2,1)S(1)} %copy-done.39, bf16[4,2,3,208,208]{4,3,2,1,0:T(8,128)(2,1)S(1)} %copy-done.24, ...), custom_call_target="tpu_custom_call" | custom-call | flops 1 | bytes 1 | tf_op jit(solution)/shard_map/attn_bwd/pallas_call | solution.py:71
  238.7 4.3 %collective-permute-start.25 = (bf16[384,768]{1,0:T(8,128)(2,1)}, bf16[384,768]{1,0:T(8,128)(2,1)}, u32[]{:S(2)}, u32[]{:S(2)}) collective-permute-start(bf16[384,768]{1,0:T(8,128)(2,1)} %get-tuple-element.170), channel_id=1, source_target_pairs={{0,4},{12,8},{1,5},{13,9},{2,6},{14,10},{3,7},{15,11},{16,20},{28,... | collective-permute-start | bytes 1769480 | tf_op jit(solution)/shard_map/ppermute | solution.py:589
  261.8 11.1 %collective-permute-done.26 = bf16[384,768]{1,0:T(8,128)(2,1)S(1)} collective-permute-done((bf16[384,768]{1,0:T(8,128)(2,1)S(1)}, bf16[384,768]{1,0:T(8,128)(2,1)S(1)}, u32[]{:S(2)}, u32[]{:S(2)}) %collective-permute-start.26) | collective-permute-done | bytes 589856 | tf_op jit(solution)/shard_map/ppermute | solution.py:595
  282.2 7.7 %collective-permute-done.29 = bf16[384,768]{1,0:T(8,128)(2,1)S(1)} collective-permute-done((bf16[384,768]{1,0:T(8,128)(2,1)S(1)}, bf16[384,768]{1,0:T(8,128)(2,1)S(1)}, u32[]{:S(2)}, u32[]{:S(2)}) %collective-permute-start.29) | collective-permute-done | bytes 589856 | tf_op jit(solution)/shard_map/ppermute | solution.py:589
  290.1 4.6 %collective-permute-start.33 = (bf16[384,768]{1,0:T(8,128)(2,1)S(1)}, bf16[384,768]{1,0:T(8,128)(2,1)S(1)}, u32[]{:S(2)}, u32[]{:S(2)}) collective-permute-start(bf16[384,768]{1,0:T(8,128)(2,1)S(1)} %get-tuple-element.179), channel_id=1, source_target_pairs={{0,4},{12,8},{1,5},{13,9},{2,6},{14,10},{3,7},{15,11},{16,20},{28,... | collective-permute-start | bytes 1769480 | tf_op jit(solution)/shard_map/ppermute | solution.py:595
  309.2 4.8 %collective-permute-done.35 = bf16[288,768]{1,0:T(8,128)(2,1)S(1)} collective-permute-done((bf16[288,768]{1,0:T(8,128)(2,1)S(1)}, bf16[288,768]{1,0:T(8,128)(2,1)S(1)}, u32[]{:S(2)}, u32[]{:S(2)}) %collective-permute-start.35) | collective-permute-done | bytes 442400 | tf_op jit(solution)/shard_map/ppermute | solution.py:589
  316.4 15.3 %collective-permute-start.41 = (bf16[288,768]{1,0:T(8,128)(2,1)S(1)}, bf16[288,768]{1,0:T(8,128)(2,1)S(1)}, u32[]{:S(2)}, u32[]{:S(2)}) collective-permute-start(bf16[288,768]{1,0:T(8,128)(2,1)S(1)} %get-tuple-element.193), channel_id=1, source_target_pairs={{0,4},{12,8},{1,5},{13,9},{2,6},{14,10},{3,7},{15,11},{16,20},{28,... | collective-permute-start | bytes 1327112 | tf_op jit(solution)/shard_map/ppermute | solution.py:595
  333.2 4.6 %collective-permute-start.45 = (bf16[192,768]{1,0:T(8,128)(2,1)S(1)}, bf16[192,768]{1,0:T(8,128)(2,1)S(1)}, u32[]{:S(2)}, u32[]{:S(2)}) collective-permute-start(bf16[192,768]{1,0:T(8,128)(2,1)S(1)} %bitcast_add_fusion), channel_id=1, source_target_pairs={{0,4},{12,8},{1,5},{13,9},{2,6},{14,10},{3,7},{15,11},{16,20},{28,... | collective-permute-start | bytes 884744 | tf_op jit(solution)/shard_map/ppermute | solution.py:589
  340.8 4.4 %collective-permute-start.44 = (f32[1,5952]{1,0:T(1,128)S(1)}, f32[1,5952]{1,0:T(1,128)S(1)}, u32[]{:S(2)}, u32[]{:S(2)}) collective-permute-start(f32[1,5952]{1,0:T(1,128)S(1)} %bitcast_add_fusion.1), channel_id=1, source_target_pairs={{0,4},{12,8},{1,5},{13,9},{2,6},{14,10},{3,7},{15,11},{16,20},{28,... | collective-permute-start | bytes 71432 | tf_op jit(solution)/shard_map/ppermute | solution.py:589
  361.7 6.9 %collective-permute-done.51 = bf16[288,768]{1,0:T(8,128)(2,1)S(1)} collective-permute-done((bf16[288,768]{1,0:T(8,128)(2,1)S(1)}, bf16[288,768]{1,0:T(8,128)(2,1)S(1)}, u32[]{:S(2)}, u32[]{:S(2)}) %collective-permute-start.51) | collective-permute-done | bytes 442400 | tf_op jit(solution)/shard_map/ppermute | solution.py:602
  (431 shorter events, 195.7 us)
Async XLA Ops:
  0.7 23.0 %collective-permute-start.2 = (bf16[192,768]{1,0:T(8,128)(2,1)}, bf16[192,768]{1,0:T(8,128)(2,1)}, u32[]{:S(2)}, u32[]{:S(2)}) collective-permute-start(bf16[192,768]{1,0:T(8,128)(2,1)} %bitcast.123), channel_id=1, source_target_pairs={{0,1},{1,0},{2,3},{3,2},{4,5},{5,4},{6,7},{7,6},{8,9},{9,8},{10,11... | collective-permute-start | bytes 884744 | tf_op jit(solution)/shard_map/ppermute | solution.py:348
  9.1 29.8 %collective-permute-start.1 = (bf16[608,768]{1,0:T(8,128)(2,1)}, bf16[608,768]{1,0:T(8,128)(2,1)}, u32[]{:S(2)}, u32[]{:S(2)}) collective-permute-start(bf16[608,768]{1,0:T(8,128)(2,1)} %get-tuple-element.223), channel_id=1, source_target_pairs={{0,1},{1,0},{2,3},{3,2},{4,5},{5,4},{6,7},{7,6},{8,9},{9,8},{10,11... | collective-permute-start | bytes 2801672 | tf_op jit(solution)/shard_map/ppermute | solution.py:348
  15.0 19.3 %collective-permute-start.13 = (bf16[384,768]{1,0:T(8,128)(2,1)}, bf16[384,768]{1,0:T(8,128)(2,1)}, u32[]{:S(2)}, u32[]{:S(2)}) collective-permute-start(bf16[384,768]{1,0:T(8,128)(2,1)} %select_bitcast_fusion), channel_id=1, source_target_pairs={{0,2},{1,3},{2,0},{3,1},{4,6},{5,7},{6,4},{7,5},{8,10},{9,11},{10,... | collective-permute-start | bytes 1769480 | tf_op jit(solution)/shard_map/ppermute | solution.py:348
  23.6 22.4 %collective-permute-start.10 = (bf16[384,768]{1,0:T(8,128)(2,1)}, bf16[384,768]{1,0:T(8,128)(2,1)S(1)}, u32[]{:S(2)}, u32[]{:S(2)}) collective-permute-start(bf16[384,768]{1,0:T(8,128)(2,1)} %select_bitcast_fusion.1), channel_id=1, source_target_pairs={{0,2},{1,3},{2,0},{3,1},{4,6},{5,7},{6,4},{7,5},{8,10},{9,11},{10,... | collective-permute-start | bytes 1769480 | tf_op jit(solution)/shard_map/ppermute | solution.py:348
  26.6 36.9 %collective-permute-start.9 = (bf16[768,768]{1,0:T(8,128)(2,1)}, bf16[768,768]{1,0:T(8,128)(2,1)S(1)}, u32[]{:S(2)}, u32[]{:S(2)}) collective-permute-start(bf16[768,768]{1,0:T(8,128)(2,1)} %bitcast.111), channel_id=1, source_target_pairs={{0,1},{1,0},{2,3},{3,2},{4,5},{5,4},{6,7},{7,6},{8,9},{9,8},{10,11... | collective-permute-start | bytes 3538952 | tf_op jit(solution)/shard_map/ppermute | solution.py:348
  34.3 29.4 %collective-permute-start = (bf16[768,768]{1,0:T(8,128)(2,1)S(1)}, bf16[768,768]{1,0:T(8,128)(2,1)S(1)}, u32[]{:S(2)}, u32[]{:S(2)}) collective-permute-start(bf16[768,768]{1,0:T(8,128)(2,1)S(1)} %bitcast.112), channel_id=1, source_target_pairs={{0,1},{1,0},{2,3},{3,2},{4,5},{5,4},{6,7},{7,6},{8,9},{9,8},{10,11... | collective-permute-start | bytes 3538952 | tf_op jit(solution)/shard_map/ppermute | solution.py:348
  38.9 25.1 %collective-permute-start.5 = (bf16[608,768]{1,0:T(8,128)(2,1)S(1)}, bf16[608,768]{1,0:T(8,128)(2,1)S(1)}, u32[]{:S(2)}, u32[]{:S(2)}) collective-permute-start(bf16[608,768]{1,0:T(8,128)(2,1)S(1)} %maximum_select_fusion.5), channel_id=1, source_target_pairs={{0,1},{1,0},{2,3},{3,2},{4,5},{5,4},{6,7},{7,6},{8,9},{9,8},{10,11... | collective-permute-start | bytes 2801672 | tf_op jit(solution)/shard_map/ppermute | solution.py:348
  52.4 24.7 %collective-permute-start.15 = (bf16[768,768]{1,0:T(8,128)(2,1)S(1)}, bf16[768,768]{1,0:T(8,128)(2,1)S(1)}, u32[]{:S(2)}, u32[]{:S(2)}) collective-permute-start(bf16[768,768]{1,0:T(8,128)(2,1)S(1)} %maximum_select_fusion.3), channel_id=1, source_target_pairs={{0,1},{1,0},{2,3},{3,2},{4,5},{5,4},{6,7},{7,6},{8,9},{9,8},{10,11... | collective-permute-start | bytes 3538952 | tf_op jit(solution)/shard_map/ppermute | solution.py:348
  98.6 34.1 %collective-permute-start.17 = (bf16[416,768]{1,0:T(8,128)(2,1)S(1)}, bf16[416,768]{1,0:T(8,128)(2,1)S(1)}, u32[]{:S(2)}, u32[]{:S(2)}) collective-permute-start(bf16[416,768]{1,0:T(8,128)(2,1)S(1)} %ffn_fwd.9), channel_id=1, source_target_pairs={{0,16},{16,0},{1,17},{17,1},{2,18},{18,2},{3,19},{19,3},{4,20},{20... | collective-permute-start | bytes 1916936 | tf_op jit(solution)/shard_map/ppermute | solution.py:348
  132.3 33.7 %collective-permute-start.18 = (bf16[416,768]{1,0:T(8,128)(2,1)}, bf16[416,768]{1,0:T(8,128)(2,1)}, u32[]{:S(2)}, u32[]{:S(2)}) collective-permute-start(bf16[416,768]{1,0:T(8,128)(2,1)} %attn_bwd.4), channel_id=1, source_target_pairs={{0,16},{16,0},{1,17},{17,1},{2,18},{18,2},{3,19},{19,3},{4,20},{20... | collective-permute-start | bytes 1916936 | tf_op jit(solution)/shard_map/ppermute | solution.py:348
  164.5 23.8 %collective-permute-start.19 = (bf16[416,768]{1,0:T(8,128)(2,1)}, bf16[416,768]{1,0:T(8,128)(2,1)}, u32[]{:S(2)}, u32[]{:S(2)}) collective-permute-start(bf16[416,768]{1,0:T(8,128)(2,1)} %attn_bwd.5), channel_id=1, source_target_pairs={{0,16},{16,0},{1,17},{17,1},{2,18},{18,2},{3,19},{19,3},{4,20},{20... | collective-permute-start | bytes 1916936 | tf_op jit(solution)/shard_map/ppermute | solution.py:348
  208.0 28.3 %collective-permute-start.22 = (bf16[768,768]{1,0:T(8,128)(2,1)}, bf16[768,768]{1,0:T(8,128)(2,1)}, u32[]{:S(2)}, u32[]{:S(2)}) collective-permute-start(bf16[768,768]{1,0:T(8,128)(2,1)} %slice_bitcast_fusion.1), channel_id=1, source_target_pairs={{0,2},{1,3},{2,0},{3,1},{4,6},{5,7},{6,4},{7,5},{8,10},{9,11},{10,... | collective-permute-start | bytes 3538952 | tf_op jit(solution)/shard_map/ppermute | solution.py:348
  235.7 18.7 %collective-permute-start.24 = (bf16[2,192,768]{2,1,0:T(8,128)(2,1)}, bf16[2,192,768]{2,1,0:T(8,128)(2,1)}, u32[]{:S(2)}, u32[]{:S(2)}) collective-permute-start(bf16[2,192,768]{2,1,0:T(8,128)(2,1)} %wgrad.21), channel_id=1, source_target_pairs={{0,1},{1,0},{2,3},{3,2},{4,5},{5,4},{6,7},{7,6},{8,9},{9,8},{10,11... | collective-permute-start | bytes 1769480 | tf_op jit(solution)/shard_map/ppermute | solution.py:348
  246.6 27.9 %collective-permute-start.27 = (bf16[768,768]{1,0:T(8,128)(2,1)}, bf16[768,768]{1,0:T(8,128)(2,1)}, u32[]{:S(2)}, u32[]{:S(2)}) collective-permute-start(bf16[768,768]{1,0:T(8,128)(2,1)} %slice_bitcast_fusion), channel_id=1, source_target_pairs={{0,2},{1,3},{2,0},{3,1},{4,6},{5,7},{6,4},{7,5},{8,10},{9,11},{10,... | collective-permute-start | bytes 3538952 | tf_op jit(solution)/shard_map/ppermute | solution.py:348
  261.1 19.6 %collective-permute-start.28 = (bf16[384,768]{1,0:T(8,128)(2,1)S(1)}, bf16[384,768]{1,0:T(8,128)(2,1)S(1)}, u32[]{:S(2)}, u32[]{:S(2)}) collective-permute-start(bf16[384,768]{1,0:T(8,128)(2,1)S(1)} %add.107), channel_id=1, source_target_pairs={{4,8},{8,4},{5,9},{9,5},{6,10},{10,6},{7,11},{11,7},{20,24},{24,20... | collective-permute-start | bytes 1769480 | tf_op jit(solution)/shard_map/ppermute | solution.py:602
  279.2 22.1 %collective-permute-start.32 = (bf16[576,768]{1,0:T(8,128)(2,1)S(1)}, bf16[576,768]{1,0:T(8,128)(2,1)S(1)}, u32[]{:S(2)}, u32[]{:S(2)}) collective-permute-start(bf16[576,768]{1,0:T(8,128)(2,1)S(1)} %slice_bitcast_fusion.2), channel_id=1, source_target_pairs={{0,2},{1,3},{2,0},{3,1},{4,6},{5,7},{6,4},{7,5},{8,10},{9,11},{10,... | collective-permute-start | bytes 2654216 | tf_op jit(solution)/shard_map/ppermute | solution.py:348
  294.9 20.0 %collective-permute-start.37 = (bf16[384,768]{1,0:T(8,128)(2,1)S(1)}, bf16[384,768]{1,0:T(8,128)(2,1)S(1)}, u32[]{:S(2)}, u32[]{:S(2)}) collective-permute-start(bf16[384,768]{1,0:T(8,128)(2,1)S(1)} %add.113), channel_id=1, source_target_pairs={{4,0},{8,12},{5,1},{9,13},{6,2},{10,14},{7,3},{11,15},{20,16},{24,... | collective-permute-start | bytes 1769480 | tf_op jit(solution)/shard_map/ppermute | solution.py:602
  306.8 25.0 %collective-permute-start.39 = (f32[1,5952]{1,0:T(1,128)S(1)}, f32[1,5952]{1,0:T(1,128)S(1)}, u32[]{:S(2)}, u32[]{:S(2)}) collective-permute-start(f32[1,5952]{1,0:T(1,128)S(1)} %slice_bitcast_fusion.4), channel_id=1, source_target_pairs={{0,2},{1,3},{2,0},{3,1},{4,6},{5,7},{6,4},{7,5},{8,10},{9,11},{10,... | collective-permute-start | bytes 71432 | tf_op jit(solution)/shard_map/ppermute | solution.py:348
  307.8 25.4 %collective-permute-start.40 = (bf16[192,768]{1,0:T(8,128)(2,1)S(1)}, bf16[192,768]{1,0:T(8,128)(2,1)S(1)}, u32[]{:S(2)}, u32[]{:S(2)}) collective-permute-start(bf16[192,768]{1,0:T(8,128)(2,1)S(1)} %slice_bitcast_fusion.3), channel_id=1, source_target_pairs={{0,2},{1,3},{2,0},{3,1},{4,6},{5,7},{6,4},{7,5},{8,10},{9,11},{10,... | collective-permute-start | bytes 884744 | tf_op jit(solution)/shard_map/ppermute | solution.py:348
  314.2 31.2 %collective-permute-start.42 = (bf16[288,768]{1,0:T(8,128)(2,1)S(1)}, bf16[288,768]{1,0:T(8,128)(2,1)S(1)}, u32[]{:S(2)}, u32[]{:S(2)}) collective-permute-start(bf16[288,768]{1,0:T(8,128)(2,1)S(1)} %add.118), channel_id=1, source_target_pairs={{4,8},{8,4},{5,9},{9,5},{6,10},{10,6},{7,11},{11,7},{20,24},{24,20... | collective-permute-start | bytes 1327112 | tf_op jit(solution)/shard_map/ppermute | solution.py:602
  315.0 31.8 %collective-permute-start.43 = (bf16[384,768]{1,0:T(8,128)(2,1)S(1)}, bf16[384,768]{1,0:T(8,128)(2,1)S(1)}, u32[]{:S(2)}, u32[]{:S(2)}) collective-permute-start(bf16[384,768]{1,0:T(8,128)(2,1)S(1)} %add.117), channel_id=1, source_target_pairs={{4,0},{8,12},{5,1},{9,13},{6,2},{10,14},{7,3},{11,15},{20,16},{24,... | collective-permute-start | bytes 1769480 | tf_op jit(solution)/shard_map/ppermute | solution.py:602
  316.4 24.5 %collective-permute-start.41 = (bf16[288,768]{1,0:T(8,128)(2,1)S(1)}, bf16[288,768]{1,0:T(8,128)(2,1)S(1)}, u32[]{:S(2)}, u32[]{:S(2)}) collective-permute-start(bf16[288,768]{1,0:T(8,128)(2,1)S(1)} %get-tuple-element.193), channel_id=1, source_target_pairs={{0,4},{12,8},{1,5},{13,9},{2,6},{14,10},{3,7},{15,11},{16,20},{28,... | collective-permute-start | bytes 1327112 | tf_op jit(solution)/shard_map/ppermute | solution.py:595
  331.8 18.2 %collective-permute-start.46 = (bf16[384,768]{1,0:T(8,128)(2,1)S(1)}, bf16[384,768]{1,0:T(8,128)(2,1)S(1)}, u32[]{:S(2)}, u32[]{:S(2)}) collective-permute-start(bf16[384,768]{1,0:T(8,128)(2,1)S(1)} %add.123), channel_id=1, source_target_pairs={{4,0},{8,12},{5,1},{9,13},{6,2},{10,14},{7,3},{11,15},{20,16},{24,... | collective-permute-start | bytes 1769480 | tf_op jit(solution)/shard_map/ppermute | solution.py:602
  350.2 18.4 %collective-permute-start.51 = (bf16[288,768]{1,0:T(8,128)(2,1)S(1)}, bf16[288,768]{1,0:T(8,128)(2,1)S(1)}, u32[]{:S(2)}, u32[]{:S(2)}) collective-permute-start(bf16[288,768]{1,0:T(8,128)(2,1)S(1)} %add.130), channel_id=1, source_target_pairs={{4,0},{8,12},{5,1},{9,13},{6,2},{10,14},{7,3},{11,15},{20,16},{24,... | collective-permute-start | bytes 1327112 | tf_op jit(solution)/shard_map/ppermute | solution.py:602
  (126 other events, 1178.8 us)
